TPU v7x, 32 devices: a whole 2x2x4 slice. The times are simulated.
32 devices in a mesh: rep: 8 (over y, x, core), grp: 4 (over z).
Axes of the slice: x: 2, y: 2, z: 4, core: 2. Of those that a mesh axis runs over, the one named last changes fastest.
Arguments:
- layer_input: bfloat16 [8, 1024, 2048], P('rep', 'grp'), may hold values from -6 to 6
- w_qkv: bfloat16 [2048, 1920], P('grp'), may hold values from -0.125 to 0.125
- w_out: bfloat16 [1280, 2048], P('grp'), may hold values from -2.5 to 2.5
- w_in: bfloat16 [5120, 2, 2048], P('grp'), may hold values from -0.125 to 0.125
- w_down: bfloat16 [5120, 2048], P('grp'), may hold values from -0.078125 to 0.078125
- attn_gain: float32 [2048], replicated, may hold values from 0.1 to 1.9
- ffn_gain: float32 [2048], replicated, may hold values from 0.1 to 1.9
- q_gain: float32 [64], replicated, may hold values from 0.1 to 1.9
- k_gain: float32 [64], replicated, may hold values from 0.1 to 1.9
- cotangent: bfloat16 [8, 1024, 2048], P('rep', 'grp'), may hold values from -6 to 6
- prefix_len: int32 [8], replicated, may hold values from 102 to 512, as said below
- seq_slot: int32 [8], P('rep'), may hold values from 0 to 7, each once
Outputs:
- layer_output: bfloat16 [8, 1024, 2048], P('rep', 'grp')
- input_grad: float32 [8, 1024, 2048], P('rep', 'grp')
- d_w_qkv: float32 [2048, 1920], P('grp')
- d_w_out: float32 [1280, 2048], P('grp')
- d_w_in: float32 [5120, 2, 2048], P('grp')
- d_w_down: float32 [5120, 2048], P('grp')
- d_attn_gain: float32 [2048], replicated
- d_ffn_gain: float32 [2048], replicated
- d_q_gain: float32 [64], replicated
- d_k_gain: float32 [64], replicated
Inputs may be any that keep to these rules, and one draw needn't show every extreme that they name: `prefix_len`: prefix length of each sequence; both ends of the range are taken by some sequence. `seq_slot`: a permutation of the sequence numbers 0 to 7.
All inputs are finite; a program needn't handle non-finite values.
Results may differ from a plain program's by a relative error of at most 0.015.
The roundings to bfloat16 on the way count: a program that leaves them out, or rounds other values in their place, can miss the bound.
Values may be sent and summed in bfloat16 or wider, within the bound.
No kernel may reach another device: no remote copies, remote signals or barrier semaphores. Data moves between devices by JAX's collectives and lax.ppermute only.
A program may use at most 256 MiB of HBM per device.

v0:
```python
import jax
import jax.numpy as jnp
from jax import lax
from jax.sharding import PartitionSpec as P

QUERY_HEADS = 20
KEY_VALUE_HEADS = 5
HEAD_SIZE = 64


NORM_EPSILON = 1e-06
ROPE_THETA = 10000.0
MASK_FLOOR = -1e30


def rope_tables(positions, head_dim):
    half_dim = head_dim // 2
    freqs = ROPE_THETA ** (-(2.0 * jnp.arange(half_dim, dtype=jnp.float32)) / head_dim)
    angles = positions.astype(jnp.float32)[:, None] * freqs[None, :]
    return (jnp.cos(angles), jnp.sin(angles))


def rotate(values, cos_table, sin_table):
    half_dim = values.shape[-1] // 2
    first_half = values[..., :half_dim]
    second_half = values[..., half_dim:]
    cos_b = cos_table[:, None, :]
    sin_b = sin_table[:, None, :]
    return jnp.concatenate(
        [first_half * cos_b - second_half * sin_b, second_half * cos_b + first_half * sin_b],
        axis=-1,
    )


def unrotate(gradient, cos_table, sin_table):
    half_dim = gradient.shape[-1] // 2
    first_half = gradient[..., :half_dim]
    second_half = gradient[..., half_dim:]
    cos_b = cos_table[:, None, :]
    sin_b = sin_table[:, None, :]
    return jnp.concatenate(
        [first_half * cos_b + second_half * sin_b, second_half * cos_b - first_half * sin_b],
        axis=-1,
    )


def norm_forward(values, gain):
    inv_scale = lax.rsqrt(jnp.mean(values * values, axis=-1, keepdims=True) + NORM_EPSILON)
    normed = values * inv_scale
    return (normed * gain, normed, inv_scale)


def norm_back(grad_out, normed, inv_scale, gain):
    scaled = grad_out * gain
    return inv_scale * (scaled - normed * jnp.mean(scaled * normed, axis=-1, keepdims=True))


def silu_back(gate_vals, up_vals, grad_mixed):
    sigmoid_g = jax.nn.sigmoid(gate_vals)
    silu_gate = gate_vals * sigmoid_g
    grad_gate = grad_mixed * up_vals * sigmoid_g * (1.0 + gate_vals * (1.0 - sigmoid_g))
    grad_up = grad_mixed * silu_gate
    return jnp.stack([grad_gate, grad_up], axis=1).astype(jnp.bfloat16)


def fold_rows(left_rows, weight):
    return jnp.dot(
        left_rows,
        lax.all_gather(weight, "grp", axis=0, tiled=True),
        preferred_element_type=jnp.float32,
    )


def map_rows(gradient, weight):
    return lax.dot_general(
        gradient,
        lax.all_gather(weight, "grp", axis=0, tiled=True),
        (((1,), (1,)), ((), ())),
        preferred_element_type=jnp.float32,
    )


def row_shares(left_rows, gradient):
    return lax.psum_scatter(
        lax.dot_general(
            left_rows, gradient, (((0,), (0,)), ((), ())), preferred_element_type=jnp.float32
        ),
        "grp",
        scatter_dimension=0,
        tiled=True,
    )


def masked_scores(query_rows, key_row_block, query_pos, key_pos, prefix):
    scores = lax.dot_general(
        query_rows, key_row_block, (((1,), (1,)), ((), ())), preferred_element_type=jnp.float32
    )
    scores = scores * query_rows.shape[1] ** (-0.5)
    allowed = (key_pos[None, :] <= query_pos[:, None]) | (key_pos[None, :] < prefix)
    return jnp.where(allowed, scores, MASK_FLOOR)


def per_device(
    layer_input,
    w_qkv,
    w_out,
    w_in,
    w_down,
    attn_gain,
    ffn_gain,
    q_gain,
    k_gain,
    cotangent,
    prefix_len,
    seq_slot,
):
    inputs_f = layer_input[0].astype(jnp.float32)
    token_rows = inputs_f.shape[0]
    member = lax.axis_index("grp")
    sequence_length = token_rows * lax.axis_size("grp")
    query_width = QUERY_HEADS * HEAD_SIZE
    key_value_width = KEY_VALUE_HEADS * HEAD_SIZE
    group_width = QUERY_HEADS // KEY_VALUE_HEADS
    positions = member * token_rows + jnp.arange(token_rows, dtype=jnp.int32)
    key_pos = jnp.arange(sequence_length, dtype=jnp.int32)
    query_pos = jnp.tile(positions, group_width)
    slot_ids = jnp.arange(prefix_len.shape[0], dtype=jnp.int32)
    prefix = jnp.sum(jnp.where(slot_ids == seq_slot[0], prefix_len, 0))
    cos_table, sin_table = rope_tables(positions, HEAD_SIZE)
    scaled_one, normed_one, inv_one = norm_forward(inputs_f, attn_gain)
    xn_low = scaled_one.astype(jnp.bfloat16)
    query_key_value = fold_rows(xn_low, w_qkv)
    queries = query_key_value[:, :query_width].reshape(token_rows, QUERY_HEADS, HEAD_SIZE)
    key_entries = query_key_value[:, query_width : query_width + key_value_width].reshape(
        token_rows, KEY_VALUE_HEADS, HEAD_SIZE
    )
    value_row_block = query_key_value[:, query_width + key_value_width :]
    q_scaled, q_normed, q_inv = norm_forward(queries, q_gain)
    k_scaled, k_normed, k_inv = norm_forward(key_entries, k_gain)
    query_lowered = rotate(q_scaled, cos_table, sin_table).astype(jnp.bfloat16)
    k_low = rotate(k_scaled, cos_table, sin_table).astype(jnp.bfloat16)
    local_kv = jnp.concatenate(
        [k_low.reshape(token_rows, key_value_width), value_row_block.astype(jnp.bfloat16)], axis=1
    )
    full_key_value = lax.all_gather(local_kv, "grp", axis=0, tiled=True)
    head_keys = (
        full_key_value[:, :key_value_width]
        .reshape(sequence_length, KEY_VALUE_HEADS, HEAD_SIZE)
        .transpose(1, 0, 2)
    )
    head_values = (
        full_key_value[:, key_value_width:]
        .reshape(sequence_length, KEY_VALUE_HEADS, HEAD_SIZE)
        .transpose(1, 0, 2)
    )
    head_queries = (
        query_lowered.reshape(token_rows, KEY_VALUE_HEADS, group_width, HEAD_SIZE)
        .transpose(1, 2, 0, 3)
        .reshape(KEY_VALUE_HEADS, group_width * token_rows, HEAD_SIZE)
    )

    def head_forward(operands):
        head_q, head_k, head_v = operands
        scores = masked_scores(head_q, head_k, query_pos, key_pos, prefix)
        row_top = jnp.max(scores, axis=1, keepdims=True)
        exp_scores = jnp.exp(scores - row_top)
        row_total = jnp.sum(exp_scores, axis=1, keepdims=True)
        probabilities = (exp_scores / row_total).astype(jnp.bfloat16)
        head_out = jnp.dot(probabilities, head_v, preferred_element_type=jnp.float32)
        return (head_out, (row_top + jnp.log(row_total))[:, 0])

    attn_heads, log_sums = lax.map(head_forward, (head_queries, head_keys, head_values))
    attn_low = (
        attn_heads.astype(jnp.bfloat16)
        .reshape(KEY_VALUE_HEADS, group_width, token_rows, HEAD_SIZE)
        .transpose(2, 0, 1, 3)
        .reshape(token_rows, query_width)
    )
    hidden_f = inputs_f + fold_rows(attn_low, w_out)
    scaled_two, normed_two, inv_two = norm_forward(hidden_f, ffn_gain)
    hn_low = scaled_two.astype(jnp.bfloat16)
    grad_low = cotangent[0]
    grad_out_f = grad_low.astype(jnp.float32)
    gathered_hn, gathered_grad = (
        lax.all_gather(hn_low, "grp", axis=0, tiled=True),
        lax.all_gather(grad_low, "grp", axis=0, tiled=True),
    )
    proj_all = jnp.einsum("td,fgd->tgf", gathered_hn, w_in, preferred_element_type=jnp.float32)
    mixed_all = (jax.nn.silu(proj_all[:, 0]) * proj_all[:, 1]).astype(jnp.bfloat16)
    row_block = mixed_all
    branch_ffn = lax.psum_scatter(
        jnp.dot(row_block, w_down, preferred_element_type=jnp.float32),
        "grp",
        scatter_dimension=0,
        tiled=True,
    )
    grad_mixed = lax.dot_general(
        gathered_grad, w_down, (((1,), (1,)), ((), ())), preferred_element_type=jnp.float32
    )
    grad_proj = silu_back(proj_all[:, 0], proj_all[:, 1], grad_mixed)
    d_w_in_part = jnp.einsum(
        "tgf,td->fgd", grad_proj, gathered_hn, preferred_element_type=jnp.float32
    )
    d_w_down_part = lax.dot_general(
        mixed_all, gathered_grad, (((0,), (0,)), ((), ())), preferred_element_type=jnp.float32
    )
    row_block = grad_proj
    grad_hn = lax.psum_scatter(
        jnp.einsum("tgf,fgd->td", row_block, w_in, preferred_element_type=jnp.float32),
        "grp",
        scatter_dimension=0,
        tiled=True,
    )
    out_low = (hidden_f + branch_ffn).astype(jnp.bfloat16)
    d_ffn_gain = jnp.sum(grad_hn * normed_two, axis=0)
    grad_hidden = grad_out_f + norm_back(grad_hn, normed_two, inv_two, ffn_gain)
    grad_attn = grad_hidden.astype(jnp.bfloat16)
    d_w_out_part = row_shares(attn_low, grad_attn)
    head_gradient = map_rows(grad_attn, w_out).astype(jnp.bfloat16)
    grad_head_rows = (
        head_gradient.reshape(token_rows, KEY_VALUE_HEADS, group_width, HEAD_SIZE)
        .transpose(1, 2, 0, 3)
        .reshape(KEY_VALUE_HEADS, group_width * token_rows, HEAD_SIZE)
    )

    def head_backward(operands):
        head_q, head_k, head_v, head_grad, head_lse = operands
        scores = masked_scores(head_q, head_k, query_pos, key_pos, prefix)
        probabilities = jnp.exp(scores - head_lse[:, None])
        probs_low = probabilities.astype(jnp.bfloat16)
        grad_probs = lax.dot_general(
            head_grad, head_v, (((1,), (1,)), ((), ())), preferred_element_type=jnp.float32
        )
        inner = jnp.sum(probabilities * grad_probs, axis=1, keepdims=True)
        grad_scores = (probabilities * (grad_probs - inner)).astype(jnp.bfloat16)
        scale_factor = head_q.shape[1] ** (-0.5)
        grad_query = jnp.dot(grad_scores, head_k, preferred_element_type=jnp.float32) * scale_factor
        grad_key = (
            lax.dot_general(
                grad_scores, head_q, (((0,), (0,)), ((), ())), preferred_element_type=jnp.float32
            )
            * scale_factor
        )
        grad_value = lax.dot_general(
            probs_low, head_grad, (((0,), (0,)), ((), ())), preferred_element_type=jnp.float32
        )
        return (grad_query, grad_key, grad_value)

    query_head_gradient, grad_k_heads, grad_v_heads = lax.map(
        head_backward, (head_queries, head_keys, head_values, grad_head_rows, log_sums)
    )
    grad_kv_full = jnp.concatenate(
        [
            grad_k_heads.transpose(1, 0, 2).reshape(sequence_length, key_value_width),
            grad_v_heads.transpose(1, 0, 2).reshape(sequence_length, key_value_width),
        ],
        axis=1,
    )
    key_value_gradient = lax.psum_scatter(grad_kv_full, "grp", scatter_dimension=0, tiled=True)
    grad_q_rot = (
        query_head_gradient.reshape(KEY_VALUE_HEADS, group_width, token_rows, HEAD_SIZE)
        .transpose(2, 0, 1, 3)
        .reshape(token_rows, QUERY_HEADS, HEAD_SIZE)
    )
    rotated_key_gradient = key_value_gradient[:, :key_value_width].reshape(
        token_rows, KEY_VALUE_HEADS, HEAD_SIZE
    )
    grad_values = key_value_gradient[:, key_value_width:]
    grad_q_norm = unrotate(grad_q_rot, cos_table, sin_table)
    grad_k_norm = unrotate(rotated_key_gradient, cos_table, sin_table)
    d_q_gain = jnp.sum(grad_q_norm * q_normed, axis=(0, 1))
    d_k_gain = jnp.sum(grad_k_norm * k_normed, axis=(0, 1))
    grad_queries = norm_back(grad_q_norm, q_normed, q_inv, q_gain)
    grad_keys = norm_back(grad_k_norm, k_normed, k_inv, k_gain)
    grad_qkv = jnp.concatenate(
        [
            grad_queries.reshape(token_rows, query_width),
            grad_keys.reshape(token_rows, key_value_width),
            grad_values,
        ],
        axis=1,
    ).astype(jnp.bfloat16)
    d_w_qkv_part = row_shares(xn_low, grad_qkv)
    grad_xn = map_rows(grad_qkv, w_qkv)
    d_attn_gain = jnp.sum(grad_xn * normed_one, axis=0)
    input_side = grad_hidden + norm_back(grad_xn, normed_one, inv_one, attn_gain)
    gain_totals = lax.psum((d_attn_gain, d_ffn_gain, d_q_gain, d_k_gain), ("rep", "grp"))
    weight_totals = lax.psum((d_w_qkv_part, d_w_out_part, d_w_in_part, d_w_down_part), "rep")
    return (
        out_low[None],
        input_side[None],
        weight_totals[0],
        weight_totals[1],
        weight_totals[2],
        weight_totals[3],
        gain_totals[0],
        gain_totals[1],
        gain_totals[2],
        gain_totals[3],
    )


def solution(mesh):
    in_specs = (
        P("rep", "grp", None),
        P("grp", None),
        P("grp", None),
        P("grp", None, None),
        P("grp", None),
        P(),
        P(),
        P(),
        P(),
        P("rep", "grp", None),
        P(),
        P("rep"),
    )
    out_specs = (
        P("rep", "grp", None),
        P("rep", "grp", None),
        P("grp", None),
        P("grp", None),
        P("grp", None, None),
        P("grp", None),
        P(),
        P(),
        P(),
        P(),
    )
    return jax.shard_map(
        per_device, mesh=mesh, in_specs=in_specs, out_specs=out_specs, check_vma=False
    )
```

profile of v0, /device:TPU:0, one launch (start us, length us, event | category | flops | bytes accessed | tf_op | source)
XLA Modules:
  0.0 1868.8 jit_solution(347175399952361775)
XLA Ops:
  8.9 144.5 %all-gather.7.cloned.1.call-done = bf16[2048,1920]{1,0:T(8,128)(2,1)} async-done(((bf16[512,1920]{1,0:T(8,128)(2,1)}), bf16[2048,1920]{1,0:T(8,128)(2,1)}) %all-gather.7.cloned.1.call-update) | async-done | bytes 7864336 | tf_op jit(solution)/shard_map/all_gather | solution.py:69
  153.4 5.6 fusion.97
  175.2 22.9 %all-gather.9.cloned.1.call-done = bf16[1024,640]{1,0:T(8,128)(2,1)} async-done(((bf16[256,640]{1,0:T(8,128)(2,1)}), bf16[1024,640]{1,0:T(8,128)(2,1)}) %all-gather.9.cloned.1.call-update) | async-done | bytes 1310736 | tf_op jit(solution)/shard_map/all_gather | solution.py:145
  208.7 41.3 %while.32 = (s32[]{:T(128)}, bf16[5,1024,64]{1,2,0:T(8,128)(2,1)}, f32[5,1024]{1,0:T(8,128)S(1)}, s32[]{:T(128)}, bf16[5,1024,64]{2,1,0:T(8,128)(2,1)S(1)}, /*in...) while((s32[]{:T(128)}, bf16[5,1024,64]{1,2,0:T(8,128)(2,1)}, ...), condition=%wide.region_7.8_spmd.clone.clone.clone, body=%wide.region_4.7_spmd.clone.clone.sunk.clone | while | flops 287309824 | bytes 13704293 | solution.py:172
  253.2 43.5 %all-gather.11.cloned.1.call-done = bf16[1280,2048]{1,0:T(8,128)(2,1)} async-done(((bf16[320,2048]{1,0:T(8,128)(2,1)}), bf16[1280,2048]{1,0:T(8,128)(2,1)}) %all-gather.11.cloned.1.call-update) | async-done | bytes 5242896 | tf_op jit(solution)/shard_map/all_gather | solution.py:69
  303.5 78.1 %all-gather.13.cloned.1.call-done = bf16[1024,2048]{1,0:T(8,128)(2,1)} async-done(((bf16[256,2048]{1,0:T(8,128)(2,1)}), bf16[1024,2048]{1,0:T(8,128)(2,1)}) %all-gather.13.cloned.1.call-update) | async-done | bytes 4194320 | tf_op jit(solution)/shard_map/all_gather | solution.py:185
  381.6 28.6 %fusion.62 = f32[1024,2,1280]{2,0,1:T(8,128)} fusion(bf16[1280,2,2048]{2,1,0:T(2,128)(2,1)} %param.19, bf16[1024,2048]{1,0:T(8,128)(2,1)} %all-gather.13.cloned.1.call-done), kind=kOutput, calls=%fused_computation.71 | convolution fusion | flops 10737418240 | bytes 25165824 | tf_op jit(solution)/shard_map/td,fgd->tgf/dot_general | solution.py:188
  410.2 52.2 %all-gather.15.cloned.1.call-done = bf16[1,1024,2048]{2,1,0:T(8,128)(2,1)} async-done(((bf16[1,256,2048]{2,1,0:T(8,128)(2,1)}), bf16[1,1024,2048]{2,1,0:T(8,128)(2,1)}) %all-gather.15.cloned.1.call-update) | async-done | bytes 4194320 | tf_op jit(solution)/shard_map/all_gather | solution.py:186
  462.4 14.0 fusion.80
  478.8 16.3 fusion.66
  495.2 10.7 fusion.106
  506.0 132.3 %reduce-scatter.8.cloned.1.call-done = f32[256,2048]{1,0:T(8,128)} async-done(((f32[1024,2048]{1,0:T(8,128)}), f32[256,2048]{1,0:T(8,128)}) %reduce-scatter.8.cloned.1.call-update) | async-done | bytes 2097168 | tf_op jit(solution)/shard_map/reduce_scatter | solution.py:208
  641.0 145.4 %reduce-scatter.6.cloned.1.call-done = f32[256,2048]{1,0:T(8,128)} async-done(((f32[1024,2048]{1,0:T(8,128)}), f32[256,2048]{1,0:T(8,128)}) %reduce-scatter.6.cloned.1.call-update) | async-done | bytes 2097168 | tf_op jit(solution)/shard_map/reduce_scatter | solution.py:191
  797.1 60.1 %while.33 = (s32[]{:T(128)}, f32[5,1024,64]{1,2,0:T(8,128)}, f32[5,1024,64]{1,2,0:T(8,128)}, f32[5,1024,64]{1,2,0:T(8,128)S(1)}, s32[]{:T(128)}, /*index=5*/bf16...) while((s32[]{:T(128)}, f32[5,1024,64]{1,2,0:T(8,128)}, ...), condition=%wide.region_14.15_spmd.clone.clone.clone, body=%wide.region_12.14_spmd.clone.clone.sunk.clone | while | flops 682754048 | bytes 34123900 | solution.py:249
  885.2 31.7 %reduce-scatter.10.cloned.1.call-done = f32[256,640]{1,0:T(8,128)} async-done(((f32[1024,640]{1,0:T(8,128)}), f32[256,640]{1,0:T(8,128)}) %reduce-scatter.10.cloned.1.call-update) | async-done | bytes 655376 | tf_op jit(solution)/shard_map/reduce_scatter | solution.py:259
  924.3 9.2 fusion.95
  933.6 11.3 fusion.69
  944.9 14.6 convolution_bitcast_fusion
  959.5 138.1 %reduce-scatter.14.cloned.1.call-done = f32[320,2048]{1,0:T(8,128)} async-done(((f32[1280,2048]{1,0:T(8,128)}), f32[320,2048]{1,0:T(8,128)}) %reduce-scatter.14.cloned.1.call-update) | async-done | bytes 2621456 | tf_op jit(solution)/shard_map/reduce_scatter | solution.py:84
  1097.6 265.9 %reduce-scatter.12.cloned.1.call-done = f32[512,1920]{1,0:T(8,128)} async-done(((f32[2048,1920]{1,0:T(8,128)}), f32[512,1920]{1,0:T(8,128)}) %reduce-scatter.12.cloned.1.call-update) | async-done | bytes 3932176 | tf_op jit(solution)/shard_map/reduce_scatter | solution.py:84
  1365.7 7.3 fusion.87
  1373.0 42.3 %all-reduce = (f32[2048]{0:T(1024)}, f32[2048]{0:T(1024)}, f32[64]{0:T(128)}, f32[64]{0:T(128)}) all-reduce(f32[2048]{0:T(1024)S(1)} %get-tuple-element.357, f32[2048]{0:T(1024)S(1)} %copy-done.28, f32[64]{0:T(128)S(1)} %reduce_sum.162, f32[64]{0:T(128)S(1)} %reduce_sum.165), channel_id=1, replica_groups=mesh['rep'=8,'grp'=4] {'rep','grp'}, use_global_device_ids=true, to_apply=%region_26.27 | all-reduce | flops 4224 | bytes 33792 | tf_op jit(solution)/shard_map/psum | solution.py:287
  1418.9 399.8 %all-reduce.4.cloned.1.call-done = (f32[512,1920]{1,0:T(8,128)}, f32[320,2048]{1,0:T(8,128)}, f32[1280,2,2048]{0,2,1:T(8,128)}, f32[1280,2048]{1,0:T(8,128)}) async-done(((f32[512,1920]{1,0:T(8,128)}, f32[320,2048]{1,0:T(8,128)}, f32[1280,2,2048]{0,2,1:T(8,128)}, f32[1280,2048]{1,0:T(8,128)}), (f32[512,1920]{1,0:T(8,128)}, f32[320,2048]{1,0:T(8,128)}, f32[1280,2,2048]{0,2,1:T(8,128)}, ...) | async-done | bytes 38010896 | tf_op jit(solution)/shard_map/psum | solution.py:288
  1818.8 31.4 %copy.158 = f32[1280,2,2048]{2,1,0:T(2,128)} copy(f32[1280,2,2048]{0,2,1:T(8,128)} %get-tuple-element.403) | data formatting | bytes 41943040
  (279 shorter events, 206.8 us)
Async XLA Ops:
  7.2 146.2 %copy-start.26 = (f32[2048]{0:T(1024)S(1)}, f32[2048]{0:T(1024)}, u32[]{:S(2)}) copy-start(f32[2048]{0:T(1024)} %param.21) | copy-start | bytes 24580
  7.2 146.2 %all-gather.7.cloned.1.call-start = ((), (), s32[]{:S(2)}) async-start(), calls=%async_computation.5 | async-start | bytes 9830400 | tf_op jit(solution)/shard_map/all_gather | solution.py:69
  7.9 190.1 %all-gather.9.cloned.1.call-start = ((), (), s32[]{:S(2)}) async-start(), calls=%async_computation.6 | async-start | bytes 1638400 | tf_op jit(solution)/shard_map/all_gather | solution.py:145
  8.7 150.3 %copy-start.30 = (f32[256]{0:T(256)}, f32[256]{0:T(256)S(1)}, u32[]{:S(2)}) copy-start(f32[256]{0:T(256)S(1)} %add_rsqrt_fusion.3) | copy-start | bytes 3076
  8.9 164.8 %copy-start.17 = (f32[256,32]{0,1:T(8,128)}, f32[256,32]{0,1:T(8,128)S(1)}, u32[]{:S(2)}) copy-start(f32[256,32]{0,1:T(8,128)S(1)} %get-tuple-element.432) | copy-start | bytes 98308
  8.9 164.8 %copy-start.19 = (f32[256,32]{0,1:T(8,128)}, f32[256,32]{0,1:T(8,128)S(1)}, u32[]{:S(2)}) copy-start(f32[256,32]{0,1:T(8,128)S(1)} %get-tuple-element.433) | copy-start | bytes 98308
  159.0 11.3 copy-start.10
  167.0 129.7 %all-gather.11.cloned.1.call-start = ((), (), s32[]{:S(2)}) async-start(), calls=%async_computation.7 | async-start | bytes 6553600 | tf_op jit(solution)/shard_map/all_gather | solution.py:69
  167.8 213.9 %all-gather.13.cloned.1.call-start = ((), (), s32[]{:S(2)}) async-start(), calls=%async_computation.8 | async-start | bytes 5242880 | tf_op jit(solution)/shard_map/all_gather | solution.py:185
  250.0 46.7 %copy-start.11 = (bf16[5,1024,64]{2,1,0:T(8,128)(2,1)}, bf16[5,1024,64]{2,1,0:T(8,128)(2,1)S(1)}, u32[]{:S(2)}) copy-start(bf16[5,1024,64]{2,1,0:T(8,128)(2,1)S(1)} %get-tuple-element.713) | copy-start | bytes 1966084
  302.4 160.0 %all-gather.15.cloned.1.call-start = ((), (), s32[]{:S(2)}) async-start(), calls=%async_computation.14 | async-start | bytes 5242880 | tf_op jit(solution)/shard_map/all_gather | solution.py:186
  302.9 335.3 %reduce-scatter.8.cloned.1.call-start = ((), (), s32[]{:S(2)}) async-start(), calls=%async_computation.10 | async-start | bytes 10485760 | tf_op jit(solution)/shard_map/reduce_scatter | solution.py:208
  495.1 291.3 %reduce-scatter.6.cloned.1.call-start = ((), (), s32[]{:S(2)}) async-start(), calls=%async_computation.9 | async-start | bytes 10485760 | tf_op jit(solution)/shard_map/reduce_scatter | solution.py:191
  505.9 411.1 %reduce-scatter.10.cloned.1.call-start = ((), (), s32[]{:S(2)}) async-start(), calls=%async_computation.11 | async-start | bytes 3276800 | tf_op jit(solution)/shard_map/reduce_scatter | solution.py:259
  506.0 280.5 %copy-start.12 = (bf16[1,256,2048]{2,1,0:T(8,128)(2,1)S(1)}, bf16[1,256,2048]{2,1,0:T(8,128)(2,1)}, u32[]{:S(2)}) copy-start(bf16[1,256,2048]{2,1,0:T(8,128)(2,1)} %param.25) | copy-start | bytes 3145732
  864.0 233.6 %reduce-scatter.14.cloned.1.call-start = ((), (), s32[]{:S(2)}) async-start(), calls=%async_computation.13 | async-start | bytes 13107200 | tf_op jit(solution)/shard_map/reduce_scatter | solution.py:84
  871.2 492.3 %reduce-scatter.12.cloned.1.call-start = ((), (), s32[]{:S(2)}) async-start(), calls=%async_computation.12 | async-start | bytes 19660800 | tf_op jit(solution)/shard_map/reduce_scatter | solution.py:84
  885.2 33.0 %copy-start.9 = (f32[256,320]{0,1:T(8,128)S(1)}, f32[256,320]{0,1:T(8,128)}, u32[]{:S(2)}) copy-start(f32[256,320]{0,1:T(8,128)} %copy-done.8) | copy-start | bytes 983044
  885.2 33.0 %copy-start.24 = (f32[256,5]{0,1:T(8,128)S(1)}, f32[256,5]{0,1:T(8,128)}, u32[]{:S(2)}) copy-start(f32[256,5]{0,1:T(8,128)} %copy-done.23) | copy-start | bytes 15364
  933.5 885.2 %all-reduce.4.cloned.1.call-start = ((), (), s32[]{:S(2)}) async-start(), calls=%async_computation.15 | async-start | bytes 76021760 | tf_op jit(solution)/shard_map/psum | solution.py:288
  933.6 11.3 copy-start.36
  933.6 11.3 copy-start.39
  933.6 11.3 copy-start.41
  1818.8 35.9 %copy-start.15 = (f32[320,2048]{1,0:T(8,128)S(1)}, f32[320,2048]{1,0:T(8,128)}, u32[]{:S(2)}) copy-start(f32[320,2048]{1,0:T(8,128)} %get-tuple-element.670) | copy-start | bytes 7864324
  (29 other events, 78.7 us)
Sparse Core Ops, SparseCore 0:
  9.6 143.7 all-gather.6
  167.1 30.9 all-gather.8
  199.7 97.0 all-gather.10
  302.5 79.1 all-gather.12
  383.1 79.2 all-gather.14
  495.2 143.0 reduce-scatter.7
  641.2 145.1 reduce-scatter.5
  864.1 52.8 reduce-scatter.9
  919.9 177.6 reduce-scatter.13
  1099.8 263.6 reduce-scatter.11
  1368.3 450.3 all-reduce.3
where the time goes:
time: 1870 us
  waiting for transfers between devices  1460 us (78%)
  matrix products  211 us (11%)
  local copies, waits for them, and re-layouts  92.3 us (5%)
  other arithmetic  49.7 us (3%)
  blocking collectives  42.3 us (2%)
    reduce_scatter x2, waiting for transfers between devices, row_shares(): lax.psum_scatter(lax.dot_general(left_rows, gradient, (((0,), (0,)), ((),...  404 us
    psum x1, waiting for transfers between devices, per_device(): lax.psum((d_w_qkv_part, d_w_out_part, d_w_in_part, d_w_down_part), 'rep')  400 us
    all_gather x2, waiting for transfers between devices, fold_rows(): lax.all_gather(weight, 'grp', axis=0, tiled=True)  188 us
    reduce_scatter x1, waiting for transfers between devices, per_device(): lax.psum_scatter(jnp.dot(row_block, w_down, preferred_element_type=jnp.fl...  145 us
    reduce_scatter x1, waiting for transfers between devices, per_device(): lax.psum_scatter(jnp.einsum('tgf,fgd->td', row_block, w_in, preferred_ele...  132 us
    all_gather x1, waiting for transfers between devices, per_device(): lax.all_gather(hn_low, 'grp', axis=0, tiled=True)  78.1 us
    unnamed x93, local copies, waits for them, and re-layouts  59.6 us
    all_gather x1, waiting for transfers between devices, per_device(): lax.all_gather(grad_low, 'grp', axis=0, tiled=True)  52.2 us
  transfers between devices with their start and end apart: 11, of which 11 were waited for; matrix products, arithmetic and copies ran while one was open for 9% of the time, Pallas kernels for 0%

commit v1 on v0

v1 whole, which is shorter than its diff:
```python
import functools

import jax
import jax.numpy as jnp
from jax import lax
from jax.experimental import pallas as pl
from jax.experimental.pallas import tpu as pltpu
from jax.sharding import PartitionSpec as P

QUERY_HEADS = 20
KEY_VALUE_HEADS = 5
HEAD_SIZE = 64
GROUP = QUERY_HEADS // KEY_VALUE_HEADS
QUERY_WIDTH = QUERY_HEADS * HEAD_SIZE
KEY_VALUE_WIDTH = KEY_VALUE_HEADS * HEAD_SIZE
NORM_EPSILON = 1e-06
ROPE_THETA = 10000.0
LOG2E = 1.4426950408889634
BF = jnp.bfloat16
F32 = jnp.float32


def dot(a, b, ca, cb):
    return lax.dot_general(a, b, (((ca,), (cb,)), ((), ())), preferred_element_type=F32)


def rep_orders():
    bits = lax.axis_size("rep").bit_length() - 1
    rest = list(range(1, bits))
    return [0] + rest, [0] + rest[::-1]


def bit_of(b):
    return (lax.axis_index("rep") >> b) & 1


def swap(x, b):
    n = lax.axis_size("rep")
    return lax.ppermute(x, "rep", [(i, i ^ (1 << b)) for i in range(n)])


def place_of(order):
    place = 0
    for b in order:
        place = place * 2 + bit_of(b)
    return place


def rep_scatter(x, order, axis):
    for b in order:
        half = x.shape[axis] // 2
        bit = bit_of(b)
        away = lax.dynamic_slice_in_dim(x, (1 - bit) * half, half, axis).astype(BF)
        keep = lax.dynamic_slice_in_dim(x, bit * half, half, axis)
        x = keep.astype(F32) + swap(away, b).astype(F32)
    return x


def rep_gather(x, order, axis):
    for b in order[::-1]:
        other = swap(x, b)
        x = jnp.where(
            bit_of(b) == 0,
            jnp.concatenate([x, other], axis),
            jnp.concatenate([other, x], axis),
        )
    return x


EDGE = [(0, 1), (1, 0), (2, 3), (3, 2)]
MID = [(1, 2), (2, 1)]
OUTWARD = [(1, 0), (2, 3)]
INWARD = [(0, 1), (3, 2)]


def ring(n):
    return [(i, (i + 1) % n) for i in range(n)]


def slot_sources():
    n = lax.axis_size("grp")
    g = lax.axis_index("grp")
    if n == 4:
        return [g, g ^ 1, jnp.where(g < 2, 2, 1), jnp.where(g < 2, 3, 0)]
    return [lax.rem(g + n - k, n) for k in range(n)]


def spread(x):
    n = lax.axis_size("grp")
    if n == 4:
        g = lax.axis_index("grp")
        middle = (g == 1) | (g == 2)
        p1 = lax.ppermute(x, "grp", EDGE)
        p2 = lax.ppermute(x, "grp", MID)
        p3 = lax.ppermute(p1, "grp", MID)
        p4 = lax.ppermute(p2, "grp", OUTWARD)
        p5 = lax.ppermute(p3, "grp", OUTWARD)
        return [x, p1, jnp.where(middle, p2, p4), jnp.where(middle, p3, p5)]
    slots = [x]
    for _ in range(n - 1):
        slots.append(lax.ppermute(slots[-1], "grp", ring(n)))
    return slots


def collect(parts):
    n = lax.axis_size("grp")

    def send(x, pairs):
        return lax.ppermute(x.astype(BF), "grp", pairs).astype(F32)

    if n == 4:
        q1 = send(parts[3], INWARD)
        q2 = send(parts[3] + q1, MID)
        q3 = send(parts[2], INWARD)
        q4 = send(parts[2] + q3, MID)
        q5 = send(parts[1] + q2, EDGE)
        return parts[0] + q4 + q5
    total = parts[1]
    for k in list(range(2, n)) + [0]:
        total = send(total, ring(n)) + parts[k]
    return total


def fetch_shards(w, axis):
    n = lax.axis_size("grp")
    g = lax.axis_index("grp")
    orders = rep_orders()
    half = w.shape[axis] // 2
    size = half // lax.axis_size("rep")
    pieces = [
        lax.dynamic_slice_in_dim(w, i * half + place_of(order) * size, size, axis)
        for i, order in enumerate(orders)
    ]
    mine = jnp.stack(pieces)
    shards = []
    for k in range(1, n):
        there = lax.ppermute(mine, "grp", [(i, (i + k) % n) for i in range(n)])
        shards.append(there)
    there = jnp.stack(shards, 1)
    halves = [rep_gather(there[i], order, axis + 1) for i, order in enumerate(orders)]
    whole = jnp.concatenate(halves, axis + 1)
    return [(lax.rem(g + n - k, n), whole[k - 1]) for k in range(1, n)]


def assemble(w, shards):
    g = lax.axis_index("grp")
    rows = w.shape[0]
    full = jnp.zeros((rows * lax.axis_size("grp"), w.shape[1]), w.dtype)
    for source, shard in [(g, w)] + shards:
        full = lax.dynamic_update_slice_in_dim(full, shard, source * rows, 0)
    return full


def sum_everywhere(x):
    for b in range(lax.axis_size("rep").bit_length() - 1):
        x = x + swap(x, b)
    n = lax.axis_size("grp")
    for b in range(n.bit_length() - 1):
        x = x + lax.ppermute(x, "grp", [(i, i ^ (1 << b)) for i in range(n)])
    return x


def mask_limit(info_ref, tokens):
    query_pos = info_ref[1] + lax.broadcasted_iota(jnp.int32, (1, tokens), 1)
    return jnp.maximum(query_pos + 1, info_ref[0])


def forward_kernel(info_ref, q_ref, k_ref, v_ref, o_ref, of_ref, inv_ref):
    slots, _, tokens = k_ref.shape
    limit = mask_limit(info_ref, tokens)
    for h in range(GROUP):
        rows = slice(h * HEAD_SIZE, (h + 1) * HEAD_SIZE)
        q = q_ref[rows, :]
        total = jnp.zeros((1, tokens), F32)
        acc = jnp.zeros((HEAD_SIZE, tokens), F32)
        for s in range(slots):
            key_pos = info_ref[2 + s] + lax.broadcasted_iota(jnp.int32, (tokens, tokens), 0)
            t = dot(k_ref[s], q, 0, 0) * (HEAD_SIZE**-0.5 * LOG2E)
            e = jnp.where(key_pos < limit, jnp.exp2(t), 0.0)
            total = total + jnp.sum(e, axis=0, keepdims=True)
            acc = acc + dot(v_ref[s], e.astype(BF), 1, 0)
        inv = 1.0 / total
        out = acc * inv
        o_ref[rows, :] = out.astype(BF)
        of_ref[rows, :] = out
        inv_ref[0, h : h + 1, :] = inv


def backward_kernel(info_ref, q_ref, k_ref, v_ref, g_ref, of_ref, inv_ref, dq_ref, dk_ref, dv_ref):
    slots, _, tokens = k_ref.shape
    limit = mask_limit(info_ref, tokens)
    for h in range(GROUP):
        rows = slice(h * HEAD_SIZE, (h + 1) * HEAD_SIZE)
        q = q_ref[rows, :]
        grad = g_ref[rows, :]
        inv = inv_ref[0, h : h + 1, :]
        delta = jnp.sum(of_ref[rows, :] * grad.astype(F32), axis=0, keepdims=True)
        acc = jnp.zeros((HEAD_SIZE, tokens), F32)
        for s in range(slots):
            key_pos = info_ref[2 + s] + lax.broadcasted_iota(jnp.int32, (tokens, tokens), 0)
            t = dot(k_ref[s], q, 0, 0) * (HEAD_SIZE**-0.5 * LOG2E)
            p = jnp.where(key_pos < limit, jnp.exp2(t) * inv, 0.0)
            dp = dot(v_ref[s], grad, 0, 0)
            ds = (p * (dp - delta)).astype(BF)
            acc = acc + dot(k_ref[s], ds, 1, 0)
            dk = dot(q, ds, 1, 1) * HEAD_SIZE**-0.5
            dv = dot(grad, p.astype(BF), 1, 1)
            if h == 0:
                dk_ref[s] = dk
                dv_ref[s] = dv
            else:
                dk_ref[s] += dk
                dv_ref[s] += dv
        dq_ref[rows, :] = acc * HEAD_SIZE**-0.5


def attention_specs(slots, tokens):
    heads = pl.BlockSpec((GROUP * HEAD_SIZE, tokens), lambda c, info: (c, 0))
    keys = pl.BlockSpec((slots, HEAD_SIZE, tokens), lambda c, info: (0, c, 0))
    values = pl.BlockSpec((slots, HEAD_SIZE, tokens), lambda c, info: (0, KEY_VALUE_HEADS + c, 0))
    inverse = pl.BlockSpec((1, GROUP, tokens), lambda c, info: (c, 0, 0))
    return heads, keys, values, inverse


def attention_forward(info, q, kv):
    slots, _, tokens = kv.shape
    heads, keys, values, inverse = attention_specs(slots, tokens)
    return pl.pallas_call(
        forward_kernel,
        grid_spec=pltpu.PrefetchScalarGridSpec(
            num_scalar_prefetch=1,
            grid=(KEY_VALUE_HEADS,),
            in_specs=[heads, keys, values],
            out_specs=[heads, heads, inverse],
        ),
        out_shape=[
            jax.ShapeDtypeStruct((QUERY_WIDTH, tokens), BF),
            jax.ShapeDtypeStruct((QUERY_WIDTH, tokens), F32),
            jax.ShapeDtypeStruct((KEY_VALUE_HEADS, GROUP, tokens), F32),
        ],
        compiler_params=pltpu.CompilerParams(vmem_limit_bytes=48 * 2**20),
        cost_estimate=pl.CostEstimate(
            flops=16 * slots * tokens * tokens * QUERY_WIDTH,
            bytes_accessed=8 * QUERY_WIDTH * tokens,
            transcendentals=QUERY_HEADS * slots * tokens * tokens,
        ),
        name="attention_forward",
    )(info, q, kv, kv)


def attention_backward(info, q, kv, grad, of, inv):
    slots, _, tokens = kv.shape
    heads, keys, values, inverse = attention_specs(slots, tokens)
    return pl.pallas_call(
        backward_kernel,
        grid_spec=pltpu.PrefetchScalarGridSpec(
            num_scalar_prefetch=1,
            grid=(KEY_VALUE_HEADS,),
            in_specs=[heads, keys, values, heads, heads, inverse],
            out_specs=[heads, keys, keys],
        ),
        out_shape=[
            jax.ShapeDtypeStruct((QUERY_WIDTH, tokens), F32),
            jax.ShapeDtypeStruct((slots, KEY_VALUE_WIDTH, tokens), F32),
            jax.ShapeDtypeStruct((slots, KEY_VALUE_WIDTH, tokens), F32),
        ],
        compiler_params=pltpu.CompilerParams(vmem_limit_bytes=48 * 2**20),
        cost_estimate=pl.CostEstimate(
            flops=40 * slots * tokens * tokens * QUERY_WIDTH,
            bytes_accessed=16 * QUERY_WIDTH * tokens,
            transcendentals=QUERY_HEADS * slots * tokens * tokens,
        ),
        name="attention_backward",
    )(info, q, kv, kv, grad, of, inv)


def inverse_rms(values, axis):
    return lax.rsqrt(jnp.mean(values * values, axis=axis, keepdims=True) + NORM_EPSILON)


def norm_back(grad_out, normed, inv_scale, gain, axis):
    scaled = grad_out * gain
    return inv_scale * (scaled - normed * jnp.mean(scaled * normed, axis=axis, keepdims=True))


def rotate(values, cos_t, sin_t, sign):
    half = HEAD_SIZE // 2
    first, second = values[:, :half], values[:, half:]
    sin_t = sin_t * sign
    return jnp.concatenate([first * cos_t - second * sin_t, second * cos_t + first * sin_t], axis=1)


def per_device(
    layer_input,
    w_qkv,
    w_out,
    w_in,
    w_down,
    attn_gain,
    ffn_gain,
    q_gain,
    k_gain,
    cotangent,
    prefix_len,
    seq_slot,
):
    xf = layer_input[0].astype(F32)
    tokens, width = xf.shape
    g = lax.axis_index("grp")
    sources = slot_sources()
    positions = g * tokens + jnp.arange(tokens, dtype=jnp.int32)
    slot_ids = jnp.arange(prefix_len.shape[0], dtype=jnp.int32)
    prefix = jnp.sum(jnp.where(slot_ids == seq_slot[0], prefix_len, 0))
    info = jnp.stack([prefix, g * tokens] + [s * tokens for s in sources]).astype(jnp.int32)
    half = HEAD_SIZE // 2
    freqs = ROPE_THETA ** (-(2.0 * jnp.arange(half, dtype=F32)) / HEAD_SIZE)
    angles = freqs[:, None] * positions.astype(F32)[None, :]
    cos_t, sin_t = jnp.cos(angles), jnp.sin(angles)
    w_gate, w_up = w_in[:, 0], w_in[:, 1]

    inv_one = inverse_rms(xf, 1)
    normed_one = xf * inv_one
    xn = (normed_one * attn_gain).astype(BF)

    w_kv, w_q = w_qkv[:, QUERY_WIDTH:], w_qkv[:, :QUERY_WIDTH]
    kv_shards = fetch_shards(w_kv, 0)
    q_shards = fetch_shards(w_q, 0)
    out_shards = fetch_shards(w_out, 1)
    rows = w_qkv.shape[0]

    def project(own, shards):
        total = 0.0
        for source, shard in [(g, own)] + shards:
            total = total + dot(
                shard, lax.dynamic_slice_in_dim(xn, source * rows, rows, 1), 0, 1
            )
        return total

    kv_t = project(w_kv, kv_shards)
    k_raw = kv_t[:KEY_VALUE_WIDTH].reshape(KEY_VALUE_HEADS, HEAD_SIZE, tokens)
    k_inv = inverse_rms(k_raw, 1)
    k_normed = k_raw * k_inv
    k_low = rotate(k_normed * k_gain[:, None], cos_t, sin_t, 1.0).astype(BF)
    local_kv = jnp.concatenate(
        [k_low.reshape(KEY_VALUE_WIDTH, tokens), kv_t[KEY_VALUE_WIDTH:].astype(BF)], 0
    )
    kv = jnp.stack(spread(local_kv))
    q_t = project(w_q, q_shards)
    q_raw = q_t.reshape(QUERY_HEADS, HEAD_SIZE, tokens)
    q_inv = inverse_rms(q_raw, 1)
    q_normed = q_raw * q_inv
    q_low = rotate(q_normed * q_gain[:, None], cos_t, sin_t, 1.0).astype(BF)
    q_low = q_low.reshape(QUERY_WIDTH, tokens)

    ob, of, soft_inv = attention_forward(info, q_low, kv)
    w_out_full = assemble(w_out, out_shards)
    hid = xf + dot(ob, w_out_full, 0, 0)
    inv_two = inverse_rms(hid, 1)
    normed_two = hid * inv_two
    hn = (normed_two * ffn_gain).astype(BF)

    dy = cotangent[0]
    dy_slots = spread(dy)
    hn_slots = spread(hn)
    m_slots, dg_slots, du_slots, dhn_parts, out_parts = [], [], [], [], []
    for hn_s, dy_s in zip(hn_slots, dy_slots):
        gate = dot(hn_s, w_gate, 1, 1)
        up = dot(hn_s, w_up, 1, 1)
        dm = dot(dy_s, w_down, 1, 1)
        sg = jax.nn.sigmoid(gate)
        act = gate * sg
        m_s = (act * up).astype(BF)
        dg_s = (dm * up * sg * (1.0 + gate * (1.0 - sg))).astype(BF)
        du_s = (dm * act).astype(BF)
        m_slots.append(m_s)
        dg_slots.append(dg_s)
        du_slots.append(du_s)
        dhn_parts.append(dot(dg_s, w_gate, 1, 0) + dot(du_s, w_up, 1, 0))
    dhn = collect(dhn_parts)
    out_parts = [dot(m_s, w_down, 1, 0) for m_s in m_slots]
    layer_output = (hid + collect(out_parts)).astype(BF)

    order_a, order_b = rep_orders()
    hn_all = jnp.concatenate(hn_slots, 0)
    dy_all = jnp.concatenate(dy_slots, 0)

    def reduced(left_slots, right):
        left = jnp.concatenate(left_slots, 0)
        bit = bit_of(0)
        cols = right.shape[1] // 2
        away = dot(left, lax.dynamic_slice_in_dim(right, (1 - bit) * cols, cols, 1), 0, 0)
        keep = dot(left, lax.dynamic_slice_in_dim(right, bit * cols, cols, 1), 0, 0)
        both = keep + swap(away.astype(BF), 0).astype(F32)
        cut = both.shape[0] // 2
        top = rep_scatter(both[:cut], order_a[1:], 1).astype(BF)
        low = rep_scatter(both[cut:], order_b[1:], 1).astype(BF)
        return jnp.concatenate([rep_gather(top, order_a, 1), rep_gather(low, order_b, 1)], 0)

    d_w_down = reduced(m_slots, dy_all).astype(F32)
    d_w_gate = reduced(dg_slots, hn_all)
    d_w_up = reduced(du_slots, hn_all)
    d_w_in = jnp.stack([d_w_gate, d_w_up], 1).astype(F32)

    d_ffn_gain = jnp.sum(dhn * normed_two, axis=0)
    dhid = dy.astype(F32) + norm_back(dhn, normed_two, inv_two, ffn_gain, 1)
    dab = dhid.astype(BF)

    def reduced_all(x, axis):
        parts = []
        cut = x.shape[2 if axis == 1 else 1] // 2
        for i, order in enumerate((order_a, order_b)):
            piece = x[:, i * cut : (i + 1) * cut] if axis == 2 else x[:, :, i * cut : (i + 1) * cut]
            piece = rep_scatter(piece, order, axis)
            own = collect([lax.dynamic_index_in_dim(piece, s, 0, False) for s in sources])
            parts.append(rep_gather(own.astype(BF), order, axis - 1))
        return jnp.concatenate(parts, 2 - axis).astype(F32)

    members = lax.axis_size("grp")
    d_w_out = reduced_all(dot(ob, dab, 1, 0).reshape(members, w_out.shape[0], width), 2)
    dob = dot(w_out_full, dab, 1, 1).astype(BF)
    dq_rot, dk_part, dv_part = attention_backward(info, q_low, kv, dob, of, soft_inv)
    dq_n = rotate(dq_rot.reshape(QUERY_HEADS, HEAD_SIZE, tokens), cos_t, sin_t, -1.0)
    d_q_gain = jnp.sum(dq_n * q_normed, axis=(0, 2))
    dq = norm_back(dq_n, q_normed, q_inv, q_gain[:, None], 1).reshape(QUERY_WIDTH, tokens)
    dq = dq.astype(BF)
    d_w_q = reduced_all(dot(xn, dq, 0, 1).reshape(members, rows, QUERY_WIDTH), 1)
    dkv_part = jnp.concatenate([dk_part, dv_part], 1)
    dkv = collect([dkv_part[i] for i in range(members)])
    dk_n = rotate(
        dkv[:KEY_VALUE_WIDTH].reshape(KEY_VALUE_HEADS, HEAD_SIZE, tokens), cos_t, sin_t, -1.0
    )
    d_k_gain = jnp.sum(dk_n * k_normed, axis=(0, 2))
    dk = norm_back(dk_n, k_normed, k_inv, k_gain[:, None], 1).reshape(KEY_VALUE_WIDTH, tokens)
    dkv = jnp.concatenate([dk, dkv[KEY_VALUE_WIDTH:]], 0).astype(BF)
    d_w_kv = reduced_all(dot(xn, dkv, 0, 1).reshape(members, rows, 2 * KEY_VALUE_WIDTH), 1)
    d_w_qkv = jnp.concatenate([d_w_q, d_w_kv], 1)

    w_q_full = assemble(w_q, q_shards)
    w_kv_full = assemble(w_kv, kv_shards)
    dxn = dot(dq, w_q_full, 0, 1) + dot(dkv, w_kv_full, 0, 1)
    d_attn_gain = jnp.sum(dxn * normed_one, axis=0)
    input_grad = dhid + norm_back(dxn, normed_one, inv_one, attn_gain, 1)
    gains = sum_everywhere(jnp.concatenate([d_attn_gain, d_ffn_gain, d_q_gain, d_k_gain]))
    return (
        layer_output[None],
        input_grad[None],
        d_w_qkv,
        d_w_out,
        d_w_in,
        d_w_down,
        gains[:width],
        gains[width : 2 * width],
        gains[2 * width : 2 * width + HEAD_SIZE],
        gains[2 * width + HEAD_SIZE :],
    )


def solution(mesh):
    in_specs = (
        P("rep", "grp", None),
        P("grp", None),
        P("grp", None),
        P("grp", None, None),
        P("grp", None),
        P(),
        P(),
        P(),
        P(),
        P("rep", "grp", None),
        P(),
        P("rep"),
    )
    out_specs = (
        P("rep", "grp", None),
        P("rep", "grp", None),
        P("grp", None),
        P("grp", None),
        P("grp", None, None),
        P("grp", None),
        P(),
        P(),
        P(),
        P(),
    )
    return jax.shard_map(
        per_device, mesh=mesh, in_specs=in_specs, out_specs=out_specs, check_vma=False
    )
```

time: 1870 us -> 1020 us (0.55)
  waiting for transfers between devices: 1460 us -> 281 us
  starting transfers between devices: 1.26 us -> 254 us
  other arithmetic: 49.7 us -> 136 us
  matrix products: 211 us -> 132 us
  local copies, waits for them, and re-layouts: 92.3 us -> 166 us
  blocking collectives: 42.3 us -> 0 us
  Pallas kernels: 0 us -> 35.1 us
    reduce_scatter x5 -> x0, waiting for transfers between devices: 713 us -> none  [the longest x2 404 us: row_shares(): lax.psum_scatter(lax.dot_general(left_rows, gradient, (((0,), (0,)), ((),...]
    psum x1 -> x0, waiting for transfers between devices: 400 us -> none  [per_device(): lax.psum((d_w_qkv_part, d_w_out_part, d_w_in_part, d_w_down_part), 'rep')]
    all_gather x5 -> x0, waiting for transfers between devices: 341 us -> none  [the longest x2 188 us: fold_rows(): lax.all_gather(weight, 'grp', axis=0, tiled=True)]
    ppermute x0 -> x161, waiting for transfers between devices: none -> 281 us  [the longest x90 132 us: swap(): return lax.ppermute(x, 'rep', [(i, i ^ 1 << b) for i in range(n)])]
    ppermute x0 -> x161, starting transfers between devices: none -> 254 us  [the longest x45 139 us: send(): return lax.ppermute(x.astype(BF), 'grp', pairs).astype(F32)]
    dot_general x47 -> x45, matrix products: 211 us -> 132 us  [dot(): lax.dot_general(a, b, (((ca,), (cb,)), ((), ())), preferred_element_type=...]
    select_n x0 -> x58, other arithmetic: none -> 49.5 us  [the longest x54 47.8 us: rep_gather(): jnp.where(bit_of(b) == 0, jnp.concatenate([x, other], axis), jnp.concaten...]
    psum x1 -> x0, blocking collectives: 42.3 us -> none  [per_device(): lax.psum((d_attn_gain, d_ffn_gain, d_q_gain, d_k_gain), ('rep', 'grp'))]
  transfers between devices with their start and end apart: 11 -> 161, of which waited for: 11 -> 56; matrix products, arithmetic and copies ran while one was open for 9% -> 42% of each run, Pallas kernels for 0% -> 3%
where the time goes in v1:
time: 1020 us; the launch traced here: 1010 us
  waiting for transfers between devices  281 us (28%)
  starting transfers between devices  254 us (25%)
  local copies, waits for them, and re-layouts  166 us (16%)
  other arithmetic  136 us (13%)
  matrix products  132 us (13%)
  Pallas kernels  35.1 us (3%)
    ppermute x45, starting transfers between devices, send(): return lax.ppermute(x.astype(BF), 'grp', pairs).astype(F32)  139 us
    ppermute x90, waiting for transfers between devices, swap(): return lax.ppermute(x, 'rep', [(i, i ^ 1 << b) for i in range(n)])  132 us
    dot_general x45, matrix products, dot(): lax.dot_general(a, b, (((ca,), (cb,)), ((), ())), preferred_element_type=...  132 us
    ppermute x90, starting transfers between devices, swap(): return lax.ppermute(x, 'rep', [(i, i ^ 1 << b) for i in range(n)])  77.6 us
    ppermute x45, waiting for transfers between devices, send(): return lax.ppermute(x.astype(BF), 'grp', pairs).astype(F32)  55.2 us
    unnamed x313, local copies, waits for them, and re-layouts  53.8 us
    select_n x54, other arithmetic, rep_gather(): jnp.where(bit_of(b) == 0, jnp.concatenate([x, other], axis), jnp.concaten...  47.8 us
    ppermute x3, waiting for transfers between devices, spread(): p4 = lax.ppermute(p2, 'grp', OUTWARD)  40.3 us
  transfers between devices with their start and end apart: 161, of which 56 were waited for; matrix products, arithmetic and copies ran while one was open for 42% of the time, Pallas kernels for 3%

profile of v1, /device:TPU:0, one launch (start us, length us, event | category | flops | bytes accessed | tf_op | source)
XLA Modules:
  0.0 1009.5 jit_solution(4272360264890179199)
XLA Ops:
  22.3 21.4 %fusion.130 = (bf16[1280,1,2048]{2,1,0:T(2,128)(2,1)}, bf16[1280,1,2048]{2,1,0:T(2,128)(2,1)}) fusion(bf16[1280,2,2048]{2,1,0:T(2,128)(2,1)} %param.15), kind=kLoop, calls=%fused_computation.445 | loop fusion | bytes 20971520 | tf_op jit(solution)/shard_map/slice | solution.py:319
  52.1 16.9 %copy_bitcast_fusion = (bf16[1280,2048]{1,0:T(8,128)(2,1)}, bf16[1280,2048]{1,0:T(8,128)(2,1)}) fusion(bf16[1280,1,2048]{2,1,0:T(2,128)(2,1)} %get-tuple-element.91, bf16[1280,1,2048]{2,1,0:T(2,128)(2,1)} %get-tuple-element.90), kind=kLoop, calls=%fused_computation.4 | loop fusion | bytes 20971520 | tf_op jit(solution)/shard_map/squeeze | solution.py:319
  111.1 7.9 collective-permute-done.4
  140.4 23.9 %collective-permute-done.20 = bf16[640,256]{1,0:T(8,128)(2,1)S(1)} collective-permute-done((bf16[640,256]{1,0:T(8,128)(2,1)S(1)}, bf16[640,256]{1,0:T(8,128)(2,1)S(1)}, u32[]{:S(2)}, u32[]{:S(2)}) %collective-permute-start.20) | collective-permute-done | bytes 327712 | tf_op jit(solution)/shard_map/ppermute | solution.py:96
  196.6 9.4 collective-permute-done.22
  207.2 10.3 %attention_forward.1 = (bf16[1280,256]{1,0:T(8,128)(2,1)S(1)}, f32[1280,256]{1,0:T(8,128)S(1)}, f32[5,4,256]{2,1,0:T(4,128)S(1)}) custom-call(s32[6]{0:T(128)S(1)} %stack.111.info_ref, bf16[1280,256]{1,0:T(8,128)(2,1)S(1)} %bitcast.368, bf16[4,640,256]{2,1,0:T(8,128)(2,1)S(1)} %pad_maximum_fusion.7.k_ref.v_ref, ...), custom_call_target="tpu_custom_call" | custom-call | flops 5368709120 | bytes 2621440 | tf_op jit(solution)/shard_map/attention_forward/pallas_call | solution.py:228
  238.4 10.5 %collective-permute-done.36 = bf16[256,2048]{1,0:T(8,128)(2,1)S(1)} collective-permute-done((bf16[256,2048]{1,0:T(8,128)(2,1)S(1)}, bf16[256,2048]{1,0:T(8,128)(2,1)S(1)}, u32[]{:S(2)}, u32[]{:S(2)}) %collective-permute-start.36) | collective-permute-done | bytes 1048608 | tf_op jit(solution)/shard_map/ppermute | solution.py:93
  262.8 8.6 collective-permute-done.48
  273.3 16.4 %collective-permute-done.33 = bf16[256,2048]{1,0:T(8,128)(2,1)S(1)} collective-permute-done((bf16[256,2048]{1,0:T(8,128)(2,1)S(1)}, bf16[256,2048]{1,0:T(8,128)(2,1)S(1)}, u32[]{:S(2)}, u32[]{:S(2)}) %collective-permute-start.33) | collective-permute-done | bytes 1048608 | tf_op jit(solution)/shard_map/ppermute | solution.py:96
  314.4 10.1 %collective-permute-done.38 = bf16[256,2048]{1,0:T(8,128)(2,1)S(1)} collective-permute-done((bf16[256,2048]{1,0:T(8,128)(2,1)S(1)}, bf16[256,2048]{1,0:T(8,128)(2,1)S(1)}, u32[]{:S(2)}, u32[]{:S(2)}) %collective-permute-start.38) | collective-permute-done | bytes 1048608 | tf_op jit(solution)/shard_map/ppermute | solution.py:97
  366.4 11.3 %collective-permute-done.49 = bf16[256,2048]{1,0:T(8,128)(2,1)S(1)} collective-permute-done((bf16[256,2048]{1,0:T(8,128)(2,1)}, bf16[256,2048]{1,0:T(8,128)(2,1)S(1)}, u32[]{:S(2)}, u32[]{:S(2)}) %collective-permute-start.49) | collective-permute-done | bytes 1048608 | tf_op jit(solution)/shard_map/ppermute | solution.py:109
  378.8 16.1 %collective-permute-done.39 = bf16[256,2048]{1,0:T(8,128)(2,1)S(1)} collective-permute-done((bf16[256,2048]{1,0:T(8,128)(2,1)}, bf16[256,2048]{1,0:T(8,128)(2,1)S(1)}, u32[]{:S(2)}, u32[]{:S(2)}) %collective-permute-start.39) | collective-permute-done | bytes 1048608 | tf_op jit(solution)/shard_map/ppermute | solution.py:109
  404.9 22.8 %collective-permute-start.51 = (bf16[256,2048]{1,0:T(8,128)(2,1)}, bf16[256,2048]{1,0:T(8,128)(2,1)S(1)}, u32[]{:S(2)}, u32[]{:S(2)}) collective-permute-start(bf16[256,2048]{1,0:T(8,128)(2,1)} %add_convert_fusion), channel_id=1, source_target_pairs={{0,1},{1,0},{2,3},{3,2},{4,5},{5,4},{6,7},{7,6},{8,9},{9,8},{10,11... | collective-permute-start | bytes 3145736 | tf_op jit(solution)/shard_map/ppermute | solution.py:109
  460.1 14.2 %collective-permute-done.41 = bf16[256,2048]{1,0:T(8,128)(2,1)S(1)} collective-permute-done((bf16[256,2048]{1,0:T(8,128)(2,1)}, bf16[256,2048]{1,0:T(8,128)(2,1)S(1)}, u32[]{:S(2)}, u32[]{:S(2)}) %collective-permute-start.41) | collective-permute-done | bytes 1048608 | tf_op jit(solution)/shard_map/ppermute | solution.py:109
  488.0 24.9 %attention_backward.1 = (f32[1280,256]{1,0:T(8,128)S(1)}, f32[4,320,256]{2,1,0:T(8,128)S(1)}, f32[4,320,256]{2,1,0:T(8,128)S(1)}) custom-call(s32[6]{0:T(128)S(1)} %copy-done.6, bf16[1280,256]{1,0:T(8,128)(2,1)S(1)} %bitcast.369, bf16[4,640,256]{2,1,0:T(8,128)(2,1)} %copy-done.2, bf16[4,640,256]{2,1,0:T(8,128)(2,1)} %copy-done.2, ...), custom_call_target="tpu_custom_call" | custom-call | flops 13421772800 | bytes 5242880 | tf_op jit(solution)/shard_map/attention_backward/pallas_call | solution.py:254
  537.6 8.9 fusion.129
  678.6 10.3 %collective-permute-done.132 = bf16[640,512]{0,1:T(8,128)(2,1)S(1)} collective-permute-done((bf16[640,512]{0,1:T(8,128)(2,1)S(1)}, bf16[640,512]{0,1:T(8,128)(2,1)S(1)}, u32[]{:S(2)}, u32[]{:S(2)}) %collective-permute-start.132) | collective-permute-done | bytes 655392 | tf_op jit(solution)/shard_map/ppermute | solution.py:39
  709.7 16.5 %collective-permute-done.113 = bf16[4,160,512]{2,1,0:T(8,128)(2,1)S(1)} collective-permute-done((bf16[4,160,512]{2,1,0:T(8,128)(2,1)S(1)}, bf16[4,160,512]{2,1,0:T(8,128)(2,1)S(1)}, u32[]{:S(2)}, u32[]{:S(2)}) %collective-permute-start.113) | collective-permute-done | bytes 655392 | tf_op jit(solution)/shard_map/ppermute | solution.py:39
  743.6 9.9 collective-permute-done.81
  777.0 11.8 %collective-permute-start.86 = (bf16[64,320]{1,0:T(8,128)(2,1)S(1)}, bf16[64,320]{1,0:T(8,128)(2,1)S(1)}, u32[]{:S(2)}, u32[]{:S(2)}) collective-permute-start(bf16[64,320]{1,0:T(8,128)(2,1)S(1)} %fusion.90), channel_id=1, source_target_pairs={{0,1},{1,0},{2,3},{3,2},{4,5},{5,4},{6,7},{7,6},{8,9},{9,8},{10,11... | collective-permute-start | bytes 122888 | tf_op jit(solution)/shard_map/ppermute | solution.py:109
  850.1 23.9 %collective-permute-start.64 = (bf16[64,640]{1,0:T(8,128)(2,1)S(1)}, bf16[64,640]{1,0:T(8,128)(2,1)S(1)}, u32[]{:S(2)}, u32[]{:S(2)}) collective-permute-start(bf16[64,640]{1,0:T(8,128)(2,1)S(1)} %fusion.80), channel_id=1, source_target_pairs={{0,1},{1,0},{2,3},{3,2},{4,5},{5,4},{6,7},{7,6},{8,9},{9,8},{10,11... | collective-permute-start | bytes 245768 | tf_op jit(solution)/shard_map/ppermute | solution.py:109
  930.5 12.4 %maximum_convert_fusion = f32[1280,2,2048]{0,2,1:T(8,128)} fusion(bf16[1280,1,2048]{0,2,1:T(8,128)(2,1)} %maximum_bitcast_fusion.1, bf16[1280,1,2048]{0,2,1:T(8,128)(2,1)} %maximum_bitcast_fusion), kind=kLoop, calls=%fused_computation | loop fusion | flops 10485760 | bytes 31457280 | tf_op jit(solution)/shard_map/convert_element_type | solution.py:402
  950.8 31.3 %copy.192 = f32[1280,2,2048]{2,1,0:T(2,128)} copy(f32[1280,2,2048]{0,2,1:T(8,128)} %maximum_convert_fusion) | data formatting | bytes 41943040
  982.1 11.2 %copy.193 = f32[1280,2048]{1,0:T(8,128)} copy(f32[1280,2048]{0,1:T(8,128)} %maximum_convert_fusion.1) | data formatting | bytes 20971520
  (945 shorter events, 643.3 us)
Async XLA Ops:
  2.5 72.8 %collective-permute-start.2 = (bf16[2,32,1280]{2,1,0:T(8,128)(2,1)S(1)}, bf16[2,32,1280]{2,1,0:T(8,128)(2,1)}, u32[]{:S(2)}, u32[]{:S(2)}) collective-permute-start(bf16[2,32,1280]{2,1,0:T(8,128)(2,1)S(1)} %pad_maximum_fusion.25), channel_id=1, source_target_pairs={{0,3},{1,0},{2,1},{3,2},{4,7},{5,4},{6,5},{7,6},{8,11},{9,8},{10,9... | collective-permute-start | bytes 491528 | tf_op jit(solution)/shard_map/ppermute | solution.py:137
  7.6 68.0 %collective-permute-start.1 = (bf16[2,32,1280]{2,1,0:T(8,128)(2,1)S(1)}, bf16[2,32,1280]{2,1,0:T(8,128)(2,1)}, u32[]{:S(2)}, u32[]{:S(2)}) collective-permute-start(bf16[2,32,1280]{2,1,0:T(8,128)(2,1)S(1)} %pad_maximum_fusion.25), channel_id=1, source_target_pairs={{0,2},{1,3},{2,0},{3,1},{4,6},{5,7},{6,4},{7,5},{8,10},{9,11},{10,... | collective-permute-start | bytes 491528 | tf_op jit(solution)/shard_map/ppermute | solution.py:137
  10.3 59.4 %collective-permute-start.11 = (bf16[2,32,640]{2,1,0:T(8,128)(2,1)S(1)}, bf16[2,32,640]{2,1,0:T(8,128)(2,1)S(1)}, u32[]{:S(2)}, u32[]{:S(2)}) collective-permute-start(bf16[2,32,640]{2,1,0:T(8,128)(2,1)S(1)} %pad_maximum_fusion.28), channel_id=1, source_target_pairs={{0,3},{1,0},{2,1},{3,2},{4,7},{5,4},{6,5},{7,6},{8,11},{9,8},{10,9... | collective-permute-start | bytes 245768 | tf_op jit(solution)/shard_map/ppermute | solution.py:137
  10.9 58.9 %collective-permute-start.10 = (bf16[2,32,640]{2,1,0:T(8,128)(2,1)S(1)}, bf16[2,32,640]{2,1,0:T(8,128)(2,1)S(1)}, u32[]{:S(2)}, u32[]{:S(2)}) collective-permute-start(bf16[2,32,640]{2,1,0:T(8,128)(2,1)S(1)} %pad_maximum_fusion.28), channel_id=1, source_target_pairs={{0,2},{1,3},{2,0},{3,1},{4,6},{5,7},{6,4},{7,5},{8,10},{9,11},{10,... | collective-permute-start | bytes 245768 | tf_op jit(solution)/shard_map/ppermute | solution.py:137
  13.3 60.3 %collective-permute-start.9 = (bf16[2,32,640]{2,1,0:T(8,128)(2,1)S(1)}, bf16[2,32,640]{2,1,0:T(8,128)(2,1)S(1)}, u32[]{:S(2)}, u32[]{:S(2)}) collective-permute-start(bf16[2,32,640]{2,1,0:T(8,128)(2,1)S(1)} %pad_maximum_fusion.28), channel_id=1, source_target_pairs={{0,1},{1,2},{2,3},{3,0},{4,5},{5,6},{6,7},{7,4},{8,9},{9,10},{10,1... | collective-permute-start | bytes 245768 | tf_op jit(solution)/shard_map/ppermute | solution.py:137
  167.8 67.8 %collective-permute-start.47 = (bf16[256,2048]{1,0:T(8,128)(2,1)}, bf16[256,2048]{1,0:T(8,128)(2,1)}, u32[]{:S(2)}, u32[]{:S(2)}) collective-permute-start(bf16[256,2048]{1,0:T(8,128)(2,1)} %collective-permute-done.46), channel_id=1, source_target_pairs={{1,2},{2,1},{5,6},{6,5},{9,10},{10,9},{13,14},{14,13},{17,18},{18,... | collective-permute-start | bytes 3145736 | tf_op jit(solution)/shard_map/ppermute | solution.py:95
  169.5 67.6 %collective-permute-start.43 = (bf16[256,2048]{1,0:T(8,128)(2,1)}, bf16[256,2048]{1,0:T(8,128)(2,1)}, u32[]{:S(2)}, u32[]{:S(2)}) collective-permute-start(bf16[256,2048]{1,0:T(8,128)(2,1)} %collective-permute-done.42), channel_id=1, source_target_pairs={{1,0},{2,3},{5,4},{6,7},{9,8},{10,11},{13,12},{14,15},{17,16},{18,... | collective-permute-start | bytes 3145736 | tf_op jit(solution)/shard_map/ppermute | solution.py:96
  342.0 111.8 %collective-permute-start.45 = (bf16[256,2048]{1,0:T(8,128)(2,1)S(1)}, bf16[256,2048]{1,0:T(8,128)(2,1)S(1)}, u32[]{:S(2)}, u32[]{:S(2)}) collective-permute-start(bf16[256,2048]{1,0:T(8,128)(2,1)S(1)} %add_convert_fusion.2), channel_id=1, source_target_pairs={{1,2},{2,1},{5,6},{6,5},{9,10},{10,9},{13,14},{14,13},{17,18},{18,... | collective-permute-start | bytes 3145736 | tf_op jit(solution)/shard_map/ppermute | solution.py:109
  363.4 70.7 %collective-permute-start.123 = (bf16[1280,1024]{0,1:T(8,128)(2,1)}, bf16[1280,1024]{0,1:T(8,128)(2,1)}, u32[]{:S(2)}, u32[]{:S(2)}) collective-permute-start(bf16[1280,1024]{0,1:T(8,128)(2,1)} %convolution_convert_fusion.2), channel_id=1, source_target_pairs={{0,4},{4,0},{8,12},{12,8},{16,20},{20,16},{24,28},{28,24},{1,5},{5... | collective-permute-start | bytes 7864328 | tf_op jit(solution)/shard_map/ppermute | solution.py:39
  401.2 57.4 %collective-permute-start.35 = (bf16[256,2048]{1,0:T(8,128)(2,1)}, bf16[256,2048]{1,0:T(8,128)(2,1)S(1)}, u32[]{:S(2)}, u32[]{:S(2)}) collective-permute-start(bf16[256,2048]{1,0:T(8,128)(2,1)} %add_convert_fusion.6), channel_id=1, source_target_pairs={{1,2},{2,1},{5,6},{6,5},{9,10},{10,9},{13,14},{14,13},{17,18},{18,... | collective-permute-start | bytes 3145736 | tf_op jit(solution)/shard_map/ppermute | solution.py:109
  441.6 122.4 %collective-permute-start.140 = (bf16[640,512]{0,1:T(8,128)(2,1)}, bf16[640,512]{0,1:T(8,128)(2,1)}, u32[]{:S(2)}, u32[]{:S(2)}) collective-permute-start(bf16[640,512]{0,1:T(8,128)(2,1)} %dynamic-slice_convert_fusion.6), channel_id=1, source_target_pairs={{0,16},{4,20},{8,24},{12,28},{16,0},{20,4},{24,8},{28,12},{1,17},{... | collective-permute-start | bytes 1966088 | tf_op jit(solution)/shard_map/ppermute | solution.py:39
  453.8 118.1 %collective-permute-start.135 = (bf16[640,512]{0,1:T(8,128)(2,1)}, bf16[640,512]{0,1:T(8,128)(2,1)S(1)}, u32[]{:S(2)}, u32[]{:S(2)}) collective-permute-start(bf16[640,512]{0,1:T(8,128)(2,1)} %dynamic-slice_convert_fusion.7), channel_id=1, source_target_pairs={{0,8},{4,12},{8,0},{12,4},{16,24},{20,28},{24,16},{28,20},{1,9},{5... | collective-permute-start | bytes 1966088 | tf_op jit(solution)/shard_map/ppermute | solution.py:39
  455.3 111.5 %collective-permute-start.129 = (bf16[640,512]{0,1:T(8,128)(2,1)}, bf16[640,512]{0,1:T(8,128)(2,1)}, u32[]{:S(2)}, u32[]{:S(2)}) collective-permute-start(bf16[640,512]{0,1:T(8,128)(2,1)} %dynamic-slice_convert_fusion.8), channel_id=1, source_target_pairs={{0,16},{4,20},{8,24},{12,28},{16,0},{20,4},{24,8},{28,12},{1,17},{... | collective-permute-start | bytes 1966088 | tf_op jit(solution)/shard_map/ppermute | solution.py:39
  458.5 115.0 %collective-permute-start.124 = (bf16[640,512]{0,1:T(8,128)(2,1)}, bf16[640,512]{0,1:T(8,128)(2,1)}, u32[]{:S(2)}, u32[]{:S(2)}) collective-permute-start(bf16[640,512]{0,1:T(8,128)(2,1)} %dynamic-slice_convert_fusion.9), channel_id=1, source_target_pairs={{0,8},{4,12},{8,0},{12,4},{16,24},{20,28},{24,16},{28,20},{1,9},{5... | collective-permute-start | bytes 1966088 | tf_op jit(solution)/shard_map/ppermute | solution.py:39
  474.3 100.9 %collective-permute-start.151 = (bf16[640,512]{0,1:T(8,128)(2,1)}, bf16[640,512]{0,1:T(8,128)(2,1)}, u32[]{:S(2)}, u32[]{:S(2)}) collective-permute-start(bf16[640,512]{0,1:T(8,128)(2,1)} %dynamic-slice_convert_fusion.4), channel_id=1, source_target_pairs={{0,16},{4,20},{8,24},{12,28},{16,0},{20,4},{24,8},{28,12},{1,17},{... | collective-permute-start | bytes 1966088 | tf_op jit(solution)/shard_map/ppermute | solution.py:39
  573.5 85.7 %collective-permute-start.57 = (bf16[4,256,640]{2,1,0:T(8,128)(2,1)}, bf16[4,256,640]{2,1,0:T(8,128)(2,1)}, u32[]{:S(2)}, u32[]{:S(2)}) collective-permute-start(bf16[4,256,640]{2,1,0:T(8,128)(2,1)} %dynamic-slice_convert_fusion.3), channel_id=1, source_target_pairs={{0,4},{4,0},{8,12},{12,8},{16,20},{20,16},{24,28},{28,24},{1,5},{5... | collective-permute-start | bytes 3932168 | tf_op jit(solution)/shard_map/ppermute | solution.py:39
  709.3 203.1 %collective-permute-start.144 = (bf16[640,1024]{0,1:T(8,128)(2,1)S(1)}, bf16[640,1024]{0,1:T(8,128)(2,1)}, u32[]{:S(2)}, u32[]{:S(2)}) collective-permute-start(bf16[640,1024]{0,1:T(8,128)(2,1)S(1)} %maximum_select_fusion.13), channel_id=1, source_target_pairs={{0,4},{4,0},{8,12},{12,8},{16,20},{20,16},{24,28},{28,24},{1,5},{5... | collective-permute-start | bytes 3932168 | tf_op jit(solution)/shard_map/ppermute | solution.py:39
  726.2 189.2 %collective-permute-start.139 = (bf16[640,1024]{0,1:T(8,128)(2,1)}, bf16[640,1024]{0,1:T(8,128)(2,1)}, u32[]{:S(2)}, u32[]{:S(2)}) collective-permute-start(bf16[640,1024]{0,1:T(8,128)(2,1)} %maximum_select_fusion.12), channel_id=1, source_target_pairs={{0,4},{4,0},{8,12},{12,8},{16,20},{20,16},{24,28},{28,24},{1,5},{5... | collective-permute-start | bytes 3932168 | tf_op jit(solution)/shard_map/ppermute | solution.py:39
  733.3 62.5 %collective-permute-start.59 = (bf16[4,64,640]{2,1,0:T(8,128)(2,1)}, bf16[4,64,640]{2,1,0:T(8,128)(2,1)}, u32[]{:S(2)}, u32[]{:S(2)}) collective-permute-start(bf16[4,64,640]{2,1,0:T(8,128)(2,1)} %dynamic-slice_convert_fusion.29), channel_id=1, source_target_pairs={{0,16},{4,20},{8,24},{12,28},{16,0},{20,4},{24,8},{28,12},{1,17},{... | collective-permute-start | bytes 983048 | tf_op jit(solution)/shard_map/ppermute | solution.py:39
  792.9 126.7 %collective-permute-start.133 = (bf16[640,1024]{0,1:T(8,128)(2,1)}, bf16[640,1024]{0,1:T(8,128)(2,1)S(1)}, u32[]{:S(2)}, u32[]{:S(2)}) collective-permute-start(bf16[640,1024]{0,1:T(8,128)(2,1)} %maximum_select_fusion.11), channel_id=1, source_target_pairs={{0,4},{4,0},{8,12},{12,8},{16,20},{20,16},{24,28},{28,24},{1,5},{5... | collective-permute-start | bytes 3932168 | tf_op jit(solution)/shard_map/ppermute | solution.py:39
  915.4 77.9 %collective-permute-start.66 = (bf16[128,640]{1,0:T(8,128)(2,1)S(1)}, bf16[128,640]{1,0:T(8,128)(2,1)}, u32[]{:S(2)}, u32[]{:S(2)}) collective-permute-start(bf16[128,640]{1,0:T(8,128)(2,1)S(1)} %maximum_select_fusion.48), channel_id=1, source_target_pairs={{0,8},{4,12},{8,0},{12,4},{16,24},{20,28},{24,16},{28,20},{1,9},{5... | collective-permute-start | bytes 491528 | tf_op jit(solution)/shard_map/ppermute | solution.py:39
  919.7 74.8 %collective-permute-start.77 = (bf16[128,640]{1,0:T(8,128)(2,1)S(1)}, bf16[128,640]{1,0:T(8,128)(2,1)}, u32[]{:S(2)}, u32[]{:S(2)}) collective-permute-start(bf16[128,640]{1,0:T(8,128)(2,1)S(1)} %maximum_select_fusion.49), channel_id=1, source_target_pairs={{0,16},{4,20},{8,24},{12,28},{16,0},{20,4},{24,8},{28,12},{1,17},{... | collective-permute-start | bytes 491528 | tf_op jit(solution)/shard_map/ppermute | solution.py:39
  921.6 74.5 %collective-permute-start.121 = (bf16[160,512]{1,0:T(8,128)(2,1)S(1)}, bf16[160,512]{1,0:T(8,128)(2,1)S(1)}, u32[]{:S(2)}, u32[]{:S(2)}) collective-permute-start(bf16[160,512]{1,0:T(8,128)(2,1)S(1)} %maximum_select_fusion.51), channel_id=1, source_target_pairs={{0,16},{4,20},{8,24},{12,28},{16,0},{20,4},{24,8},{28,12},{1,17},{... | collective-permute-start | bytes 491528 | tf_op jit(solution)/shard_map/ppermute | solution.py:39
  928.7 68.3 %collective-permute-start.110 = (bf16[160,512]{1,0:T(8,128)(2,1)S(1)}, bf16[160,512]{1,0:T(8,128)(2,1)}, u32[]{:S(2)}, u32[]{:S(2)}) collective-permute-start(bf16[160,512]{1,0:T(8,128)(2,1)S(1)} %maximum_select_fusion.50), channel_id=1, source_target_pairs={{0,8},{4,12},{8,0},{12,4},{16,24},{20,28},{24,16},{28,20},{1,9},{5... | collective-permute-start | bytes 491528 | tf_op jit(solution)/shard_map/ppermute | solution.py:39
  (292 other events, 3914.6 us)

commit v2 on v1

v2 whole, which is shorter than its diff:
```python
import functools

import jax
import jax.numpy as jnp
from jax import lax
from jax.experimental import pallas as pl
from jax.experimental.pallas import tpu as pltpu
from jax.sharding import PartitionSpec as P

QUERY_HEADS = 20
KEY_VALUE_HEADS = 5
HEAD_SIZE = 64
GROUP = QUERY_HEADS // KEY_VALUE_HEADS
QUERY_WIDTH = QUERY_HEADS * HEAD_SIZE
KEY_VALUE_WIDTH = KEY_VALUE_HEADS * HEAD_SIZE
NORM_EPSILON = 1e-06
ROPE_THETA = 10000.0
LOG2E = 1.4426950408889634
BF = jnp.bfloat16
F32 = jnp.float32


def dot(a, b, ca, cb):
    return lax.dot_general(a, b, (((ca,), (cb,)), ((), ())), preferred_element_type=F32)


def rep_orders():
    bits = lax.axis_size("rep").bit_length() - 1
    rest = list(range(1, bits))
    return [0] + rest, [0] + rest[::-1]


def bit_of(b):
    return (lax.axis_index("rep") >> b) & 1


def swap(x, b):
    n = lax.axis_size("rep")
    return lax.ppermute(x, "rep", [(i, i ^ (1 << b)) for i in range(n)])


def place_of(order):
    place = 0
    for b in order:
        place = place * 2 + bit_of(b)
    return place


def send_half(x, b, axis):
    half = x.shape[axis] // 2
    away = lax.dynamic_slice_in_dim(x, (1 - bit_of(b)) * half, half, axis)
    return swap(away.astype(BF), b)


def add_half(x, recv, b, axis):
    half = x.shape[axis] // 2
    keep = lax.dynamic_slice_in_dim(x, bit_of(b) * half, half, axis)
    return keep.astype(F32) + recv.astype(F32)


def rest_count():
    return lax.axis_size("rep") // 2


def swap_rest(x, j):
    n = lax.axis_size("rep")
    return lax.ppermute(x, "rep", [(i, i ^ (2 * j)) for i in range(n)])


def rest_swaps(x):
    return [x] + [swap_rest(x, j) for j in range(1, rest_count())]


def join_pair(mine, other, b, axis):
    return jnp.where(
        bit_of(b) == 0,
        jnp.concatenate([mine, other], axis),
        jnp.concatenate([other, mine], axis),
    )


def rest_place():
    return lax.axis_index("rep") >> 1


def rest_join(got, axis):
    held = dict(enumerate(got))
    for b in range(rest_count().bit_length() - 1):
        step = 1 << b
        held = {
            i: join_pair(held[i], held[i | step], b + 1, axis) for i in held if not i & step
        }
        held = lax.optimization_barrier(held)
    return held[0]


EDGE = [(0, 1), (1, 0), (2, 3), (3, 2)]
MID = [(1, 2), (2, 1)]
OUTWARD = [(1, 0), (2, 3)]
INWARD = [(0, 1), (3, 2)]


def move(x, pairs):
    return lax.ppermute(x, "grp", pairs)


def ring(n):
    return [(i, (i + 1) % n) for i in range(n)]


class Spread:
    def __init__(self, x):
        self.n = lax.axis_size("grp")
        self.held = [x]

    def hop(self, k):
        held = self.held
        if self.n != 4:
            if k == 1:
                for _ in range(self.n - 1):
                    held.append(move(held[-1], ring(self.n)))
        elif k == 1:
            held += [move(held[0], EDGE), move(held[0], MID)]
        elif k == 2:
            held += [move(held[1], MID), move(held[2], OUTWARD)]
        else:
            held += [move(held[3], OUTWARD)]

    def slot(self, k):
        held = self.held
        if self.n != 4 or k < 2:
            return held[k]
        g = lax.axis_index("grp")
        middle = (g == 1) | (g == 2)
        return jnp.where(middle, held[k], held[k + 2])


class Collect:
    def __init__(self, parts):
        self.n = lax.axis_size("grp")
        self.parts = list(parts)
        self.held = {}

    def send(self, x, pairs):
        return move(x.astype(BF), pairs)

    def plus(self, k, name):
        return self.parts[k].astype(F32) + self.held[name].astype(F32)

    def hop(self, name):
        if self.n != 4:
            return
        parts, held = self.parts, self.held
        if name == "far":
            held["far"] = self.send(parts[3], INWARD)
        elif name == "next":
            held["next"] = self.send(parts[2], INWARD)
        elif name == "far_mid":
            held["far_mid"] = self.send(self.plus(3, "far"), MID)
        elif name == "next_mid":
            held["next_mid"] = self.send(self.plus(2, "next"), MID)
        else:
            held["edge"] = self.send(self.plus(1, "far_mid"), EDGE)

    def result(self):
        parts, held = self.parts, self.held
        if self.n == 4:
            return self.plus(0, "edge") + held["next_mid"].astype(F32)
        total = parts[1].astype(F32)
        for k in list(range(2, self.n)) + [0]:
            total = self.send(total, ring(self.n)).astype(F32) + parts[k].astype(F32)
        return total


def shift(x, k):
    n = lax.axis_size("grp")
    return move(x, [(i, (i + k) % n) for i in range(n)])


def from_shift(k):
    n = lax.axis_size("grp")
    return lax.rem(lax.axis_index("grp") + n - k, n)


class Direct:
    def __init__(self, send):
        n = lax.axis_size("grp")
        self.held = [send[0].astype(F32)] + [shift(send[k].astype(BF), n - k) for k in range(1, n)]

    def result(self):
        total = self.held[0]
        for x in self.held[1:]:
            total = total + x.astype(F32)
        return total


class Shards:
    def __init__(self, w):
        self.w = w
        self.held = None

    def fetch(self):
        n = lax.axis_size("grp")
        size = self.w.shape[0] // lax.axis_size("rep")
        place = bit_of(0) * rest_count() + rest_place()
        mine = lax.dynamic_slice_in_dim(self.w, place * size, size, 0)
        self.held = [shift(mine, k) for k in range(1, n)]

    def rest(self):
        self.held = rest_swaps(jnp.stack(self.held))

    def core(self):
        mine = rest_join(self.held, 1)
        self.held = [mine, swap(mine, 0)]

    def whole(self):
        return join_pair(*self.held, 0, 1)

    def shards(self):
        n = lax.axis_size("grp")
        g = lax.axis_index("grp")
        whole = self.whole()
        return [(g, self.w)] + [(from_shift(k), whole[k - 1]) for k in range(1, n)]


def tie(*values):
    return lax.optimization_barrier(values)


def hold(*movers):
    held = lax.optimization_barrier([m.held for m in movers])
    for m, h in zip(movers, held):
        m.held = h


def hold_with(values, *movers):
    values, held = lax.optimization_barrier((values, [m.held for m in movers]))
    for m, h in zip(movers, held):
        m.held = h
    return values


class Reduced:
    def __init__(self, product, axis):
        self.axis = axis
        core = bit_of(0)
        self.held = [product(1 - core).astype(BF), product(core)]

    def core(self):
        away, keep = self.held
        self.held = [keep, swap(away, 0)]

    def block(self, x, place):
        size = x.shape[self.axis] // rest_count()
        return lax.dynamic_slice_in_dim(x, place * size, size, self.axis)

    def rest(self):
        keep, recv = self.held
        x = keep + recv.astype(F32)
        place = rest_place()
        recv = [
            swap_rest(self.block(x, place ^ j).astype(BF), j) for j in range(1, rest_count())
        ]
        self.held = [x] + recv

    def members(self):
        x = self.block(self.held[0], rest_place())
        for recv in self.held[1:]:
            x = x + recv.astype(F32)
        n = lax.axis_size("grp")
        self.held = Direct(
            [lax.dynamic_index_in_dim(x, from_shift(k), 0, False) for k in range(n)]
        ).held

    def back(self):
        total = self.held[0]
        for x in self.held[1:]:
            total = total + x.astype(F32)
        self.held = rest_swaps(total.astype(BF))

    def last(self):
        mine = rest_join(self.held, self.axis - 1)
        self.held = [mine, swap(mine, 0)]

    def result(self):
        return join_pair(*self.held, 0, self.axis - 1).astype(F32)


class RepSum:
    def __init__(self, away, keep, axis):
        self.axis = axis
        self.held = [away, keep]

    def core(self):
        away, keep = self.held
        self.held = [keep, swap(away, 0)]

    def block(self, x, place):
        size = x.shape[self.axis] // rest_count()
        return lax.dynamic_slice_in_dim(x, place * size, size, self.axis)

    def rest(self):
        keep, recv = self.held
        x = keep + recv.astype(F32)
        place = rest_place()
        recv = [
            swap_rest(self.block(x, place ^ j).astype(BF), j) for j in range(1, rest_count())
        ]
        self.held = [x] + recv

    def back(self):
        x = self.block(self.held[0], rest_place())
        for recv in self.held[1:]:
            x = x + recv.astype(F32)
        self.held = rest_swaps(x.astype(BF))

    def last(self):
        mine = rest_join(self.held, self.axis)
        self.held = [mine, swap(mine, 0)]

    def result(self):
        return join_pair(*self.held, 0, self.axis).astype(F32)


def mask_limit(info_ref, tokens):
    query_pos = info_ref[1] + lax.broadcasted_iota(jnp.int32, (1, tokens), 1)
    return jnp.maximum(query_pos + 1, info_ref[0])


def forward_kernel(info_ref, q_ref, k_ref, v_ref, o_ref, of_ref, inv_ref):
    slots, _, tokens = k_ref.shape
    limit = mask_limit(info_ref, tokens)
    for h in range(GROUP):
        rows = slice(h * HEAD_SIZE, (h + 1) * HEAD_SIZE)
        q = q_ref[rows, :]
        total = jnp.zeros((1, tokens), F32)
        acc = jnp.zeros((HEAD_SIZE, tokens), F32)
        for s in range(slots):
            key_pos = info_ref[2 + s] + lax.broadcasted_iota(jnp.int32, (tokens, tokens), 0)
            t = dot(k_ref[s], q, 0, 0) * (HEAD_SIZE**-0.5 * LOG2E)
            e = jnp.where(key_pos < limit, jnp.exp2(t), 0.0)
            total = total + jnp.sum(e, axis=0, keepdims=True)
            acc = acc + dot(v_ref[s], e.astype(BF), 1, 0)
        inv = 1.0 / total
        out = acc * inv
        o_ref[rows, :] = out.astype(BF)
        of_ref[rows, :] = out
        inv_ref[0, h : h + 1, :] = inv


def backward_kernel(info_ref, q_ref, k_ref, v_ref, g_ref, of_ref, inv_ref, dq_ref, dk_ref, dv_ref):
    slots, _, tokens = k_ref.shape
    limit = mask_limit(info_ref, tokens)
    for h in range(GROUP):
        rows = slice(h * HEAD_SIZE, (h + 1) * HEAD_SIZE)
        q = q_ref[rows, :]
        grad = g_ref[rows, :]
        inv = inv_ref[0, h : h + 1, :]
        delta = jnp.sum(of_ref[rows, :] * grad.astype(F32), axis=0, keepdims=True)
        acc = jnp.zeros((HEAD_SIZE, tokens), F32)
        for s in range(slots):
            key_pos = info_ref[2 + s] + lax.broadcasted_iota(jnp.int32, (tokens, tokens), 0)
            t = dot(k_ref[s], q, 0, 0) * (HEAD_SIZE**-0.5 * LOG2E)
            p = jnp.where(key_pos < limit, jnp.exp2(t) * inv, 0.0)
            dp = dot(v_ref[s], grad, 0, 0)
            ds = (p * (dp - delta)).astype(BF)
            acc = acc + dot(k_ref[s], ds, 1, 0)
            dk = dot(q, ds, 1, 1) * HEAD_SIZE**-0.5
            dv = dot(grad, p.astype(BF), 1, 1)
            if h == 0:
                dk_ref[s] = dk
                dv_ref[s] = dv
            else:
                dk_ref[s] += dk
                dv_ref[s] += dv
        dq_ref[rows, :] = acc * HEAD_SIZE**-0.5


def attention_specs(slots, tokens):
    heads = pl.BlockSpec((GROUP * HEAD_SIZE, tokens), lambda c, info: (c, 0))
    keys = pl.BlockSpec((slots, HEAD_SIZE, tokens), lambda c, info: (0, c, 0))
    values = pl.BlockSpec((slots, HEAD_SIZE, tokens), lambda c, info: (0, KEY_VALUE_HEADS + c, 0))
    inverse = pl.BlockSpec((1, GROUP, tokens), lambda c, info: (c, 0, 0))
    return heads, keys, values, inverse


def attention_forward(info, q, kv):
    slots, _, tokens = kv.shape
    heads, keys, values, inverse = attention_specs(slots, tokens)
    return pl.pallas_call(
        forward_kernel,
        grid_spec=pltpu.PrefetchScalarGridSpec(
            num_scalar_prefetch=1,
            grid=(KEY_VALUE_HEADS,),
            in_specs=[heads, keys, values],
            out_specs=[heads, heads, inverse],
        ),
        out_shape=[
            jax.ShapeDtypeStruct((QUERY_WIDTH, tokens), BF),
            jax.ShapeDtypeStruct((QUERY_WIDTH, tokens), F32),
            jax.ShapeDtypeStruct((KEY_VALUE_HEADS, GROUP, tokens), F32),
        ],
        compiler_params=pltpu.CompilerParams(vmem_limit_bytes=48 * 2**20),
        cost_estimate=pl.CostEstimate(flops=0, bytes_accessed=2**20, transcendentals=0),
        name="attention_forward",
    )(info, q, kv, kv)


def attention_backward(info, q, kv, grad, of, inv):
    slots, _, tokens = kv.shape
    heads, keys, values, inverse = attention_specs(slots, tokens)
    return pl.pallas_call(
        backward_kernel,
        grid_spec=pltpu.PrefetchScalarGridSpec(
            num_scalar_prefetch=1,
            grid=(KEY_VALUE_HEADS,),
            in_specs=[heads, keys, values, heads, heads, inverse],
            out_specs=[heads, keys, keys],
        ),
        out_shape=[
            jax.ShapeDtypeStruct((QUERY_WIDTH, tokens), F32),
            jax.ShapeDtypeStruct((slots, KEY_VALUE_WIDTH, tokens), F32),
            jax.ShapeDtypeStruct((slots, KEY_VALUE_WIDTH, tokens), F32),
        ],
        compiler_params=pltpu.CompilerParams(vmem_limit_bytes=48 * 2**20),
        cost_estimate=pl.CostEstimate(flops=0, bytes_accessed=2**20, transcendentals=0),
        name="attention_backward",
    )(info, q, kv, kv, grad, of, inv)


VMEM = 56 * 2**20


def split_kernel(w_ref, gate_ref, up_ref, s_ref):
    rows = gate_ref.shape[0]
    step = w_ref.shape[0] // rows
    s_ref[...] = w_ref[...].astype(F32)
    for c in range(step // 2):
        lanes = slice(c * 128, (c + 1) * 128)
        gate_ref[:, lanes] = s_ref[pl.ds(2 * c, rows, stride=step), :].astype(BF)
        up_ref[:, lanes] = s_ref[pl.ds(2 * c + 1, rows, stride=step), :].astype(BF)


def split_gate_up(w_in):
    units, _, width = w_in.shape
    step = width // 64
    flat = w_in.reshape(units, 2, width // 128, 128).transpose(0, 2, 1, 3)
    flat = flat.reshape(units * step, 128)
    block = 128
    half = pl.BlockSpec((block, width), lambda i: (i, 0))
    return pl.pallas_call(
        split_kernel,
        grid=(units // block,),
        in_specs=[pl.BlockSpec((block * step, 128), lambda i: (i, 0))],
        out_specs=[half, half],
        out_shape=[jax.ShapeDtypeStruct((units, width), BF)] * 2,
        scratch_shapes=[pltpu.VMEM((block * step, 128), F32)],
        compiler_params=pltpu.CompilerParams(vmem_limit_bytes=VMEM),
        cost_estimate=pl.CostEstimate(flops=0, bytes_accessed=2**20, transcendentals=0),
        name="split_gate_up",
    )(flat)


FFN_CUTS = 5


def ffn_kernel(hn_ref, dy_ref, g_hbm, u_hbm, d_hbm, lhs_ref, dhn_ref, out_ref, wg, wu, wd, sems):
    block = wg.shape[0] // FFN_CUTS
    copies = []
    for i in range(FFN_CUTS):
        rows = pl.ds(i * block, block)
        pairs = ((g_hbm, wg), (u_hbm, wu), (d_hbm, wd))
        copies.append(
            [
                pltpu.make_async_copy(src.at[rows], dst.at[rows], sems.at[j, i])
                for j, (src, dst) in enumerate(pairs)
            ]
        )
        for copy in copies[-1]:
            copy.start()
    hn, dy = hn_ref[...], dy_ref[...]
    for i in range(FFN_CUTS):
        for copy in copies[i]:
            copy.wait()
        rows = pl.ds(i * block, block)
        gate = dot(wg[rows, :], hn, 1, 1)
        up = dot(wu[rows, :], hn, 1, 1)
        dm = dot(wd[rows, :], dy, 1, 1)
        sg = 1.0 / (1.0 + jnp.exp(-gate))
        act = gate * sg
        lhs_ref[0, rows, :] = (act * up).astype(BF)
        lhs_ref[1, rows, :] = (dm * up * sg * (1.0 + gate * (1.0 - sg))).astype(BF)
        lhs_ref[2, rows, :] = (dm * act).astype(BF)
    step = 512
    for n in range(wg.shape[1] // step):
        lanes = pl.ds(n * step, step)
        dhn = dot(lhs_ref[1], wg[:, lanes], 0, 0) + dot(lhs_ref[2], wu[:, lanes], 0, 0)
        dhn_ref[:, lanes] = dhn.astype(dhn_ref.dtype)
        out_ref[:, lanes] = dot(lhs_ref[0], wd[:, lanes], 0, 0).astype(out_ref.dtype)


def ffn_slot(hn, dy, w_gate, w_up, w_down, kind):
    tokens, width = hn.shape
    units = w_gate.shape[0]
    whole = pl.BlockSpec(memory_space=pltpu.VMEM)
    far = pl.BlockSpec(memory_space=pl.ANY)
    return pl.pallas_call(
        ffn_kernel,
        in_specs=[whole, whole, far, far, far],
        out_specs=[whole, whole, whole],
        out_shape=[
            jax.ShapeDtypeStruct((3, units, tokens), BF),
            jax.ShapeDtypeStruct((tokens, width), kind),
            jax.ShapeDtypeStruct((tokens, width), kind),
        ],
        scratch_shapes=[pltpu.VMEM((units, width), BF)] * 3
        + [pltpu.SemaphoreType.DMA((3, FFN_CUTS))],
        compiler_params=pltpu.CompilerParams(vmem_limit_bytes=VMEM),
        cost_estimate=pl.CostEstimate(flops=0, bytes_accessed=2**20, transcendentals=0),
        name="ffn_slot",
    )(hn, dy, w_gate, w_up, w_down)


def grad_kernel(slots, *refs):
    rows = jnp.concatenate([r[0] for r in refs[:slots]], 1)
    right = jnp.concatenate([r[...] for r in refs[slots : 2 * slots]], 0)
    half = right.shape[1] // 2
    out_ref = refs[-1]
    for i in range(2):
        lanes = slice(i * half, (i + 1) * half)
        out_ref[:, lanes] = dot(rows, right[:, lanes], 1, 0).astype(BF)


def weight_grads(c, many, left, right):
    slots = len(left)
    _, units, tokens = left[0].shape
    width = right[0].shape[1]
    cut = units // 2
    lefts = pl.BlockSpec((1, cut, tokens), lambda i, m: (c + i, m, 0))
    rights = pl.BlockSpec((tokens, width), lambda i, m: (0, 0))
    return pl.pallas_call(
        functools.partial(grad_kernel, slots),
        grid=(many, 2),
        in_specs=[lefts] * slots + [rights] * slots,
        out_specs=pl.BlockSpec((cut, width), lambda i, m: (2 * i + m, 0)),
        out_shape=jax.ShapeDtypeStruct((many * units, width), BF),
        compiler_params=pltpu.CompilerParams(vmem_limit_bytes=VMEM),
        cost_estimate=pl.CostEstimate(flops=0, bytes_accessed=2**20, transcendentals=0),
        name="weight_grads",
    )(*left, *right)


def interleave_kernel(gate_ref, up_ref, out_ref):
    out_ref[:, 0, :] = gate_ref[...].astype(F32)
    out_ref[:, 1, :] = up_ref[...].astype(F32)


def interleave(both):
    units, width = both.shape[0] // 2, both.shape[1]
    block = 128
    blocks = units // block
    return pl.pallas_call(
        interleave_kernel,
        grid=(blocks,),
        in_specs=[
            pl.BlockSpec((block, width), lambda i: (i, 0)),
            pl.BlockSpec((block, width), lambda i: (blocks + i, 0)),
        ],
        out_specs=pl.BlockSpec((block, 2, width), lambda i: (i, 0, 0)),
        out_shape=jax.ShapeDtypeStruct((units, 2, width), F32),
        compiler_params=pltpu.CompilerParams(vmem_limit_bytes=VMEM),
        cost_estimate=pl.CostEstimate(flops=0, bytes_accessed=2**20, transcendentals=0),
        name="interleave",
    )(both, both)


def qkv_grad_kernel(slots, info_ref, *refs):
    xn, dq, dkv = refs[:slots], refs[slots : 2 * slots], refs[2 * slots : 3 * slots]
    away_ref, keep_ref = refs[3 * slots :]
    left = jnp.concatenate([r[...] for r in xn], 0)
    split = dq[0].shape[0]
    i = pl.program_id(0)
    for lanes, grads in ((slice(0, split), dq), (slice(split, None), dkv)):
        product = dot(left, jnp.concatenate([r[...] for r in grads], 1), 0, 1)

        @pl.when(i == 0)
        def _():
            away_ref[:, lanes] = product.astype(BF)

        @pl.when(i == 1)
        def _():
            keep_ref[:, lanes] = product


def qkv_grad(core, xn, dq, dkv):
    slots = len(xn)
    tokens, rows = xn[0].shape
    columns = dq[0].shape[0] + dkv[0].shape[0]
    half = pl.BlockSpec((tokens, rows // 2), lambda i, info: (0, info[0] ^ (1 - i)))
    out = pl.BlockSpec((rows // 2, columns), lambda i, info: (0, 0))
    return pl.pallas_call(
        functools.partial(qkv_grad_kernel, slots),
        grid_spec=pltpu.PrefetchScalarGridSpec(
            num_scalar_prefetch=1,
            grid=(2,),
            in_specs=[half] * slots
            + [pl.BlockSpec(x.shape, lambda i, info: (0, 0)) for x in [*dq, *dkv]],
            out_specs=[out, out],
        ),
        out_shape=[
            jax.ShapeDtypeStruct((rows // 2, columns), BF),
            jax.ShapeDtypeStruct((rows // 2, columns), F32),
        ],
        compiler_params=pltpu.CompilerParams(vmem_limit_bytes=VMEM),
        cost_estimate=pl.CostEstimate(flops=0, bytes_accessed=2**20, transcendentals=0),
        name="qkv_grad",
    )(core.reshape(1).astype(jnp.int32), *xn, *dq, *dkv)


def features_kernel(info_ref, dq_ref, dkv_ref, q_ref, kv_ref, more_q_ref, more_kv_ref, out_ref):
    k = pl.program_id(0)

    @pl.when(k == 0)
    def _():
        out_ref[...] = dot(dq_ref[...], q_ref[...], 0, 1) + dot(dkv_ref[...], kv_ref[...], 0, 1)

    @pl.when(k > 0)
    def _():
        product = dot(dq_ref[...], more_q_ref[0], 0, 1)
        out_ref[...] = product + dot(dkv_ref[...], more_kv_ref[0], 0, 1)


def features_grad(sources, dq, dkv, q, kv, more_q, more_kv):
    rows = q.shape[0]
    tokens = dq.shape[1]
    members = len(sources)
    whole = [pl.BlockSpec(x.shape, lambda k, info: (0, 0)) for x in (dq, dkv, q, kv)]
    more = [
        pl.BlockSpec((1,) + x.shape[1:], lambda k, info: (jnp.maximum(k - 1, 0), 0, 0))
        for x in (more_q, more_kv)
    ]
    return pl.pallas_call(
        features_kernel,
        grid_spec=pltpu.PrefetchScalarGridSpec(
            num_scalar_prefetch=1,
            grid=(members,),
            in_specs=whole + more,
            out_specs=pl.BlockSpec((tokens, rows), lambda k, info: (0, info[k])),
        ),
        out_shape=jax.ShapeDtypeStruct((tokens, rows * members), F32),
        compiler_params=pltpu.CompilerParams(vmem_limit_bytes=VMEM),
        cost_estimate=pl.CostEstimate(flops=0, bytes_accessed=2**20, transcendentals=0),
        name="features_grad",
    )(jnp.stack(sources).astype(jnp.int32), dq, dkv, q, kv, more_q, more_kv)


def inverse_rms(values, axis):
    return lax.rsqrt(jnp.mean(values * values, axis=axis, keepdims=True) + NORM_EPSILON)


def norm_back(grad_out, normed, inv_scale, gain, axis):
    scaled = grad_out * gain
    return inv_scale * (scaled - normed * jnp.mean(scaled * normed, axis=axis, keepdims=True))


def rotate(values, cos_t, sin_t, sign):
    half = HEAD_SIZE // 2
    first, second = values[:, :half], values[:, half:]
    sin_t = sin_t * sign
    return jnp.concatenate([first * cos_t - second * sin_t, second * cos_t + first * sin_t], axis=1)


def per_device(
    layer_input,
    w_qkv,
    w_out,
    w_in,
    w_down,
    attn_gain,
    ffn_gain,
    q_gain,
    k_gain,
    cotangent,
    prefix_len,
    seq_slot,
):
    xf = layer_input[0].astype(F32)
    tokens, width = xf.shape
    g = lax.axis_index("grp")
    core = bit_of(0)
    sources = [from_shift(k) for k in range(lax.axis_size("grp"))]
    positions = g * tokens + jnp.arange(tokens, dtype=jnp.int32)
    slot_ids = jnp.arange(prefix_len.shape[0], dtype=jnp.int32)
    prefix = jnp.sum(jnp.where(slot_ids == seq_slot[0], prefix_len, 0))
    info = jnp.stack([prefix, g * tokens] + [s * tokens for s in sources]).astype(jnp.int32)
    half = HEAD_SIZE // 2
    freqs = ROPE_THETA ** (-(2.0 * jnp.arange(half, dtype=F32)) / HEAD_SIZE)
    angles = freqs[:, None] * positions.astype(F32)[None, :]
    cos_t, sin_t = jnp.cos(angles), jnp.sin(angles)
    w_gate, w_up = split_gate_up(w_in)

    inv_one = inverse_rms(xf, 1)
    normed_one = xf * inv_one
    xn = (normed_one * attn_gain).astype(BF)
    dy = cotangent[0]
    rows = w_qkv.shape[0]
    members = lax.axis_size("grp")

    def project(shards):
        total = 0.0
        for source, shard in shards:
            total = total + dot(
                shard, lax.dynamic_slice_in_dim(xn, source * rows, rows, 1), 0, 1
            )
        return total

    kv_w = Shards(w_qkv[:, QUERY_WIDTH:])
    kv_w.fetch()
    xn, w_qkv, w_out, dy, w_in = hold_with((xn, w_qkv, w_out, dy, w_in), kv_w)
    q_w = Shards(w_qkv[:, :QUERY_WIDTH])
    q_w.fetch()
    kv_w.rest()
    w_out, dy, w_in = hold_with((w_out, dy, w_in), kv_w, q_w)
    kv_w.core()
    kv_t = project(kv_w.shards())
    k_raw = kv_t[:KEY_VALUE_WIDTH].reshape(KEY_VALUE_HEADS, HEAD_SIZE, tokens)
    k_inv = inverse_rms(k_raw, 1)
    k_normed = k_raw * k_inv
    k_low = rotate(k_normed * k_gain[:, None], cos_t, sin_t, 1.0).astype(BF)
    local_kv = jnp.concatenate(
        [k_low.reshape(KEY_VALUE_WIDTH, tokens), kv_t[KEY_VALUE_WIDTH:].astype(BF)], 0
    )
    local_kv, dy, w_in, w_out = hold_with((local_kv, dy, w_in, w_out), q_w)
    kv = [local_kv] + [shift(local_kv, k) for k in range(1, members)]
    q_w.rest()
    w_gate, w_up = split_gate_up(w_in)
    kv, w_gate, w_up, dy, w_out = hold_with((kv, w_gate, w_up, dy, w_out), q_w)
    out_w = Shards(w_out)
    out_w.fetch()
    q_w.core()
    q_t = project(q_w.shards())
    q_raw = q_t.reshape(QUERY_HEADS, HEAD_SIZE, tokens)
    q_inv = inverse_rms(q_raw, 1)
    q_normed = q_raw * q_inv
    q_low = rotate(q_normed * q_gain[:, None], cos_t, sin_t, 1.0).astype(BF)
    q_low = q_low.reshape(QUERY_WIDTH, tokens)
    kv, q_low, q_raw, dy = hold_with((kv, q_low, q_raw, dy), out_w)
    kv = jnp.stack(kv)

    dy_s = Spread(dy)
    dy_s.hop(1)
    out_w.rest()
    ob, of, soft_inv = attention_forward(info, q_low, kv)
    ob, of, soft_inv = hold_with((ob, of, soft_inv), out_w, dy_s)
    dy_s.hop(2)
    out_w.core()
    out_shards = out_w.shards()
    hid = xf
    for source, shard in out_shards:
        part = lax.dynamic_slice_in_dim(ob, source * w_out.shape[0], w_out.shape[0], 0)
        hid = hid + dot(part, shard, 0, 0)
    inv_two = inverse_rms(hid, 1)
    normed_two = hid * inv_two
    hn = (normed_two * ffn_gain).astype(BF)
    hn, hid = tie(hn, hid)

    def slot(k):
        kind = F32 if k == 0 else BF
        return ffn_slot(hn_s.slot(k), dy_s.slot(k), w_gate, w_up, w_down, kind)

    hn_s = Spread(hn)
    hn_s.hop(1)
    done = [slot(0)]
    done = hold_with(done, hn_s, dy_s)
    hn_s.hop(2)
    dy_s.hop(3)
    done.append(slot(1))
    done = hold_with(done, hn_s, dy_s)
    hn_s.hop(3)
    done.append(slot(2))
    done = hold_with(done, hn_s)
    dhn_c = Collect([d[1] for d in done])
    dhn_c.parts += [None] * (members - len(dhn_c.parts))
    dhn_c.hop("next")
    done += [slot(k) for k in range(3, members)]
    done = hold_with(done, dhn_c)
    lefts = [d[0] for d in done]
    dhn_c.parts = [d[1] for d in done]
    hn_slots = [hn_s.slot(k) for k in range(members)]
    dy_slots = [dy_s.slot(k) for k in range(members)]
    dhn_c.hop("far")
    dhn_c.hop("next_mid")
    d_down = weight_grads(0, 1, lefts, dy_slots)
    d_in = weight_grads(1, 2, lefts, hn_slots)
    d_down, d_in = hold_with((d_down, d_in), dhn_c)
    d_down = lax.psum(d_down, "rep")
    d_in = lax.psum(d_in, "rep")
    dhn_c.hop("far_mid")
    out_c = Collect([d[2] for d in done])
    out_c.hop("next")
    hold(dhn_c, out_c)
    dhn_c.hop("edge")
    out_c.hop("next_mid")
    hold(dhn_c, out_c)

    dhn = dhn_c.result()
    d_ffn_gain = jnp.sum(dhn * normed_two, axis=0)
    dhid = dy.astype(F32) + norm_back(dhn, normed_two, inv_two, ffn_gain, 1)
    dab = dhid.astype(BF)
    dob = jnp.zeros((QUERY_WIDTH, tokens), BF)
    for source, shard in out_shards:
        part = dot(shard, dab, 1, 1).astype(BF)
        dob = lax.dynamic_update_slice_in_dim(dob, part, source * shard.shape[0], 0)

    def out_grad(i):
        half = lax.dynamic_slice_in_dim(dab, i * (width // 2), width // 2, 1)
        return dot(ob, half, 1, 0).reshape(members, w_out.shape[0], width // 2)

    def columns_of(k):
        member = lax.rem(g + k, members)
        return lax.dynamic_slice_in_dim(xn, member * rows, rows, 1)

    xn_slots = [columns_of(0)] + [shift(columns_of(k), k) for k in range(1, members)]

    w_out_r = Reduced(out_grad, 2)
    dob, xn_slots = hold_with((dob, xn_slots), w_out_r)
    w_out_r.core()
    out_c.hop("far")
    dq_rot, dk_part, dv_part = attention_backward(info, q_low, kv, dob, of, soft_inv)
    dkv_part = [jnp.concatenate([dk_part[k], dv_part[k]], 0) for k in range(members)]
    dkv_part = [dkv_part[0]] + [x.astype(BF) for x in dkv_part[1:]]
    dq_rot, dkv_part = hold_with((dq_rot, dkv_part), w_out_r, out_c)
    dkv_c = Direct(dkv_part)
    dq_n = rotate(dq_rot.reshape(QUERY_HEADS, HEAD_SIZE, tokens), cos_t, sin_t, -1.0)
    d_q_gain = jnp.sum(dq_n * q_normed, axis=(0, 2))
    dq = norm_back(dq_n, q_normed, q_inv, q_gain[:, None], 1).reshape(QUERY_WIDTH, tokens)
    dq = dq.astype(BF)
    dq = hold_with(dq, dkv_c)
    dq_slots = [dq] + [shift(dq, k) for k in range(1, members)]
    w_out_r.rest()
    dkv = dkv_c.result()
    dk_n = rotate(
        dkv[:KEY_VALUE_WIDTH].reshape(KEY_VALUE_HEADS, HEAD_SIZE, tokens), cos_t, sin_t, -1.0
    )
    d_k_gain = jnp.sum(dk_n * k_normed, axis=(0, 2))
    dk = norm_back(dk_n, k_normed, k_inv, k_gain[:, None], 1).reshape(KEY_VALUE_WIDTH, tokens)
    dkv = jnp.concatenate([dk, dkv[KEY_VALUE_WIDTH:]], 0).astype(BF)
    dq_slots, dkv = hold_with((dq_slots, dkv), w_out_r)
    dkv_slots = [dkv] + [shift(dkv, k) for k in range(1, members)]
    w_out_r.members()
    dxn = features_grad(
        sources, dq, dkv, q_w.w, kv_w.w, q_w.whole(), kv_w.whole()
    )
    d_attn_gain = jnp.sum(dxn * normed_one, axis=0)
    input_grad = dhid + norm_back(dxn, normed_one, inv_one, attn_gain, 1)
    gains = jnp.concatenate([d_attn_gain, d_ffn_gain, d_q_gain, d_k_gain])
    dkv_slots, gains, input_grad = hold_with((dkv_slots, gains, input_grad), w_out_r)
    w_out_r.back()
    w_qkv_r = RepSum(*qkv_grad(core, xn_slots, dq_slots, dkv_slots), 0)
    w_qkv_r.core()
    gains = gains + swap(gains, 0)
    gains = hold_with(gains, w_qkv_r, w_out_r)
    w_qkv_r.rest()
    w_out_r.last()
    out_c.hop("far_mid")
    for b in rep_orders()[0][1:]:
        gains = gains + swap(gains, b)
    gains, d_in, d_down = hold_with((gains, d_in, d_down), w_qkv_r, w_out_r, out_c)
    w_qkv_r.back()
    d_w_in = interleave(d_in)
    gains = gains + move(gains, [(i, i ^ 1) for i in range(members)])
    out_c.hop("edge")
    d_w_down = d_down.astype(F32)
    gains, d_w_down, d_w_in = hold_with((gains, d_w_down, d_w_in), w_qkv_r, w_out_r, out_c)
    w_qkv_r.last()
    d_w_out = w_out_r.result()
    for b in range(1, members.bit_length() - 1):
        gains = gains + move(gains, [(i, i ^ (1 << b)) for i in range(members)])
    layer_output = (hid + out_c.result()).astype(BF)
    d_w_out, gains, layer_output = hold_with((d_w_out, gains, layer_output), w_qkv_r)
    d_w_qkv = w_qkv_r.result()
    return (
        layer_output[None],
        input_grad[None],
        d_w_qkv,
        d_w_out,
        d_w_in,
        d_w_down,
        gains[:width],
        gains[width : 2 * width],
        gains[2 * width : 2 * width + HEAD_SIZE],
        gains[2 * width + HEAD_SIZE :],
    )


def solution(mesh):
    in_specs = (
        P("rep", "grp", None),
        P("grp", None),
        P("grp", None),
        P("grp", None, None),
        P("grp", None),
        P(),
        P(),
        P(),
        P(),
        P("rep", "grp", None),
        P(),
        P("rep"),
    )
    out_specs = (
        P("rep", "grp", None),
        P("rep", "grp", None),
        P("grp", None),
        P("grp", None),
        P("grp", None, None),
        P("grp", None),
        P(),
        P(),
        P(),
        P(),
    )
    return jax.shard_map(
        per_device, mesh=mesh, in_specs=in_specs, out_specs=out_specs, check_vma=False
    )
```

time: 1020 us -> 725 us (0.71)
  local copies, waits for them, and re-layouts: 166 us -> 18.4 us
  Pallas kernels: 35.1 us -> 175 us
  matrix products: 132 us -> 16.4 us
  starting transfers between devices: 254 us -> 157 us
  other arithmetic: 136 us -> 93.7 us
  waiting for transfers between devices: 281 us -> 239 us
  between operations: 5.29 us -> 16.8 us
    pallas_call x0 -> x10, Pallas kernels: none -> 140 us  [the longest x4 62.4 us: ffn_slot(): pl.pallas_call(ffn_kernel, in_specs=[whole, whole, far, far, far], out_sp...]
    ppermute x90 -> x10, waiting for transfers between devices: 132 us -> 4.31 us  [swap(): return lax.ppermute(x, 'rep', [(i, i ^ 1 << b) for i in range(n)])]
    dot_general x45 -> x18, matrix products: 132 us -> 16.4 us  [dot(): lax.dot_general(a, b, (((ca,), (cb,)), ((), ())), preferred_element_type=...]
    ppermute x90 -> x10, starting transfers between devices: 77.6 us -> 3.08 us  [swap(): return lax.ppermute(x, 'rep', [(i, i ^ 1 << b) for i in range(n)])]
    ppermute x71 -> x70, waiting for transfers between devices: 149 us -> 213 us  [the longest x49 156 us: move(): return lax.ppermute(x, 'grp', pairs)]
    unnamed x313 -> x166, local copies, waits for them, and re-layouts: 53.8 us -> 9.94 us
    slice x7 -> x2, local copies, waits for them, and re-layouts: 36.9 us -> 1.38 us  [the longest x1 1.29 us: per_device(): kv_w = Shards(w_qkv[:, QUERY_WIDTH:])]
    ppermute x71 -> x70, starting transfers between devices: 176 us -> 154 us  [the longest x49 130 us: move(): return lax.ppermute(x, 'grp', pairs)]
  transfers between devices with their start and end apart: 161 -> 81, of which waited for: 56 -> 34; matrix products, arithmetic and copies ran while one was open for 42% -> 13% of each run, Pallas kernels for 3% -> 24%
where the time goes in v2:
time: 725 us; the launch traced here: 716 us
  waiting for transfers between devices  239 us (33%)
  Pallas kernels  175 us (24%)
  starting transfers between devices  157 us (22%)
  other arithmetic  93.7 us (13%)
  local copies, waits for them, and re-layouts  18.4 us (3%)
  between operations  16.8 us (2%)
  matrix products  16.4 us (2%)
    ppermute x49, waiting for transfers between devices, move(): return lax.ppermute(x, 'grp', pairs)  156 us
    ppermute x49, starting transfers between devices, move(): return lax.ppermute(x, 'grp', pairs)  130 us
    pallas_call x4, Pallas kernels, ffn_slot(): pl.pallas_call(ffn_kernel, in_specs=[whole, whole, far, far, far], out_sp...  62.4 us
    ppermute x21, waiting for transfers between devices, swap_rest(): return lax.ppermute(x, 'rep', [(i, i ^ 2 * j) for i in range(n)])  56.8 us
    pallas_call x2, Pallas kernels, weight_grads(): pl.pallas_call(functools.partial(grad_kernel, slots), grid=(many, 2), in_...  25.9 us
    pallas_call x1, Pallas kernels, attention_backward(): pl.pallas_call(backward_kernel, grid_spec=pltpu.PrefetchScalarGridSpec(nu...  25.2 us
    ppermute x21, starting transfers between devices, swap_rest(): return lax.ppermute(x, 'rep', [(i, i ^ 2 * j) for i in range(n)])  24.1 us
    select_n x17, other arithmetic, join_pair(): jnp.where(bit_of(b) == 0, jnp.concatenate([mine, other], axis), jnp.conca...  23.1 us
  transfers between devices with their start and end apart: 81, of which 34 were waited for; matrix products, arithmetic and copies ran while one was open for 13% of the time, Pallas kernels for 24%

profile of v2, /device:TPU:0, one launch (start us, length us, event | category | flops | bytes accessed | tf_op | source)
XLA Modules:
  0.0 716.4 jit_solution(2744021049123619842)
XLA Ops:
  67.0 20.4 %split_gate_up.1 = (bf16[1280,2048]{1,0:T(8,128)(2,1)}, bf16[1280,2048]{1,0:T(8,128)(2,1)}) custom-call(bf16[40960,128]{1,0:T(8,128)(2,1)} %bitcast.166), custom_call_target="tpu_custom_call" | custom-call | bytes 1048576 | tf_op jit(solution)/shard_map/split_gate_up/pallas_call | solution.py:451
  117.7 10.2 %attention_forward.1 = (bf16[1280,256]{1,0:T(8,128)(2,1)S(1)}, f32[1280,256]{1,0:T(8,128)S(1)}, f32[5,4,256]{2,1,0:T(4,128)S(1)}) custom-call(s32[6]{0:T(128)S(1)} %stack.101.info_ref, bf16[1280,256]{1,0:T(8,128)(2,1)S(1)} %bitcast.157, bf16[4,640,256]{2,1,0:T(8,128)(2,1)S(1)} %pad_maximum_fusion.k_ref.v_ref, ...), custom_call_target="tpu_custom_call" | custom-call | bytes 1048576 | tf_op jit(solution)/shard_map/attention_forward/pallas_call | solution.py:390
  158.4 16.1 %ffn_slot.4 = (bf16[3,1280,256]{2,1,0:T(8,128)(2,1)}, f32[256,2048]{1,0:T(8,128)}, f32[256,2048]{1,0:T(8,128)}) custom-call(bf16[256,2048]{1,0:T(8,128)(2,1)} %copy-done.18, bf16[256,2048]{1,0:T(8,128)(2,1)} %bitcast.2.dy_ref.refs_4_, bf16[1280,2048]{1,0:T(8,128)(2,1)} %get-tuple-element.302.g_hbm, bf16[1280,2048]{1,0:T(8,128)(2,1)} %get-tuple-element.303.u_hbm, ...), custom_call_target="tpu_custom_call" | custom-call | bytes 1048576 | tf_op jit(solution)/shard_map/ffn_slot/pallas_call | solution.py:507
  174.5 18.1 %collective-permute-done.26.hn_ref.refs_5_ = bf16[256,2048]{1,0:T(8,128)(2,1)S(1)} collective-permute-done((bf16[256,2048]{1,0:T(8,128)(2,1)S(1)}, bf16[256,2048]{1,0:T(8,128)(2,1)S(1)}, u32[]{:S(2)}, u32[]{:S(2)}) %collective-permute-start.26) | collective-permute-done | bytes 1048608 | tf_op jit(solution)/shard_map/ppermute | solution.py:104
  197.1 15.5 %ffn_slot.5 = (bf16[3,1280,256]{2,1,0:T(8,128)(2,1)}, bf16[256,2048]{1,0:T(8,128)(2,1)}, bf16[256,2048]{1,0:T(8,128)(2,1)}) custom-call(bf16[256,2048]{1,0:T(8,128)(2,1)} %copy-done.27, bf16[256,2048]{1,0:T(8,128)(2,1)} %collective-permute-done.23.dy_ref.refs_5_, bf16[1280,2048]{1,0:T(8,128)(2,1)} %get-tuple-element.302.g_hbm, ...), custom_call_target="tpu_custom_call" | custom-call | bytes 1048576 | tf_op jit(solution)/shard_map/ffn_slot/pallas_call | solution.py:507
  212.6 9.9 %collective-permute-done.31 = bf16[256,2048]{1,0:T(8,128)(2,1)} collective-permute-done((bf16[256,2048]{1,0:T(8,128)(2,1)}, bf16[256,2048]{1,0:T(8,128)(2,1)}, u32[]{:S(2)}, u32[]{:S(2)}) %collective-permute-start.31) | collective-permute-done | bytes 1048608 | tf_op jit(solution)/shard_map/ppermute | solution.py:104
  222.6 21.2 %collective-permute-done.32 = bf16[256,2048]{1,0:T(8,128)(2,1)} collective-permute-done((bf16[256,2048]{1,0:T(8,128)(2,1)}, bf16[256,2048]{1,0:T(8,128)(2,1)}, u32[]{:S(2)}, u32[]{:S(2)}) %collective-permute-start.32) | collective-permute-done | bytes 1048608 | tf_op jit(solution)/shard_map/ppermute | solution.py:104
  248.8 15.4 %ffn_slot.6 = (bf16[3,1280,256]{2,1,0:T(8,128)(2,1)}, bf16[256,2048]{1,0:T(8,128)(2,1)}, bf16[256,2048]{1,0:T(8,128)(2,1)}) custom-call(bf16[256,2048]{1,0:T(8,128)(2,1)} %broadcast_select_fusion.4.hn_ref, bf16[256,2048]{1,0:T(8,128)(2,1)} %broadcast_select_fusion.3.dy_ref.refs_6_, bf16[1280,2048]{1,0:T(8,128)(2,1)} %get-tuple-element.302.g_hbm, ...), custom_call_target="tpu_custom_call" | custom-call | bytes 1048576 | tf_op jit(solution)/shard_map/ffn_slot/pallas_call | solution.py:507
  275.2 15.5 %ffn_slot.7 = (bf16[3,1280,256]{2,1,0:T(8,128)(2,1)}, bf16[256,2048]{1,0:T(8,128)(2,1)}, bf16[256,2048]{1,0:T(8,128)(2,1)}) custom-call(bf16[256,2048]{1,0:T(8,128)(2,1)} %broadcast_select_fusion.2.hn_ref.refs_7_, bf16[256,2048]{1,0:T(8,128)(2,1)} %broadcast_select_fusion.1.dy_ref.refs_7_, bf16[1280,2048]{1,0:T(8,128)(2,1)} %get-tuple-element.302.g_hbm, ...), custom_call_target="tpu_custom_call" | custom-call | bytes 1048576 | tf_op jit(solution)/shard_map/ffn_slot/pallas_call | solution.py:507
  305.9 10.0 %weight_grads.2 = bf16[1280,2048]{1,0:T(8,128)(2,1)} custom-call(bf16[3,1280,256]{2,1,0:T(8,128)(2,1)} %get-tuple-element.357.refs_0_, bf16[3,1280,256]{2,1,0:T(8,128)(2,1)} %get-tuple-element.358.refs_1_, bf16[3,1280,256]{2,1,0:T(8,128)(2,1)} %get-tuple-element.359.refs_2_, bf16[3,1280,256]{2,1,0:T(8,128)(2,1)} %get-tuple-element.360.refs_3_, ...), custom_call_target="tpu_custom_call" | custom-call | bytes 1048576 | tf_op jit(solution)/shard_map/weight_grads/pallas_call | solution.py:541
  315.9 15.9 %weight_grads.3 = bf16[2560,2048]{1,0:T(8,128)(2,1)} custom-call(bf16[3,1280,256]{2,1,0:T(8,128)(2,1)} %get-tuple-element.357.refs_0_, bf16[3,1280,256]{2,1,0:T(8,128)(2,1)} %get-tuple-element.358.refs_1_, bf16[3,1280,256]{2,1,0:T(8,128)(2,1)} %get-tuple-element.359.refs_2_, bf16[3,1280,256]{2,1,0:T(8,128)(2,1)} %get-tuple-element.360.refs_3_, ...), custom_call_target="tpu_custom_call" | custom-call | bytes 1048576 | tf_op jit(solution)/shard_map/weight_grads/pallas_call | solution.py:541
  348.3 14.5 %collective-permute-start.39 = (bf16[256,2048]{1,0:T(8,128)(2,1)}, bf16[256,2048]{1,0:T(8,128)(2,1)}, u32[]{:S(2)}, u32[]{:S(2)}) collective-permute-start(bf16[256,2048]{1,0:T(8,128)(2,1)} %add_convert_fusion.4), channel_id=1, source_target_pairs={{0,1},{1,0},{2,3},{3,2},{4,5},{5,4},{6,7},{7,6},{8,9},{9,8},{10,11... | collective-permute-start | bytes 3145736 | tf_op jit(solution)/shard_map/ppermute | solution.py:104
  366.7 25.5 %collective-permute-done.39 = bf16[256,2048]{1,0:T(8,128)(2,1)} collective-permute-done((bf16[256,2048]{1,0:T(8,128)(2,1)}, bf16[256,2048]{1,0:T(8,128)(2,1)}, u32[]{:S(2)}, u32[]{:S(2)}) %collective-permute-start.39) | collective-permute-done | bytes 1048608 | tf_op jit(solution)/shard_map/ppermute | solution.py:104
  415.4 25.2 %attention_backward.1 = (f32[1280,256]{1,0:T(8,128)S(1)}, f32[4,320,256]{2,1,0:T(8,128)S(1)}, f32[4,320,256]{2,1,0:T(8,128)S(1)}) custom-call(s32[6]{0:T(128)S(1)} %stack.101.info_ref, bf16[1280,256]{1,0:T(8,128)(2,1)S(1)} %bitcast.158, bf16[4,640,256]{2,1,0:T(8,128)(2,1)} %copy-done.1, bf16[4,640,256]{2,1,0:T(8,128)(2,1)} %copy-done.1, ...), custom_call_target="tpu_custom_call" | custom-call | bytes 1048576 | tf_op jit(solution)/shard_map/attention_backward/pallas_call | solution.py:412
  461.0 18.3 %collective-permute-done.47 = bf16[640,256]{1,0:T(8,128)(2,1)} collective-permute-done((bf16[640,256]{1,0:T(8,128)(2,1)}, bf16[640,256]{1,0:T(8,128)(2,1)}, u32[]{:S(2)}, u32[]{:S(2)}) %collective-permute-start.47) | collective-permute-done | bytes 327712 | tf_op jit(solution)/shard_map/ppermute | solution.py:104
  488.9 19.2 %collective-permute-done.54 = bf16[4,320,256]{2,1,0:T(8,128)(2,1)} collective-permute-done((bf16[4,320,256]{2,1,0:T(8,128)(2,1)}, bf16[4,320,256]{2,1,0:T(8,128)(2,1)}, u32[]{:S(2)}, u32[]{:S(2)}) %collective-permute-start.54) | collective-permute-done | bytes 655392 | tf_op jit(solution)/shard_map/ppermute | solution.py:67
  508.1 19.2 %collective-permute-done.50.refs_6_ = bf16[1280,256]{1,0:T(8,128)(2,1)} collective-permute-done((bf16[1280,256]{1,0:T(8,128)(2,1)S(1)}, bf16[1280,256]{1,0:T(8,128)(2,1)}, u32[]{:S(2)}, u32[]{:S(2)}) %collective-permute-start.50) | collective-permute-done | bytes 655392 | tf_op jit(solution)/shard_map/ppermute | solution.py:104
  527.3 14.5 %collective-permute-start.55 = (bf16[640,256]{1,0:T(8,128)(2,1)S(1)}, bf16[640,256]{1,0:T(8,128)(2,1)}, u32[]{:S(2)}, u32[]{:S(2)}) collective-permute-start(bf16[640,256]{1,0:T(8,128)(2,1)S(1)} %pad_maximum_fusion.11.dkv_ref.refs_8_), channel_id=1, source_target_pairs={{0,1},{1,2},{2,3},{3,0},{4,5},{5,6},{6,7},{7,4},{8,9},{9,10},{10,1... | collective-permute-start | bytes 983048 | tf_op jit(solution)/shard_map/ppermute | solution.py:104
  551.1 9.2 %features_grad.1 = f32[256,2048]{1,0:T(8,128)} custom-call(s32[4]{0:T(128)} %pad_add_fusion.info_ref, bf16[1280,256]{1,0:T(8,128)(2,1)} %copy-done.24, bf16[640,256]{1,0:T(8,128)(2,1)} %copy-done.31, bf16[512,1280]{1,0:T(8,128)(2,1)} %copy-done.23, bf16[512,640]{1,0:T(8,128)(2,1)} %copy-done.30, bf16[3,512,1280]{2,1,0:T(8,128)(2,1)} %copy-done.8, ...), custom_call_target="tpu_custom_call" | custom-call | bytes 1048576 | tf_op jit(solution)/shard_map/features_grad/pallas_call | solution.py:642
  568.8 15.0 %collective-permute-start.60 = (bf16[320,256]{1,0:T(8,128)(2,1)S(1)}, bf16[320,256]{1,0:T(8,128)(2,1)}, u32[]{:S(2)}, u32[]{:S(2)}) collective-permute-start(bf16[320,256]{1,0:T(8,128)(2,1)S(1)} %get-tuple-element.490), channel_id=1, source_target_pairs={{0,1},{1,2},{2,3},{3,0},{4,5},{5,6},{6,7},{7,4},{8,9},{9,10},{10,1... | collective-permute-start | bytes 491528 | tf_op jit(solution)/shard_map/ppermute | solution.py:104
  624.4 10.1 %collective-permute-done.68 = bf16[64,1920]{1,0:T(8,128)(2,1)S(1)} collective-permute-done((bf16[64,1920]{1,0:T(8,128)(2,1)S(1)}, bf16[64,1920]{1,0:T(8,128)(2,1)S(1)}, u32[]{:S(2)}, u32[]{:S(2)}) %collective-permute-start.68) | collective-permute-done | bytes 245792 | tf_op jit(solution)/shard_map/ppermute | solution.py:67
  635.4 8.9 %collective-permute-done.70 = bf16[64,1920]{1,0:T(8,128)(2,1)S(1)} collective-permute-done((bf16[64,1920]{1,0:T(8,128)(2,1)S(1)}, bf16[64,1920]{1,0:T(8,128)(2,1)S(1)}, u32[]{:S(2)}, u32[]{:S(2)}) %collective-permute-start.70) | collective-permute-done | bytes 245792 | tf_op jit(solution)/shard_map/ppermute | solution.py:67
  644.9 21.8 %all-reduce.3.cloned.1.call-done = (bf16[2560,2048]{1,0:T(8,128)(2,1)}, bf16[1280,2048]{1,0:T(8,128)(2,1)}) async-done(((bf16[2560,2048]{1,0:T(8,128)(2,1)}, bf16[1280,2048]{1,0:T(8,128)(2,1)}), (bf16[2560,2048]{1,0:T(8,128)(2,1)}, bf16[1280,2048]{1,0:T(8,128)(2,1)})) %all-reduce.3.cloned.1.call-update) | async-done | bytes 15728656 | tf_op jit(solution)/shard_map/psum | solution.py:797
  676.7 13.7 %interleave.1 = f32[1280,2,2048]{2,1,0:T(2,128)} custom-call(bf16[2560,2048]{1,0:T(8,128)(2,1)} %get-tuple-element.439.gate_ref.up_ref, bf16[2560,2048]{1,0:T(8,128)(2,1)} %get-tuple-element.439.gate_ref.up_ref), custom_call_target="tpu_custom_call" | custom-call | bytes 1048576 | tf_op jit(solution)/shard_map/interleave/pallas_call | solution.py:562
  (458 shorter events, 316.4 us)
Async XLA Ops:
  7.2 659.5 %all-reduce.3.cloned.1.call-start = ((), (), s32[]{:S(2)}) async-start(), calls=%async_computation | async-start | bytes 31457280 | tf_op jit(solution)/shard_map/psum | solution.py:797
  54.8 32.7 %collective-permute-start.13 = (bf16[3,64,1280]{2,1,0:T(8,128)(2,1)S(1)}, bf16[3,64,1280]{2,1,0:T(8,128)(2,1)S(1)}, u32[]{:S(2)}, u32[]{:S(2)}) collective-permute-start(bf16[3,64,1280]{2,1,0:T(8,128)(2,1)S(1)} %pad_maximum_fusion.4), channel_id=1, source_target_pairs={{0,8},{4,12},{8,0},{12,4},{16,24},{20,28},{24,16},{28,20},{1,9},{5... | collective-permute-start | bytes 1474568 | tf_op jit(solution)/shard_map/ppermute | solution.py:67
  140.8 33.7 %collective-permute-start.28 = (bf16[256,2048]{1,0:T(8,128)(2,1)}, bf16[256,2048]{1,0:T(8,128)(2,1)}, u32[]{:S(2)}, u32[]{:S(2)}) collective-permute-start(bf16[256,2048]{1,0:T(8,128)(2,1)} %collective-permute-done.23.dy_ref.refs_5_), channel_id=1, source_target_pairs={{1,2},{2,1},{5,6},{6,5},{9,10},{10,9},{13,14},{14,13},{17,18},{18,... | collective-permute-start | bytes 3145736 | tf_op jit(solution)/shard_map/ppermute | solution.py:104
  155.0 37.7 %collective-permute-start.26 = (bf16[256,2048]{1,0:T(8,128)(2,1)S(1)}, bf16[256,2048]{1,0:T(8,128)(2,1)S(1)}, u32[]{:S(2)}, u32[]{:S(2)}) collective-permute-start(bf16[256,2048]{1,0:T(8,128)(2,1)S(1)} %multiply_convert_fusion.hn_ref.refs_4_), channel_id=1, source_target_pairs={{0,1},{1,0},{2,3},{3,2},{4,5},{5,4},{6,7},{7,6},{8,9},{9,8},{10,11... | collective-permute-start | bytes 3145736 | tf_op jit(solution)/shard_map/ppermute | solution.py:104
  156.4 36.2 %collective-permute-start.27 = (bf16[256,2048]{1,0:T(8,128)(2,1)S(1)}, bf16[256,2048]{1,0:T(8,128)(2,1)}, u32[]{:S(2)}, u32[]{:S(2)}) collective-permute-start(bf16[256,2048]{1,0:T(8,128)(2,1)S(1)} %multiply_convert_fusion.hn_ref.refs_4_), channel_id=1, source_target_pairs={{1,2},{2,1},{5,6},{6,5},{9,10},{10,9},{13,14},{14,13},{17,18},{18,... | collective-permute-start | bytes 3145736 | tf_op jit(solution)/shard_map/ppermute | solution.py:104
  195.6 48.2 %collective-permute-start.32 = (bf16[256,2048]{1,0:T(8,128)(2,1)}, bf16[256,2048]{1,0:T(8,128)(2,1)}, u32[]{:S(2)}, u32[]{:S(2)}) collective-permute-start(bf16[256,2048]{1,0:T(8,128)(2,1)} %collective-permute-done.28), channel_id=1, source_target_pairs={{1,0},{2,3},{5,4},{6,7},{9,8},{10,11},{13,12},{14,15},{17,16},{18,... | collective-permute-start | bytes 3145736 | tf_op jit(solution)/shard_map/ppermute | solution.py:104
  293.5 38.3 %collective-permute-start.36 = (bf16[256,2048]{1,0:T(8,128)(2,1)}, bf16[256,2048]{1,0:T(8,128)(2,1)S(1)}, u32[]{:S(2)}, u32[]{:S(2)}) collective-permute-start(bf16[256,2048]{1,0:T(8,128)(2,1)} %add_convert_fusion.6), channel_id=1, source_target_pairs={{1,2},{2,1},{5,6},{6,5},{9,10},{10,9},{13,14},{14,13},{17,18},{18,... | collective-permute-start | bytes 3145736 | tf_op jit(solution)/shard_map/ppermute | solution.py:104
  294.2 37.6 %collective-permute-start.35 = (bf16[256,2048]{1,0:T(8,128)(2,1)}, bf16[256,2048]{1,0:T(8,128)(2,1)}, u32[]{:S(2)}, u32[]{:S(2)}) collective-permute-start(bf16[256,2048]{1,0:T(8,128)(2,1)} %get-tuple-element.367), channel_id=1, source_target_pairs={{0,1},{3,2},{4,5},{7,6},{8,9},{11,10},{12,13},{15,14},{16,17},{19,... | collective-permute-start | bytes 3145736 | tf_op jit(solution)/shard_map/ppermute | solution.py:104
  303.5 38.8 %collective-permute-start.38 = (bf16[256,2048]{1,0:T(8,128)(2,1)}, bf16[256,2048]{1,0:T(8,128)(2,1)}, u32[]{:S(2)}, u32[]{:S(2)}) collective-permute-start(bf16[256,2048]{1,0:T(8,128)(2,1)} %get-tuple-element.372), channel_id=1, source_target_pairs={{0,1},{3,2},{4,5},{7,6},{8,9},{11,10},{12,13},{15,14},{16,17},{19,... | collective-permute-start | bytes 3145736 | tf_op jit(solution)/shard_map/ppermute | solution.py:104
  348.3 43.9 %collective-permute-start.39 = (bf16[256,2048]{1,0:T(8,128)(2,1)}, bf16[256,2048]{1,0:T(8,128)(2,1)}, u32[]{:S(2)}, u32[]{:S(2)}) collective-permute-start(bf16[256,2048]{1,0:T(8,128)(2,1)} %add_convert_fusion.4), channel_id=1, source_target_pairs={{0,1},{1,0},{2,3},{3,2},{4,5},{5,4},{6,7},{7,6},{8,9},{9,8},{10,11... | collective-permute-start | bytes 3145736 | tf_op jit(solution)/shard_map/ppermute | solution.py:104
  362.9 44.6 %collective-permute-start.41 = (bf16[256,512]{1,0:T(8,128)(2,1)}, bf16[256,512]{1,0:T(8,128)(2,1)S(1)}, u32[]{:S(2)}, u32[]{:S(2)}) collective-permute-start(bf16[256,512]{1,0:T(8,128)(2,1)} %copy-done.37), channel_id=1, source_target_pairs={{0,1},{1,2},{2,3},{3,0},{4,5},{5,6},{6,7},{7,4},{8,9},{9,10},{10,1... | collective-permute-start | bytes 786440 | tf_op jit(solution)/shard_map/ppermute | solution.py:104
  362.9 44.6 %collective-permute-start.42 = (bf16[256,512]{1,0:T(8,128)(2,1)}, bf16[256,512]{1,0:T(8,128)(2,1)S(1)}, u32[]{:S(2)}, u32[]{:S(2)}) collective-permute-start(bf16[256,512]{1,0:T(8,128)(2,1)} %copy-done.39), channel_id=1, source_target_pairs={{0,2},{1,3},{2,0},{3,1},{4,6},{5,7},{6,4},{7,5},{8,10},{9,11},{10,... | collective-permute-start | bytes 786440 | tf_op jit(solution)/shard_map/ppermute | solution.py:104
  364.8 42.7 %collective-permute-start.43 = (bf16[256,512]{1,0:T(8,128)(2,1)S(1)}, bf16[256,512]{1,0:T(8,128)(2,1)S(1)}, u32[]{:S(2)}, u32[]{:S(2)}) collective-permute-start(bf16[256,512]{1,0:T(8,128)(2,1)S(1)} %copy-done.36), channel_id=1, source_target_pairs={{0,3},{1,0},{2,1},{3,2},{4,7},{5,4},{6,5},{7,6},{8,11},{9,8},{10,9... | collective-permute-start | bytes 786440 | tf_op jit(solution)/shard_map/ppermute | solution.py:104
  408.9 34.3 %collective-permute-start.44 = (bf16[4,320,1024]{2,1,0:T(8,128)(2,1)}, bf16[4,320,1024]{2,1,0:T(8,128)(2,1)}, u32[]{:S(2)}, u32[]{:S(2)}) collective-permute-start(bf16[4,320,1024]{2,1,0:T(8,128)(2,1)} %bitcast.41), channel_id=1, source_target_pairs={{0,4},{4,0},{8,12},{12,8},{16,20},{20,16},{24,28},{28,24},{1,5},{5... | collective-permute-start | bytes 7864328 | tf_op jit(solution)/shard_map/ppermute | solution.py:39
  409.7 33.5 %collective-permute-start.45 = (bf16[256,2048]{1,0:T(8,128)(2,1)}, bf16[256,2048]{1,0:T(8,128)(2,1)}, u32[]{:S(2)}, u32[]{:S(2)}) collective-permute-start(bf16[256,2048]{1,0:T(8,128)(2,1)} %get-tuple-element.386), channel_id=1, source_target_pairs={{0,1},{3,2},{4,5},{7,6},{8,9},{11,10},{12,13},{15,14},{16,17},{19,... | collective-permute-start | bytes 3145736 | tf_op jit(solution)/shard_map/ppermute | solution.py:104
  447.5 37.0 %collective-permute-start.52 = (bf16[4,320,256]{2,1,0:T(8,128)(2,1)}, bf16[4,320,256]{2,1,0:T(8,128)(2,1)S(1)}, u32[]{:S(2)}, u32[]{:S(2)}) collective-permute-start(bf16[4,320,256]{2,1,0:T(8,128)(2,1)} %get-tuple-element.480), channel_id=1, source_target_pairs={{0,8},{4,12},{8,0},{12,4},{16,24},{20,28},{24,16},{28,20},{1,9},{5... | collective-permute-start | bytes 1966088 | tf_op jit(solution)/shard_map/ppermute | solution.py:67
  448.9 40.1 %collective-permute-start.53 = (bf16[4,320,256]{2,1,0:T(8,128)(2,1)}, bf16[4,320,256]{2,1,0:T(8,128)(2,1)}, u32[]{:S(2)}, u32[]{:S(2)}) collective-permute-start(bf16[4,320,256]{2,1,0:T(8,128)(2,1)} %get-tuple-element.479), channel_id=1, source_target_pairs={{0,16},{4,20},{8,24},{12,28},{16,0},{20,4},{24,8},{28,12},{1,17},{... | collective-permute-start | bytes 1966088 | tf_op jit(solution)/shard_map/ppermute | solution.py:67
  460.6 47.5 %collective-permute-start.54 = (bf16[4,320,256]{2,1,0:T(8,128)(2,1)}, bf16[4,320,256]{2,1,0:T(8,128)(2,1)}, u32[]{:S(2)}, u32[]{:S(2)}) collective-permute-start(bf16[4,320,256]{2,1,0:T(8,128)(2,1)} %get-tuple-element.478), channel_id=1, source_target_pairs={{0,24},{4,28},{8,16},{12,20},{16,8},{20,12},{24,0},{28,4},{1,25},{... | collective-permute-start | bytes 1966088 | tf_op jit(solution)/shard_map/ppermute | solution.py:67
  482.5 44.9 %collective-permute-start.50 = (bf16[1280,256]{1,0:T(8,128)(2,1)S(1)}, bf16[1280,256]{1,0:T(8,128)(2,1)}, u32[]{:S(2)}, u32[]{:S(2)}) collective-permute-start(bf16[1280,256]{1,0:T(8,128)(2,1)S(1)} %get-tuple-element.410.dq_ref.refs_4_), channel_id=1, source_target_pairs={{0,2},{1,3},{2,0},{3,1},{4,6},{5,7},{6,4},{7,5},{8,10},{9,11},{10,... | collective-permute-start | bytes 1966088 | tf_op jit(solution)/shard_map/ppermute | solution.py:104
  484.4 42.9 %collective-permute-start.51 = (bf16[1280,256]{1,0:T(8,128)(2,1)S(1)}, bf16[1280,256]{1,0:T(8,128)(2,1)}, u32[]{:S(2)}, u32[]{:S(2)}) collective-permute-start(bf16[1280,256]{1,0:T(8,128)(2,1)S(1)} %get-tuple-element.410.dq_ref.refs_4_), channel_id=1, source_target_pairs={{0,3},{1,0},{2,1},{3,2},{4,7},{5,4},{6,5},{7,6},{8,11},{9,8},{10,9... | collective-permute-start | bytes 1966088 | tf_op jit(solution)/shard_map/ppermute | solution.py:104
  527.3 60.0 %collective-permute-start.55 = (bf16[640,256]{1,0:T(8,128)(2,1)S(1)}, bf16[640,256]{1,0:T(8,128)(2,1)}, u32[]{:S(2)}, u32[]{:S(2)}) collective-permute-start(bf16[640,256]{1,0:T(8,128)(2,1)S(1)} %pad_maximum_fusion.11.dkv_ref.refs_8_), channel_id=1, source_target_pairs={{0,1},{1,2},{2,3},{3,0},{4,5},{5,6},{6,7},{7,4},{8,9},{9,10},{10,1... | collective-permute-start | bytes 983048 | tf_op jit(solution)/shard_map/ppermute | solution.py:104
  541.8 45.5 %collective-permute-start.56 = (bf16[640,256]{1,0:T(8,128)(2,1)S(1)}, bf16[640,256]{1,0:T(8,128)(2,1)}, u32[]{:S(2)}, u32[]{:S(2)}) collective-permute-start(bf16[640,256]{1,0:T(8,128)(2,1)S(1)} %pad_maximum_fusion.11.dkv_ref.refs_8_), channel_id=1, source_target_pairs={{0,2},{1,3},{2,0},{3,1},{4,6},{5,7},{6,4},{7,5},{8,10},{9,11},{10,... | collective-permute-start | bytes 983048 | tf_op jit(solution)/shard_map/ppermute | solution.py:104
  544.7 42.6 %collective-permute-start.57 = (bf16[640,256]{1,0:T(8,128)(2,1)S(1)}, bf16[640,256]{1,0:T(8,128)(2,1)}, u32[]{:S(2)}, u32[]{:S(2)}) collective-permute-start(bf16[640,256]{1,0:T(8,128)(2,1)S(1)} %pad_maximum_fusion.11.dkv_ref.refs_8_), channel_id=1, source_target_pairs={{0,3},{1,0},{2,1},{3,2},{4,7},{5,4},{6,5},{7,6},{8,11},{9,8},{10,9... | collective-permute-start | bytes 983048 | tf_op jit(solution)/shard_map/ppermute | solution.py:104
  549.2 37.3 %collective-permute-start.59 = (bf16[320,256]{1,0:T(8,128)(2,1)}, bf16[320,256]{1,0:T(8,128)(2,1)}, u32[]{:S(2)}, u32[]{:S(2)}) collective-permute-start(bf16[320,256]{1,0:T(8,128)(2,1)} %get-tuple-element.491), channel_id=1, source_target_pairs={{0,2},{1,3},{2,0},{3,1},{4,6},{5,7},{6,4},{7,5},{8,10},{9,11},{10,... | collective-permute-start | bytes 491528 | tf_op jit(solution)/shard_map/ppermute | solution.py:104
  (140 other events, 1948.5 us)
Sparse Core Ops, SparseCore 0:
  415.5 251.2 all-reduce.2

commit v3 on v2

--- a/solution.py
+++ b/solution.py
@@ -522,56 +522,69 @@
 
 
 def grad_kernel(slots, *refs):
-    rows = jnp.concatenate([r[0] for r in refs[:slots]], 1)
-    right = jnp.concatenate([r[...] for r in refs[slots : 2 * slots]], 0)
-    half = right.shape[1] // 2
+    left, dy, hn = refs[:slots], refs[slots : 2 * slots], refs[2 * slots : 3 * slots]
     out_ref = refs[-1]
-    for i in range(2):
-        lanes = slice(i * half, (i + 1) * half)
-        out_ref[:, lanes] = dot(rows, right[:, lanes], 1, 0).astype(BF)
-
-
-def weight_grads(c, many, left, right):
+    half = out_ref.shape[1] // 2
+
+    def product(right):
+        rows = jnp.concatenate([r[0] for r in left], 1)
+        for i in range(2):
+            lanes = slice(i * half, (i + 1) * half)
+            both = jnp.concatenate([r[:, lanes] for r in right], 0)
+            out_ref[:, lanes] = dot(rows, both, 1, 0).astype(BF)
+
+    c = pl.program_id(0)
+    pl.when(c == 0)(lambda: product(dy))
+    pl.when(c > 0)(lambda: product(hn))
+
+
+def weight_grads(left, dy, hn):
     slots = len(left)
     _, units, tokens = left[0].shape
-    width = right[0].shape[1]
+    width = dy[0].shape[1]
     cut = units // 2
-    lefts = pl.BlockSpec((1, cut, tokens), lambda i, m: (c + i, m, 0))
-    rights = pl.BlockSpec((tokens, width), lambda i, m: (0, 0))
+    lefts = pl.BlockSpec((1, cut, tokens), lambda c, m: (c, m, 0))
+    rights = pl.BlockSpec((tokens, width), lambda c, m: (0, 0))
     return pl.pallas_call(
         functools.partial(grad_kernel, slots),
-        grid=(many, 2),
-        in_specs=[lefts] * slots + [rights] * slots,
-        out_specs=pl.BlockSpec((cut, width), lambda i, m: (2 * i + m, 0)),
-        out_shape=jax.ShapeDtypeStruct((many * units, width), BF),
+        grid=(3, 2),
+        in_specs=[lefts] * slots + [rights] * (2 * slots),
+        out_specs=pl.BlockSpec((cut, width), lambda c, m: (2 * c + m, 0)),
+        out_shape=jax.ShapeDtypeStruct((3 * units, width), BF),
         compiler_params=pltpu.CompilerParams(vmem_limit_bytes=VMEM),
         cost_estimate=pl.CostEstimate(flops=0, bytes_accessed=2**20, transcendentals=0),
         name="weight_grads",
-    )(*left, *right)
-
-
-def interleave_kernel(gate_ref, up_ref, out_ref):
-    out_ref[:, 0, :] = gate_ref[...].astype(F32)
-    out_ref[:, 1, :] = up_ref[...].astype(F32)
-
-
-def interleave(both):
-    units, width = both.shape[0] // 2, both.shape[1]
+    )(*left, *dy, *hn)
+
+
+def widen_kernel(down_ref, gate_ref, up_ref, down_out, in_out):
+    down_out[...] = down_ref[...].astype(F32)
+    in_out[:, 0, :] = gate_ref[...].astype(F32)
+    in_out[:, 1, :] = up_ref[...].astype(F32)
+
+
+def widen(grads):
+    units, width = grads.shape[0] // 3, grads.shape[1]
     block = 128
     blocks = units // block
     return pl.pallas_call(
-        interleave_kernel,
+        widen_kernel,
         grid=(blocks,),
         in_specs=[
+            pl.BlockSpec((block, width), lambda i, c=c: (c * blocks + i, 0)) for c in range(3)
+        ],
+        out_specs=[
             pl.BlockSpec((block, width), lambda i: (i, 0)),
-            pl.BlockSpec((block, width), lambda i: (blocks + i, 0)),
+            pl.BlockSpec((block, 2, width), lambda i: (i, 0, 0)),
         ],
-        out_specs=pl.BlockSpec((block, 2, width), lambda i: (i, 0, 0)),
-        out_shape=jax.ShapeDtypeStruct((units, 2, width), F32),
+        out_shape=[
+            jax.ShapeDtypeStruct((units, width), F32),
+            jax.ShapeDtypeStruct((units, 2, width), F32),
+        ],
         compiler_params=pltpu.CompilerParams(vmem_limit_bytes=VMEM),
         cost_estimate=pl.CostEstimate(flops=0, bytes_accessed=2**20, transcendentals=0),
-        name="interleave",
-    )(both, both)
+        name="widen",
+    )(grads, grads, grads)
 
 
 def qkv_grad_kernel(slots, info_ref, *refs):
@@ -744,15 +757,16 @@
     q_normed = q_raw * q_inv
     q_low = rotate(q_normed * q_gain[:, None], cos_t, sin_t, 1.0).astype(BF)
     q_low = q_low.reshape(QUERY_WIDTH, tokens)
-    kv, q_low, q_raw, dy = hold_with((kv, q_low, q_raw, dy), out_w)
-    kv = jnp.stack(kv)
-
     dy_s = Spread(dy)
     dy_s.hop(1)
+    kv, q_low, q_raw = hold_with((kv, q_low, q_raw), out_w, dy_s)
+    kv = jnp.stack(kv)
+
+    dy_s.hop(2)
     out_w.rest()
     ob, of, soft_inv = attention_forward(info, q_low, kv)
     ob, of, soft_inv = hold_with((ob, of, soft_inv), out_w, dy_s)
-    dy_s.hop(2)
+    dy_s.hop(3)
     out_w.core()
     out_shards = out_w.shards()
     hid = xf
@@ -773,7 +787,6 @@
     done = [slot(0)]
     done = hold_with(done, hn_s, dy_s)
     hn_s.hop(2)
-    dy_s.hop(3)
     done.append(slot(1))
     done = hold_with(done, hn_s, dy_s)
     hn_s.hop(3)
@@ -790,11 +803,9 @@
     dy_slots = [dy_s.slot(k) for k in range(members)]
     dhn_c.hop("far")
     dhn_c.hop("next_mid")
-    d_down = weight_grads(0, 1, lefts, dy_slots)
-    d_in = weight_grads(1, 2, lefts, hn_slots)
-    d_down, d_in = hold_with((d_down, d_in), dhn_c)
-    d_down = lax.psum(d_down, "rep")
-    d_in = lax.psum(d_in, "rep")
+    grads = weight_grads(lefts, dy_slots, hn_slots)
+    grads = hold_with(grads, dhn_c)
+    grads = lax.psum_scatter(grads, "rep", scatter_dimension=0, tiled=True)
     dhn_c.hop("far_mid")
     out_c = Collect([d[2] for d in done])
     out_c.hop("next")
@@ -835,7 +846,8 @@
     d_q_gain = jnp.sum(dq_n * q_normed, axis=(0, 2))
     dq = norm_back(dq_n, q_normed, q_inv, q_gain[:, None], 1).reshape(QUERY_WIDTH, tokens)
     dq = dq.astype(BF)
-    dq = hold_with(dq, dkv_c)
+    dq, grads = hold_with((dq, grads), dkv_c)
+    grads = lax.all_gather(grads, "rep", axis=0, tiled=True)
     dq_slots = [dq] + [shift(dq, k) for k in range(1, members)]
     w_out_r.rest()
     dkv = dkv_c.result()
@@ -865,12 +877,11 @@
     out_c.hop("far_mid")
     for b in rep_orders()[0][1:]:
         gains = gains + swap(gains, b)
-    gains, d_in, d_down = hold_with((gains, d_in, d_down), w_qkv_r, w_out_r, out_c)
+    gains, grads = hold_with((gains, grads), w_qkv_r, w_out_r, out_c)
     w_qkv_r.back()
-    d_w_in = interleave(d_in)
+    d_w_down, d_w_in = widen(grads)
     gains = gains + move(gains, [(i, i ^ 1) for i in range(members)])
     out_c.hop("edge")
-    d_w_down = d_down.astype(F32)
     gains, d_w_down, d_w_in = hold_with((gains, d_w_down, d_w_in), w_qkv_r, w_out_r, out_c)
     w_qkv_r.last()
     d_w_out = w_out_r.result()

time: 725 us -> 686 us (0.946)
  waiting for transfers between devices: 239 us -> 221 us
  starting transfers between devices: 157 us -> 143 us
  other arithmetic: 93.7 us -> 83.9 us
    psum x1 -> x0, waiting for transfers between devices: 21.8 us -> none  [per_device(): d_in = lax.psum(d_in, 'rep')]
    ppermute x49, starting transfers between devices: 130 us -> 115 us  [move(): return lax.ppermute(x, 'grp', pairs)]
    pallas_call x3 -> x2, Pallas kernels: 39.6 us -> 40 us  [the longest x1 23 us: weight_grads(): pl.pallas_call(functools.partial(grad_kernel, slots), grid=(3, 2), in_spe...]
  transfers between devices with their start and end apart: 81 -> 82, of which waited for: 34 -> 35; matrix products, arithmetic and copies ran while one was open for 13% -> 12% of each run, Pallas kernels for 24% -> 26%
where the time goes in v3:
time: 686 us; the launch traced here: 678 us
  waiting for transfers between devices  221 us (32%)
  Pallas kernels  174 us (25%)
  starting transfers between devices  143 us (21%)
  other arithmetic  83.9 us (12%)
  local copies, waits for them, and re-layouts  21.3 us (3%)
  matrix products  17.4 us (3%)
  between operations  16.8 us (2%)
    ppermute x49, waiting for transfers between devices, move(): return lax.ppermute(x, 'grp', pairs)  155 us
    ppermute x49, starting transfers between devices, move(): return lax.ppermute(x, 'grp', pairs)  115 us
    pallas_call x4, Pallas kernels, ffn_slot(): pl.pallas_call(ffn_kernel, in_specs=[whole, whole, far, far, far], out_sp...  62.4 us
    ppermute x21, waiting for transfers between devices, swap_rest(): return lax.ppermute(x, 'rep', [(i, i ^ 2 * j) for i in range(n)])  61.1 us
    ppermute x21, starting transfers between devices, swap_rest(): return lax.ppermute(x, 'rep', [(i, i ^ 2 * j) for i in range(n)])  25 us
    pallas_call x1, Pallas kernels, attention_backward(): pl.pallas_call(backward_kernel, grid_spec=pltpu.PrefetchScalarGridSpec(nu...  24.9 us
    select_n x17, other arithmetic, join_pair(): jnp.where(bit_of(b) == 0, jnp.concatenate([mine, other], axis), jnp.conca...  23 us
    pallas_call x1, Pallas kernels, weight_grads(): pl.pallas_call(functools.partial(grad_kernel, slots), grid=(3, 2), in_spe...  23 us
  transfers between devices with their start and end apart: 82, of which 35 were waited for; matrix products, arithmetic and copies ran while one was open for 12% of the time, Pallas kernels for 26%

profile of v3, /device:TPU:0, one launch (start us, length us, event | category | flops | bytes accessed | tf_op | source)
XLA Modules:
  0.0 677.5 jit_solution(18092292176917445000)
XLA Ops:
  30.8 7.2 %collective-permute-done.7 = bf16[64,1280]{1,0:T(8,128)(2,1)} collective-permute-done((bf16[64,1280]{1,0:T(8,128)(2,1)}, bf16[64,1280]{1,0:T(8,128)(2,1)}, u32[]{:S(2)}, u32[]{:S(2)}) %collective-permute-start.7) | collective-permute-done | bytes 163872 | tf_op jit(solution)/shard_map/ppermute | solution.py:104
  67.1 20.4 %split_gate_up.1 = (bf16[1280,2048]{1,0:T(8,128)(2,1)}, bf16[1280,2048]{1,0:T(8,128)(2,1)}) custom-call(bf16[40960,128]{1,0:T(8,128)(2,1)} %bitcast.164), custom_call_target="tpu_custom_call" | custom-call | bytes 1048576 | tf_op jit(solution)/shard_map/split_gate_up/pallas_call | solution.py:451
  110.1 8.6 %collective-permute-done.17 = bf16[40,2048]{1,0:T(8,128)(2,1)S(1)} collective-permute-done((bf16[40,2048]{1,0:T(8,128)(2,1)S(1)}, bf16[40,2048]{1,0:T(8,128)(2,1)S(1)}, u32[]{:S(2)}, u32[]{:S(2)}) %collective-permute-start.17) | collective-permute-done | bytes 163872 | tf_op jit(solution)/shard_map/ppermute | solution.py:104
  118.7 11.5 %collective-permute-done.18 = bf16[40,2048]{1,0:T(8,128)(2,1)S(1)} collective-permute-done((bf16[40,2048]{1,0:T(8,128)(2,1)S(1)}, bf16[40,2048]{1,0:T(8,128)(2,1)S(1)}, u32[]{:S(2)}, u32[]{:S(2)}) %collective-permute-start.18) | collective-permute-done | bytes 163872 | tf_op jit(solution)/shard_map/ppermute | solution.py:104
  141.0 10.2 %attention_forward.1 = (bf16[1280,256]{1,0:T(8,128)(2,1)S(1)}, f32[1280,256]{1,0:T(8,128)S(1)}, f32[5,4,256]{2,1,0:T(4,128)S(1)}) custom-call(s32[6]{0:T(128)S(1)} %stack.101.info_ref, bf16[1280,256]{1,0:T(8,128)(2,1)S(1)} %bitcast.157, bf16[4,640,256]{2,1,0:T(8,128)(2,1)S(1)} %pad_maximum_fusion.k_ref.v_ref, ...), custom_call_target="tpu_custom_call" | custom-call | bytes 1048576 | tf_op jit(solution)/shard_map/attention_forward/pallas_call | solution.py:390
  184.2 16.0 %ffn_slot.4 = (bf16[3,1280,256]{2,1,0:T(8,128)(2,1)}, f32[256,2048]{1,0:T(8,128)}, f32[256,2048]{1,0:T(8,128)}) custom-call(bf16[256,2048]{1,0:T(8,128)(2,1)} %copy-done.20, bf16[256,2048]{1,0:T(8,128)(2,1)} %bitcast.165, bf16[1280,2048]{1,0:T(8,128)(2,1)} %get-tuple-element.310.g_hbm, bf16[1280,2048]{1,0:T(8,128)(2,1)} %get-tuple-element.311.u_hbm, ...), custom_call_target="tpu_custom_call" | custom-call | bytes 1048576 | tf_op jit(solution)/shard_map/ffn_slot/pallas_call | solution.py:507
  200.3 15.4 %collective-permute-done.28.hn_ref.refs_9_ = bf16[256,2048]{1,0:T(8,128)(2,1)} collective-permute-done((bf16[256,2048]{1,0:T(8,128)(2,1)S(1)}, bf16[256,2048]{1,0:T(8,128)(2,1)}, u32[]{:S(2)}, u32[]{:S(2)}) %collective-permute-start.28) | collective-permute-done | bytes 1048608 | tf_op jit(solution)/shard_map/ppermute | solution.py:104
  218.8 15.4 %ffn_slot.5 = (bf16[3,1280,256]{2,1,0:T(8,128)(2,1)}, bf16[256,2048]{1,0:T(8,128)(2,1)}, bf16[256,2048]{1,0:T(8,128)(2,1)}) custom-call(bf16[256,2048]{1,0:T(8,128)(2,1)} %collective-permute-done.28.hn_ref.refs_9_, bf16[256,2048]{1,0:T(8,128)(2,1)} %collective-permute-done.20.dy_ref.refs_5_, bf16[1280,2048]{1,0:T(8,128)(2,1)} %get-tuple-element.310.g_hbm, ...), custom_call_target="tpu_custom_call" | custom-call | bytes 1048576 | tf_op jit(solution)/shard_map/ffn_slot/pallas_call | solution.py:507
  234.2 10.0 %collective-permute-done.32 = bf16[256,2048]{1,0:T(8,128)(2,1)S(1)} collective-permute-done((bf16[256,2048]{1,0:T(8,128)(2,1)}, bf16[256,2048]{1,0:T(8,128)(2,1)S(1)}, u32[]{:S(2)}, u32[]{:S(2)}) %collective-permute-start.32) | collective-permute-done | bytes 1048608 | tf_op jit(solution)/shard_map/ppermute | solution.py:104
  249.1 15.5 %ffn_slot.6 = (bf16[3,1280,256]{2,1,0:T(8,128)(2,1)}, bf16[256,2048]{1,0:T(8,128)(2,1)}, bf16[256,2048]{1,0:T(8,128)(2,1)}) custom-call(bf16[256,2048]{1,0:T(8,128)(2,1)} %broadcast_select_fusion.4.hn_ref, bf16[256,2048]{1,0:T(8,128)(2,1)} %broadcast_select_fusion.3.dy_ref.refs_6_, bf16[1280,2048]{1,0:T(8,128)(2,1)} %get-tuple-element.310.g_hbm, ...), custom_call_target="tpu_custom_call" | custom-call | bytes 1048576 | tf_op jit(solution)/shard_map/ffn_slot/pallas_call | solution.py:507
  274.5 15.5 %ffn_slot.7 = (bf16[3,1280,256]{2,1,0:T(8,128)(2,1)}, bf16[256,2048]{1,0:T(8,128)(2,1)}, bf16[256,2048]{1,0:T(8,128)(2,1)}) custom-call(bf16[256,2048]{1,0:T(8,128)(2,1)} %broadcast_select_fusion.2.hn_ref.refs_11_, bf16[256,2048]{1,0:T(8,128)(2,1)} %broadcast_select_fusion.1.dy_ref.refs_7_, bf16[1280,2048]{1,0:T(8,128)(2,1)} %get-tuple-element.310.g_hbm, ...), custom_call_target="tpu_custom_call" | custom-call | bytes 1048576 | tf_op jit(solution)/shard_map/ffn_slot/pallas_call | solution.py:507
  294.7 8.8 %collective-permute-start.35 = (bf16[256,2048]{1,0:T(8,128)(2,1)}, bf16[256,2048]{1,0:T(8,128)(2,1)}, u32[]{:S(2)}, u32[]{:S(2)}) collective-permute-start(bf16[256,2048]{1,0:T(8,128)(2,1)} %get-tuple-element.378), channel_id=1, source_target_pairs={{0,1},{3,2},{4,5},{7,6},{8,9},{11,10},{12,13},{15,14},{16,17},{19,... | collective-permute-start | bytes 3145736 | tf_op jit(solution)/shard_map/ppermute | solution.py:104
  304.6 23.0 %weight_grads.1 = bf16[3840,2048]{1,0:T(8,128)(2,1)} custom-call(bf16[3,1280,256]{2,1,0:T(8,128)(2,1)} %get-tuple-element.368.refs_0_, bf16[3,1280,256]{2,1,0:T(8,128)(2,1)} %get-tuple-element.369.refs_1_, bf16[3,1280,256]{2,1,0:T(8,128)(2,1)} %get-tuple-element.370.refs_2_, bf16[3,1280,256]{2,1,0:T(8,128)(2,1)} %get-tuple-element.371.refs_3_, ...), custom_call_target="tpu_custom_call" | custom-call | bytes 1048576 | tf_op jit(solution)/shard_map/weight_grads/pallas_call | solution.py:548
  332.2 16.8 %collective-permute-done.38 = bf16[256,2048]{1,0:T(8,128)(2,1)S(1)} collective-permute-done((bf16[256,2048]{1,0:T(8,128)(2,1)}, bf16[256,2048]{1,0:T(8,128)(2,1)S(1)}, u32[]{:S(2)}, u32[]{:S(2)}) %collective-permute-start.38) | collective-permute-done | bytes 1048608 | tf_op jit(solution)/shard_map/ppermute | solution.py:104
  363.8 24.6 %collective-permute-done.39 = bf16[256,2048]{1,0:T(8,128)(2,1)} collective-permute-done((bf16[256,2048]{1,0:T(8,128)(2,1)}, bf16[256,2048]{1,0:T(8,128)(2,1)}, u32[]{:S(2)}, u32[]{:S(2)}) %collective-permute-start.39) | collective-permute-done | bytes 1048608 | tf_op jit(solution)/shard_map/ppermute | solution.py:104
  411.5 24.9 %attention_backward.1 = (f32[1280,256]{1,0:T(8,128)S(1)}, f32[4,320,256]{2,1,0:T(8,128)S(1)}, f32[4,320,256]{2,1,0:T(8,128)S(1)}) custom-call(s32[6]{0:T(128)S(1)} %stack.101.info_ref, bf16[1280,256]{1,0:T(8,128)(2,1)S(1)} %bitcast.158, bf16[4,640,256]{2,1,0:T(8,128)(2,1)} %copy-done.1, bf16[4,640,256]{2,1,0:T(8,128)(2,1)} %copy-done.1, ...), custom_call_target="tpu_custom_call" | custom-call | bytes 1048576 | tf_op jit(solution)/shard_map/attention_backward/pallas_call | solution.py:412
  446.8 20.3 %collective-permute-done.47 = bf16[640,256]{1,0:T(8,128)(2,1)S(1)} collective-permute-done((bf16[640,256]{1,0:T(8,128)(2,1)S(1)}, bf16[640,256]{1,0:T(8,128)(2,1)S(1)}, u32[]{:S(2)}, u32[]{:S(2)}) %collective-permute-start.47) | collective-permute-done | bytes 327712 | tf_op jit(solution)/shard_map/ppermute | solution.py:104
  483.7 22.9 %collective-permute-done.52 = bf16[4,320,256]{2,1,0:T(8,128)(2,1)S(1)} collective-permute-done((bf16[4,320,256]{2,1,0:T(8,128)(2,1)}, bf16[4,320,256]{2,1,0:T(8,128)(2,1)S(1)}, u32[]{:S(2)}, u32[]{:S(2)}) %collective-permute-start.52) | collective-permute-done | bytes 655392 | tf_op jit(solution)/shard_map/ppermute | solution.py:67
  511.0 16.9 %collective-permute-done.54 = bf16[4,320,256]{2,1,0:T(8,128)(2,1)} collective-permute-done((bf16[4,320,256]{2,1,0:T(8,128)(2,1)}, bf16[4,320,256]{2,1,0:T(8,128)(2,1)}, u32[]{:S(2)}, u32[]{:S(2)}) %collective-permute-start.54) | collective-permute-done | bytes 655392 | tf_op jit(solution)/shard_map/ppermute | solution.py:67
  533.4 8.0 %collective-permute-start.55 = (bf16[640,256]{1,0:T(8,128)(2,1)S(1)}, bf16[640,256]{1,0:T(8,128)(2,1)}, u32[]{:S(2)}, u32[]{:S(2)}) collective-permute-start(bf16[640,256]{1,0:T(8,128)(2,1)S(1)} %pad_maximum_fusion.11.dkv_ref.refs_8_), channel_id=1, source_target_pairs={{0,1},{1,2},{2,3},{3,0},{4,5},{5,6},{6,7},{7,4},{8,9},{9,10},{10,1... | collective-permute-start | bytes 983048 | tf_op jit(solution)/shard_map/ppermute | solution.py:104
  549.9 8.2 %features_grad.1 = f32[256,2048]{1,0:T(8,128)} custom-call(s32[4]{0:T(128)} %pad_add_fusion.info_ref, bf16[1280,256]{1,0:T(8,128)(2,1)} %copy-done.27, bf16[640,256]{1,0:T(8,128)(2,1)} %copy-done.35, bf16[512,1280]{1,0:T(8,128)(2,1)} %copy-done.26, bf16[512,640]{1,0:T(8,128)(2,1)} %copy-done.34, bf16[3,512,1280]{2,1,0:T(8,128)(2,1)} %copy-done.8, ...), custom_call_target="tpu_custom_call" | custom-call | bytes 1048576 | tf_op jit(solution)/shard_map/features_grad/pallas_call | solution.py:655
  567.2 14.8 %collective-permute-start.60 = (bf16[320,256]{1,0:T(8,128)(2,1)S(1)}, bf16[320,256]{1,0:T(8,128)(2,1)}, u32[]{:S(2)}, u32[]{:S(2)}) collective-permute-start(bf16[320,256]{1,0:T(8,128)(2,1)S(1)} %get-tuple-element.500), channel_id=1, source_target_pairs={{0,1},{1,2},{2,3},{3,0},{4,5},{5,6},{6,7},{7,4},{8,9},{9,10},{10,1... | collective-permute-start | bytes 491528 | tf_op jit(solution)/shard_map/ppermute | solution.py:104
  585.5 7.9 %qkv_grad.1 = (bf16[256,1920]{1,0:T(8,128)(2,1)}, f32[256,1920]{1,0:T(8,128)}) custom-call(s32[1]{0:T(128)} %bitcast.66.info_ref, bf16[256,512]{1,0:T(8,128)(2,1)} %get-tuple-element.418.refs_0_, bf16[256,512]{1,0:T(8,128)(2,1)} %copy-done.65, bf16[256,512]{1,0:T(8,128)(2,1)} %copy-done.66, bf16[256,512]{1,0:T(8,128)(2,1)} %copy-done.67, ...), custom_call_target="tpu_custom_call" | custom-call | bytes 1048576 | tf_op jit(solution)/shard_map/qkv_grad/pallas_call | solution.py:614
  639.0 16.9 %widen.1 = (f32[1280,2048]{1,0:T(8,128)}, f32[1280,2,2048]{2,1,0:T(2,128)}) custom-call(bf16[3840,2048]{1,0:T(8,128)(2,1)} %all-gather.2.cloned.1.call-done.down_ref.gate_ref.up_ref, bf16[3840,2048]{1,0:T(8,128)(2,1)} %all-gather.2.cloned.1.call-done.down_ref.gate_ref.up_ref, bf16[3840,2048]{1,0:T(8,128)(2,1)} %all-gather.2.cloned.1.call-done.down_ref.gate_ref.up_ref), custom_call_target="tpu_custom_call" | custom-call | bytes 1048576 | tf_op jit(solution)/shard_map/widen/pallas_call | solution.py:570
  (457 shorter events, 300.9 us)
Async XLA Ops:
  7.2 459.9 %reduce-scatter.2.cloned.1.call-start = ((), (), s32[]{:S(2)}) async-start(), calls=%async_computation.1 | async-start | bytes 17694720 | tf_op jit(solution)/shard_map/reduce_scatter | solution.py:808
  54.9 32.7 %collective-permute-start.13 = (bf16[3,64,1280]{2,1,0:T(8,128)(2,1)S(1)}, bf16[3,64,1280]{2,1,0:T(8,128)(2,1)S(1)}, u32[]{:S(2)}, u32[]{:S(2)}) collective-permute-start(bf16[3,64,1280]{2,1,0:T(8,128)(2,1)S(1)} %pad_maximum_fusion.4), channel_id=1, source_target_pairs={{0,8},{4,12},{8,0},{12,4},{16,24},{20,28},{24,16},{28,20},{1,9},{5... | collective-permute-start | bytes 1474568 | tf_op jit(solution)/shard_map/ppermute | solution.py:67
  90.4 39.9 %collective-permute-start.20 = (bf16[256,2048]{1,0:T(8,128)(2,1)S(1)}, bf16[256,2048]{1,0:T(8,128)(2,1)}, u32[]{:S(2)}, u32[]{:S(2)}) collective-permute-start(bf16[256,2048]{1,0:T(8,128)(2,1)S(1)} %bitcast.167), channel_id=1, source_target_pairs={{0,1},{1,0},{2,3},{3,2},{4,5},{5,4},{6,7},{7,6},{8,9},{9,8},{10,11... | collective-permute-start | bytes 3145736 | tf_op jit(solution)/shard_map/ppermute | solution.py:104
  90.4 39.9 %collective-permute-start.21 = (bf16[256,2048]{1,0:T(8,128)(2,1)S(1)}, bf16[256,2048]{1,0:T(8,128)(2,1)}, u32[]{:S(2)}, u32[]{:S(2)}) collective-permute-start(bf16[256,2048]{1,0:T(8,128)(2,1)S(1)} %bitcast.168), channel_id=1, source_target_pairs={{1,2},{2,1},{5,6},{6,5},{9,10},{10,9},{13,14},{14,13},{17,18},{18,... | collective-permute-start | bytes 3145736 | tf_op jit(solution)/shard_map/ppermute | solution.py:104
  94.4 35.8 %collective-permute-start.18 = (bf16[40,2048]{1,0:T(8,128)(2,1)S(1)}, bf16[40,2048]{1,0:T(8,128)(2,1)S(1)}, u32[]{:S(2)}, u32[]{:S(2)}) collective-permute-start(bf16[40,2048]{1,0:T(8,128)(2,1)S(1)} %constant_dynamic-slice_fusion.1), channel_id=1, source_target_pairs={{0,2},{1,3},{2,0},{3,1},{4,6},{5,7},{6,4},{7,5},{8,10},{9,11},{10,... | collective-permute-start | bytes 491528 | tf_op jit(solution)/shard_map/ppermute | solution.py:104
  95.9 34.3 %collective-permute-start.19 = (bf16[40,2048]{1,0:T(8,128)(2,1)S(1)}, bf16[40,2048]{1,0:T(8,128)(2,1)S(1)}, u32[]{:S(2)}, u32[]{:S(2)}) collective-permute-start(bf16[40,2048]{1,0:T(8,128)(2,1)S(1)} %constant_dynamic-slice_fusion.1), channel_id=1, source_target_pairs={{0,3},{1,0},{2,1},{3,2},{4,7},{5,4},{6,5},{7,6},{8,11},{9,8},{10,9... | collective-permute-start | bytes 491528 | tf_op jit(solution)/shard_map/ppermute | solution.py:104
  165.4 34.9 %collective-permute-start.30 = (bf16[256,2048]{1,0:T(8,128)(2,1)}, bf16[256,2048]{1,0:T(8,128)(2,1)S(1)}, u32[]{:S(2)}, u32[]{:S(2)}) collective-permute-start(bf16[256,2048]{1,0:T(8,128)(2,1)} %collective-permute-done.25), channel_id=1, source_target_pairs={{1,0},{2,3},{5,4},{6,7},{9,8},{10,11},{13,12},{14,15},{17,16},{18,... | collective-permute-start | bytes 3145736 | tf_op jit(solution)/shard_map/ppermute | solution.py:104
  179.7 35.9 %collective-permute-start.28 = (bf16[256,2048]{1,0:T(8,128)(2,1)S(1)}, bf16[256,2048]{1,0:T(8,128)(2,1)}, u32[]{:S(2)}, u32[]{:S(2)}) collective-permute-start(bf16[256,2048]{1,0:T(8,128)(2,1)S(1)} %multiply_convert_fusion.hn_ref.refs_8_), channel_id=1, source_target_pairs={{0,1},{1,0},{2,3},{3,2},{4,5},{5,4},{6,7},{7,6},{8,9},{9,8},{10,11... | collective-permute-start | bytes 3145736 | tf_op jit(solution)/shard_map/ppermute | solution.py:104
  182.2 33.5 %collective-permute-start.29 = (bf16[256,2048]{1,0:T(8,128)(2,1)S(1)}, bf16[256,2048]{1,0:T(8,128)(2,1)}, u32[]{:S(2)}, u32[]{:S(2)}) collective-permute-start(bf16[256,2048]{1,0:T(8,128)(2,1)S(1)} %multiply_convert_fusion.hn_ref.refs_8_), channel_id=1, source_target_pairs={{1,2},{2,1},{5,6},{6,5},{9,10},{10,9},{13,14},{14,13},{17,18},{18,... | collective-permute-start | bytes 3145736 | tf_op jit(solution)/shard_map/ppermute | solution.py:104
  294.0 33.6 %collective-permute-start.36 = (bf16[256,2048]{1,0:T(8,128)(2,1)}, bf16[256,2048]{1,0:T(8,128)(2,1)S(1)}, u32[]{:S(2)}, u32[]{:S(2)}) collective-permute-start(bf16[256,2048]{1,0:T(8,128)(2,1)} %add_convert_fusion.6), channel_id=1, source_target_pairs={{1,2},{2,1},{5,6},{6,5},{9,10},{10,9},{13,14},{14,13},{17,18},{18,... | collective-permute-start | bytes 3145736 | tf_op jit(solution)/shard_map/ppermute | solution.py:104
  294.7 32.9 %collective-permute-start.35 = (bf16[256,2048]{1,0:T(8,128)(2,1)}, bf16[256,2048]{1,0:T(8,128)(2,1)}, u32[]{:S(2)}, u32[]{:S(2)}) collective-permute-start(bf16[256,2048]{1,0:T(8,128)(2,1)} %get-tuple-element.378), channel_id=1, source_target_pairs={{0,1},{3,2},{4,5},{7,6},{8,9},{11,10},{12,13},{15,14},{16,17},{19,... | collective-permute-start | bytes 3145736 | tf_op jit(solution)/shard_map/ppermute | solution.py:104
  327.7 298.0 %all-gather.2.cloned.1.call-start = ((), (), s32[]{:S(2)}) async-start(), calls=%async_computation.2 | async-start | bytes 17694720 | tf_op jit(solution)/shard_map/all_gather | solution.py:850
  353.5 34.9 %collective-permute-start.39 = (bf16[256,2048]{1,0:T(8,128)(2,1)}, bf16[256,2048]{1,0:T(8,128)(2,1)}, u32[]{:S(2)}, u32[]{:S(2)}) collective-permute-start(bf16[256,2048]{1,0:T(8,128)(2,1)} %add_convert_fusion.4), channel_id=1, source_target_pairs={{0,1},{1,0},{2,3},{3,2},{4,5},{5,4},{6,7},{7,6},{8,9},{9,8},{10,11... | collective-permute-start | bytes 3145736 | tf_op jit(solution)/shard_map/ppermute | solution.py:104
  359.6 44.0 %collective-permute-start.41 = (bf16[256,512]{1,0:T(8,128)(2,1)}, bf16[256,512]{1,0:T(8,128)(2,1)S(1)}, u32[]{:S(2)}, u32[]{:S(2)}) collective-permute-start(bf16[256,512]{1,0:T(8,128)(2,1)} %copy-done.41), channel_id=1, source_target_pairs={{0,1},{1,2},{2,3},{3,0},{4,5},{5,6},{6,7},{7,4},{8,9},{9,10},{10,1... | collective-permute-start | bytes 786440 | tf_op jit(solution)/shard_map/ppermute | solution.py:104
  359.7 44.0 %collective-permute-start.42 = (bf16[256,512]{1,0:T(8,128)(2,1)}, bf16[256,512]{1,0:T(8,128)(2,1)S(1)}, u32[]{:S(2)}, u32[]{:S(2)}) collective-permute-start(bf16[256,512]{1,0:T(8,128)(2,1)} %copy-done.43), channel_id=1, source_target_pairs={{0,2},{1,3},{2,0},{3,1},{4,6},{5,7},{6,4},{7,5},{8,10},{9,11},{10,... | collective-permute-start | bytes 786440 | tf_op jit(solution)/shard_map/ppermute | solution.py:104
  362.8 40.8 %collective-permute-start.43 = (bf16[256,512]{1,0:T(8,128)(2,1)S(1)}, bf16[256,512]{1,0:T(8,128)(2,1)S(1)}, u32[]{:S(2)}, u32[]{:S(2)}) collective-permute-start(bf16[256,512]{1,0:T(8,128)(2,1)S(1)} %copy-done.40), channel_id=1, source_target_pairs={{0,3},{1,0},{2,1},{3,2},{4,7},{5,4},{6,5},{7,6},{8,11},{9,8},{10,9... | collective-permute-start | bytes 786440 | tf_op jit(solution)/shard_map/ppermute | solution.py:104
  477.2 33.8 %collective-permute-start.53 = (bf16[4,320,256]{2,1,0:T(8,128)(2,1)}, bf16[4,320,256]{2,1,0:T(8,128)(2,1)}, u32[]{:S(2)}, u32[]{:S(2)}) collective-permute-start(bf16[4,320,256]{2,1,0:T(8,128)(2,1)} %get-tuple-element.489), channel_id=1, source_target_pairs={{0,16},{4,20},{8,24},{12,28},{16,0},{20,4},{24,8},{28,12},{1,17},{... | collective-permute-start | bytes 1966088 | tf_op jit(solution)/shard_map/ppermute | solution.py:67
  478.8 49.2 %collective-permute-start.54 = (bf16[4,320,256]{2,1,0:T(8,128)(2,1)}, bf16[4,320,256]{2,1,0:T(8,128)(2,1)}, u32[]{:S(2)}, u32[]{:S(2)}) collective-permute-start(bf16[4,320,256]{2,1,0:T(8,128)(2,1)} %get-tuple-element.488), channel_id=1, source_target_pairs={{0,24},{4,28},{8,16},{12,20},{16,8},{20,12},{24,0},{28,4},{1,25},{... | collective-permute-start | bytes 1966088 | tf_op jit(solution)/shard_map/ppermute | solution.py:67
  481.6 46.4 %collective-permute-start.49 = (bf16[1280,256]{1,0:T(8,128)(2,1)S(1)}, bf16[1280,256]{1,0:T(8,128)(2,1)S(1)}, u32[]{:S(2)}, u32[]{:S(2)}) collective-permute-start(bf16[1280,256]{1,0:T(8,128)(2,1)S(1)} %get-tuple-element.422.dq_ref.refs_4_), channel_id=1, source_target_pairs={{0,1},{1,2},{2,3},{3,0},{4,5},{5,6},{6,7},{7,4},{8,9},{9,10},{10,1... | collective-permute-start | bytes 1966088 | tf_op jit(solution)/shard_map/ppermute | solution.py:104
  481.8 46.2 %collective-permute-start.50 = (bf16[1280,256]{1,0:T(8,128)(2,1)S(1)}, bf16[1280,256]{1,0:T(8,128)(2,1)}, u32[]{:S(2)}, u32[]{:S(2)}) collective-permute-start(bf16[1280,256]{1,0:T(8,128)(2,1)S(1)} %get-tuple-element.422.dq_ref.refs_4_), channel_id=1, source_target_pairs={{0,2},{1,3},{2,0},{3,1},{4,6},{5,7},{6,4},{7,5},{8,10},{9,11},{10,... | collective-permute-start | bytes 1966088 | tf_op jit(solution)/shard_map/ppermute | solution.py:104
  533.4 52.1 %collective-permute-start.55 = (bf16[640,256]{1,0:T(8,128)(2,1)S(1)}, bf16[640,256]{1,0:T(8,128)(2,1)}, u32[]{:S(2)}, u32[]{:S(2)}) collective-permute-start(bf16[640,256]{1,0:T(8,128)(2,1)S(1)} %pad_maximum_fusion.11.dkv_ref.refs_8_), channel_id=1, source_target_pairs={{0,1},{1,2},{2,3},{3,0},{4,5},{5,6},{6,7},{7,4},{8,9},{9,10},{10,1... | collective-permute-start | bytes 983048 | tf_op jit(solution)/shard_map/ppermute | solution.py:104
  541.4 44.1 %collective-permute-start.56 = (bf16[640,256]{1,0:T(8,128)(2,1)S(1)}, bf16[640,256]{1,0:T(8,128)(2,1)}, u32[]{:S(2)}, u32[]{:S(2)}) collective-permute-start(bf16[640,256]{1,0:T(8,128)(2,1)S(1)} %pad_maximum_fusion.11.dkv_ref.refs_8_), channel_id=1, source_target_pairs={{0,2},{1,3},{2,0},{3,1},{4,6},{5,7},{6,4},{7,5},{8,10},{9,11},{10,... | collective-permute-start | bytes 983048 | tf_op jit(solution)/shard_map/ppermute | solution.py:104
  543.5 42.0 %collective-permute-start.57 = (bf16[640,256]{1,0:T(8,128)(2,1)S(1)}, bf16[640,256]{1,0:T(8,128)(2,1)}, u32[]{:S(2)}, u32[]{:S(2)}) collective-permute-start(bf16[640,256]{1,0:T(8,128)(2,1)S(1)} %pad_maximum_fusion.11.dkv_ref.refs_8_), channel_id=1, source_target_pairs={{0,3},{1,0},{2,1},{3,2},{4,7},{5,4},{6,5},{7,6},{8,11},{9,8},{10,9... | collective-permute-start | bytes 983048 | tf_op jit(solution)/shard_map/ppermute | solution.py:104
  548.7 35.9 %collective-permute-start.59 = (bf16[320,256]{1,0:T(8,128)(2,1)}, bf16[320,256]{1,0:T(8,128)(2,1)}, u32[]{:S(2)}, u32[]{:S(2)}) collective-permute-start(bf16[320,256]{1,0:T(8,128)(2,1)} %get-tuple-element.501), channel_id=1, source_target_pairs={{0,2},{1,3},{2,0},{3,1},{4,6},{5,7},{6,4},{7,5},{8,10},{9,11},{10,... | collective-permute-start | bytes 491528 | tf_op jit(solution)/shard_map/ppermute | solution.py:104
  (141 other events, 1984.1 us)
Sparse Core Ops, SparseCore 0:
  327.8 107.5 reduce-scatter.1
  467.3 112.1 all-gather.1

commit v4 on v3

--- a/solution.py
+++ b/solution.py
@@ -812,7 +812,7 @@
     hold(dhn_c, out_c)
     dhn_c.hop("edge")
     out_c.hop("next_mid")
-    hold(dhn_c, out_c)
+    xn = hold_with(xn, dhn_c, out_c)
 
     dhn = dhn_c.result()
     d_ffn_gain = jnp.sum(dhn * normed_two, axis=0)

time: 686 us -> 680 us (level)
  transfers between devices with their start and end apart: 82 -> 82, of which waited for: 35 -> 36; matrix products, arithmetic and copies ran while one was open for 12% -> 12% of each run, Pallas kernels for 26% -> 26%
where the time goes in v4:
time: 680 us; the launch traced here: 671 us
  waiting for transfers between devices  218 us (32%)
  Pallas kernels  174 us (26%)
  starting transfers between devices  142 us (21%)
  other arithmetic  83.2 us (12%)
  local copies, waits for them, and re-layouts  20.8 us (3%)
  between operations  16.8 us (2%)
  matrix products  16.2 us (2%)
    ppermute x49, waiting for transfers between devices, move(): return lax.ppermute(x, 'grp', pairs)  150 us
    ppermute x49, starting transfers between devices, move(): return lax.ppermute(x, 'grp', pairs)  115 us
    pallas_call x4, Pallas kernels, ffn_slot(): pl.pallas_call(ffn_kernel, in_specs=[whole, whole, far, far, far], out_sp...  62.4 us
    ppermute x21, waiting for transfers between devices, swap_rest(): return lax.ppermute(x, 'rep', [(i, i ^ 2 * j) for i in range(n)])  61.5 us
    ppermute x21, starting transfers between devices, swap_rest(): return lax.ppermute(x, 'rep', [(i, i ^ 2 * j) for i in range(n)])  25.2 us
    pallas_call x1, Pallas kernels, attention_backward(): pl.pallas_call(backward_kernel, grid_spec=pltpu.PrefetchScalarGridSpec(nu...  24.9 us
    pallas_call x1, Pallas kernels, weight_grads(): pl.pallas_call(functools.partial(grad_kernel, slots), grid=(3, 2), in_spe...  23 us
    select_n x17, other arithmetic, join_pair(): jnp.where(bit_of(b) == 0, jnp.concatenate([mine, other], axis), jnp.conca...  23 us
  transfers between devices with their start and end apart: 82, of which 36 were waited for; matrix products, arithmetic and copies ran while one was open for 12% of the time, Pallas kernels for 26%

profile of v4, /device:TPU:0, one launch (start us, length us, event | category | flops | bytes accessed | tf_op | source)
XLA Modules:
  0.0 671.1 jit_solution(4901720071209186804)
XLA Ops:
  30.8 7.2 %collective-permute-done.7 = bf16[64,1280]{1,0:T(8,128)(2,1)} collective-permute-done((bf16[64,1280]{1,0:T(8,128)(2,1)}, bf16[64,1280]{1,0:T(8,128)(2,1)}, u32[]{:S(2)}, u32[]{:S(2)}) %collective-permute-start.7) | collective-permute-done | bytes 163872 | tf_op jit(solution)/shard_map/ppermute | solution.py:104
  65.8 20.4 %split_gate_up.1 = (bf16[1280,2048]{1,0:T(8,128)(2,1)}, bf16[1280,2048]{1,0:T(8,128)(2,1)}) custom-call(bf16[40960,128]{1,0:T(8,128)(2,1)} %bitcast.158), custom_call_target="tpu_custom_call" | custom-call | bytes 1048576 | tf_op jit(solution)/shard_map/split_gate_up/pallas_call | solution.py:451
  107.8 10.4 %collective-permute-done.17 = bf16[40,2048]{1,0:T(8,128)(2,1)S(1)} collective-permute-done((bf16[40,2048]{1,0:T(8,128)(2,1)S(1)}, bf16[40,2048]{1,0:T(8,128)(2,1)S(1)}, u32[]{:S(2)}, u32[]{:S(2)}) %collective-permute-start.17) | collective-permute-done | bytes 163872 | tf_op jit(solution)/shard_map/ppermute | solution.py:104
  118.3 10.8 %collective-permute-done.18 = bf16[40,2048]{1,0:T(8,128)(2,1)S(1)} collective-permute-done((bf16[40,2048]{1,0:T(8,128)(2,1)S(1)}, bf16[40,2048]{1,0:T(8,128)(2,1)S(1)}, u32[]{:S(2)}, u32[]{:S(2)}) %collective-permute-start.18) | collective-permute-done | bytes 163872 | tf_op jit(solution)/shard_map/ppermute | solution.py:104
  139.1 10.2 %attention_forward.1 = (bf16[1280,256]{1,0:T(8,128)(2,1)S(1)}, f32[1280,256]{1,0:T(8,128)S(1)}, f32[5,4,256]{2,1,0:T(4,128)S(1)}) custom-call(s32[6]{0:T(128)S(1)} %stack.101.info_ref, bf16[1280,256]{1,0:T(8,128)(2,1)S(1)} %bitcast.151, bf16[4,640,256]{2,1,0:T(8,128)(2,1)S(1)} %pad_maximum_fusion.k_ref.v_ref, ...), custom_call_target="tpu_custom_call" | custom-call | bytes 1048576 | tf_op jit(solution)/shard_map/attention_forward/pallas_call | solution.py:390
  182.9 16.0 %ffn_slot.4 = (bf16[3,1280,256]{2,1,0:T(8,128)(2,1)}, f32[256,2048]{1,0:T(8,128)}, f32[256,2048]{1,0:T(8,128)}) custom-call(bf16[256,2048]{1,0:T(8,128)(2,1)} %copy-done.21, bf16[256,2048]{1,0:T(8,128)(2,1)} %bitcast.161, bf16[1280,2048]{1,0:T(8,128)(2,1)} %get-tuple-element.311.g_hbm, bf16[1280,2048]{1,0:T(8,128)(2,1)} %get-tuple-element.312.u_hbm, ...), custom_call_target="tpu_custom_call" | custom-call | bytes 1048576 | tf_op jit(solution)/shard_map/ffn_slot/pallas_call | solution.py:507
  199.0 15.5 %collective-permute-done.28.hn_ref.refs_9_ = bf16[256,2048]{1,0:T(8,128)(2,1)} collective-permute-done((bf16[256,2048]{1,0:T(8,128)(2,1)S(1)}, bf16[256,2048]{1,0:T(8,128)(2,1)}, u32[]{:S(2)}, u32[]{:S(2)}) %collective-permute-start.28) | collective-permute-done | bytes 1048608 | tf_op jit(solution)/shard_map/ppermute | solution.py:104
  217.7 15.4 %ffn_slot.5 = (bf16[3,1280,256]{2,1,0:T(8,128)(2,1)}, bf16[256,2048]{1,0:T(8,128)(2,1)}, bf16[256,2048]{1,0:T(8,128)(2,1)}) custom-call(bf16[256,2048]{1,0:T(8,128)(2,1)} %collective-permute-done.28.hn_ref.refs_9_, bf16[256,2048]{1,0:T(8,128)(2,1)} %collective-permute-done.20.dy_ref.refs_5_, bf16[1280,2048]{1,0:T(8,128)(2,1)} %get-tuple-element.311.g_hbm, ...), custom_call_target="tpu_custom_call" | custom-call | bytes 1048576 | tf_op jit(solution)/shard_map/ffn_slot/pallas_call | solution.py:507
  233.1 10.0 %collective-permute-done.32 = bf16[256,2048]{1,0:T(8,128)(2,1)S(1)} collective-permute-done((bf16[256,2048]{1,0:T(8,128)(2,1)}, bf16[256,2048]{1,0:T(8,128)(2,1)S(1)}, u32[]{:S(2)}, u32[]{:S(2)}) %collective-permute-start.32) | collective-permute-done | bytes 1048608 | tf_op jit(solution)/shard_map/ppermute | solution.py:104
  248.0 15.5 %ffn_slot.6 = (bf16[3,1280,256]{2,1,0:T(8,128)(2,1)}, bf16[256,2048]{1,0:T(8,128)(2,1)}, bf16[256,2048]{1,0:T(8,128)(2,1)}) custom-call(bf16[256,2048]{1,0:T(8,128)(2,1)} %broadcast_select_fusion.4.hn_ref, bf16[256,2048]{1,0:T(8,128)(2,1)} %broadcast_select_fusion.3.dy_ref.refs_6_, bf16[1280,2048]{1,0:T(8,128)(2,1)} %get-tuple-element.311.g_hbm, ...), custom_call_target="tpu_custom_call" | custom-call | bytes 1048576 | tf_op jit(solution)/shard_map/ffn_slot/pallas_call | solution.py:507
  273.3 15.5 %ffn_slot.7 = (bf16[3,1280,256]{2,1,0:T(8,128)(2,1)}, bf16[256,2048]{1,0:T(8,128)(2,1)}, bf16[256,2048]{1,0:T(8,128)(2,1)}) custom-call(bf16[256,2048]{1,0:T(8,128)(2,1)} %broadcast_select_fusion.2.hn_ref.refs_11_, bf16[256,2048]{1,0:T(8,128)(2,1)} %broadcast_select_fusion.1.dy_ref.refs_7_, bf16[1280,2048]{1,0:T(8,128)(2,1)} %get-tuple-element.311.g_hbm, ...), custom_call_target="tpu_custom_call" | custom-call | bytes 1048576 | tf_op jit(solution)/shard_map/ffn_slot/pallas_call | solution.py:507
  293.5 8.8 %collective-permute-start.35 = (bf16[256,2048]{1,0:T(8,128)(2,1)}, bf16[256,2048]{1,0:T(8,128)(2,1)}, u32[]{:S(2)}, u32[]{:S(2)}) collective-permute-start(bf16[256,2048]{1,0:T(8,128)(2,1)} %get-tuple-element.379), channel_id=1, source_target_pairs={{0,1},{3,2},{4,5},{7,6},{8,9},{11,10},{12,13},{15,14},{16,17},{19,... | collective-permute-start | bytes 3145736 | tf_op jit(solution)/shard_map/ppermute | solution.py:104
  303.4 23.0 %weight_grads.1 = bf16[3840,2048]{1,0:T(8,128)(2,1)} custom-call(bf16[3,1280,256]{2,1,0:T(8,128)(2,1)} %get-tuple-element.369.refs_0_, bf16[3,1280,256]{2,1,0:T(8,128)(2,1)} %get-tuple-element.370.refs_1_, bf16[3,1280,256]{2,1,0:T(8,128)(2,1)} %get-tuple-element.371.refs_2_, bf16[3,1280,256]{2,1,0:T(8,128)(2,1)} %get-tuple-element.372.refs_3_, ...), custom_call_target="tpu_custom_call" | custom-call | bytes 1048576 | tf_op jit(solution)/shard_map/weight_grads/pallas_call | solution.py:548
  332.3 16.4 %collective-permute-done.38 = bf16[256,2048]{1,0:T(8,128)(2,1)S(1)} collective-permute-done((bf16[256,2048]{1,0:T(8,128)(2,1)}, bf16[256,2048]{1,0:T(8,128)(2,1)S(1)}, u32[]{:S(2)}, u32[]{:S(2)}) %collective-permute-start.38) | collective-permute-done | bytes 1048608 | tf_op jit(solution)/shard_map/ppermute | solution.py:104
  359.3 20.2 %collective-permute-done.39 = bf16[256,2048]{1,0:T(8,128)(2,1)} collective-permute-done((bf16[256,2048]{1,0:T(8,128)(2,1)}, bf16[256,2048]{1,0:T(8,128)(2,1)}, u32[]{:S(2)}, u32[]{:S(2)}) %collective-permute-start.39) | collective-permute-done | bytes 1048608 | tf_op jit(solution)/shard_map/ppermute | solution.py:104
  404.8 24.9 %attention_backward.1 = (f32[1280,256]{1,0:T(8,128)S(1)}, f32[4,320,256]{2,1,0:T(8,128)S(1)}, f32[4,320,256]{2,1,0:T(8,128)S(1)}) custom-call(s32[6]{0:T(128)S(1)} %stack.101.info_ref, bf16[1280,256]{1,0:T(8,128)(2,1)S(1)} %bitcast.152, bf16[4,640,256]{2,1,0:T(8,128)(2,1)} %copy-done.1, bf16[4,640,256]{2,1,0:T(8,128)(2,1)} %copy-done.1, ...), custom_call_target="tpu_custom_call" | custom-call | bytes 1048576 | tf_op jit(solution)/shard_map/attention_backward/pallas_call | solution.py:412
  440.6 19.6 %collective-permute-done.47 = bf16[640,256]{1,0:T(8,128)(2,1)S(1)} collective-permute-done((bf16[640,256]{1,0:T(8,128)(2,1)S(1)}, bf16[640,256]{1,0:T(8,128)(2,1)S(1)}, u32[]{:S(2)}, u32[]{:S(2)}) %collective-permute-start.47) | collective-permute-done | bytes 327712 | tf_op jit(solution)/shard_map/ppermute | solution.py:104
  477.3 22.7 %collective-permute-done.52 = bf16[4,320,256]{2,1,0:T(8,128)(2,1)S(1)} collective-permute-done((bf16[4,320,256]{2,1,0:T(8,128)(2,1)}, bf16[4,320,256]{2,1,0:T(8,128)(2,1)S(1)}, u32[]{:S(2)}, u32[]{:S(2)}) %collective-permute-start.52) | collective-permute-done | bytes 655392 | tf_op jit(solution)/shard_map/ppermute | solution.py:67
  504.8 16.3 %collective-permute-done.54 = bf16[4,320,256]{2,1,0:T(8,128)(2,1)} collective-permute-done((bf16[4,320,256]{2,1,0:T(8,128)(2,1)}, bf16[4,320,256]{2,1,0:T(8,128)(2,1)}, u32[]{:S(2)}, u32[]{:S(2)}) %collective-permute-start.54) | collective-permute-done | bytes 655392 | tf_op jit(solution)/shard_map/ppermute | solution.py:67
  525.6 9.3 %collective-permute-start.55 = (bf16[640,256]{1,0:T(8,128)(2,1)S(1)}, bf16[640,256]{1,0:T(8,128)(2,1)}, u32[]{:S(2)}, u32[]{:S(2)}) collective-permute-start(bf16[640,256]{1,0:T(8,128)(2,1)S(1)} %pad_maximum_fusion.11.dkv_ref.refs_8_), channel_id=1, source_target_pairs={{0,1},{1,2},{2,3},{3,0},{4,5},{5,6},{6,7},{7,4},{8,9},{9,10},{10,1... | collective-permute-start | bytes 983048 | tf_op jit(solution)/shard_map/ppermute | solution.py:104
  543.5 8.2 %features_grad.1 = f32[256,2048]{1,0:T(8,128)} custom-call(s32[4]{0:T(128)} %pad_add_fusion.info_ref, bf16[1280,256]{1,0:T(8,128)(2,1)} %copy-done.27, bf16[640,256]{1,0:T(8,128)(2,1)} %copy-done.37, bf16[512,1280]{1,0:T(8,128)(2,1)} %copy-done.26, bf16[512,640]{1,0:T(8,128)(2,1)} %copy-done.36, bf16[3,512,1280]{2,1,0:T(8,128)(2,1)} %copy-done.8, ...), custom_call_target="tpu_custom_call" | custom-call | bytes 1048576 | tf_op jit(solution)/shard_map/features_grad/pallas_call | solution.py:655
  560.6 15.0 %collective-permute-start.60 = (bf16[320,256]{1,0:T(8,128)(2,1)S(1)}, bf16[320,256]{1,0:T(8,128)(2,1)}, u32[]{:S(2)}, u32[]{:S(2)}) collective-permute-start(bf16[320,256]{1,0:T(8,128)(2,1)S(1)} %get-tuple-element.502), channel_id=1, source_target_pairs={{0,1},{1,2},{2,3},{3,0},{4,5},{5,6},{6,7},{7,4},{8,9},{9,10},{10,1... | collective-permute-start | bytes 491528 | tf_op jit(solution)/shard_map/ppermute | solution.py:104
  579.1 7.9 %qkv_grad.1 = (bf16[256,1920]{1,0:T(8,128)(2,1)}, f32[256,1920]{1,0:T(8,128)}) custom-call(s32[1]{0:T(128)} %bitcast.66.info_ref, bf16[256,512]{1,0:T(8,128)(2,1)} %get-tuple-element.420.refs_0_, bf16[256,512]{1,0:T(8,128)(2,1)} %copy-done.62, bf16[256,512]{1,0:T(8,128)(2,1)} %copy-done.63, bf16[256,512]{1,0:T(8,128)(2,1)} %collective-permute-done.43.refs_3_, ...), custom_call_target="tpu_custom_call" | custom-call | bytes 1048576 | tf_op jit(solution)/shard_map/qkv_grad/pallas_call | solution.py:614
  632.6 16.9 %widen.1 = (f32[1280,2048]{1,0:T(8,128)}, f32[1280,2,2048]{2,1,0:T(2,128)}) custom-call(bf16[3840,2048]{1,0:T(8,128)(2,1)} %all-gather.2.cloned.1.call-done.down_ref.gate_ref.up_ref, bf16[3840,2048]{1,0:T(8,128)(2,1)} %all-gather.2.cloned.1.call-done.down_ref.gate_ref.up_ref, bf16[3840,2048]{1,0:T(8,128)(2,1)} %all-gather.2.cloned.1.call-done.down_ref.gate_ref.up_ref), custom_call_target="tpu_custom_call" | custom-call | bytes 1048576 | tf_op jit(solution)/shard_map/widen/pallas_call | solution.py:570
  (451 shorter events, 297.9 us)
Async XLA Ops:
  7.2 453.1 %reduce-scatter.2.cloned.1.call-start = ((), (), s32[]{:S(2)}) async-start(), calls=%async_computation.1 | async-start | bytes 17694720 | tf_op jit(solution)/shard_map/reduce_scatter | solution.py:808
  54.2 32.0 %collective-permute-start.13 = (bf16[3,64,1280]{2,1,0:T(8,128)(2,1)S(1)}, bf16[3,64,1280]{2,1,0:T(8,128)(2,1)S(1)}, u32[]{:S(2)}, u32[]{:S(2)}) collective-permute-start(bf16[3,64,1280]{2,1,0:T(8,128)(2,1)S(1)} %pad_maximum_fusion.4), channel_id=1, source_target_pairs={{0,8},{4,12},{8,0},{12,4},{16,24},{20,28},{24,16},{28,20},{1,9},{5... | collective-permute-start | bytes 1474568 | tf_op jit(solution)/shard_map/ppermute | solution.py:67
  55.7 30.6 %collective-permute-start.14 = (bf16[3,64,1280]{2,1,0:T(8,128)(2,1)S(1)}, bf16[3,64,1280]{2,1,0:T(8,128)(2,1)S(1)}, u32[]{:S(2)}, u32[]{:S(2)}) collective-permute-start(bf16[3,64,1280]{2,1,0:T(8,128)(2,1)S(1)} %pad_maximum_fusion.4), channel_id=1, source_target_pairs={{0,16},{4,20},{8,24},{12,28},{16,0},{20,4},{24,8},{28,12},{1,17},{... | collective-permute-start | bytes 1474568 | tf_op jit(solution)/shard_map/ppermute | solution.py:67
  89.0 40.1 %collective-permute-start.20 = (bf16[256,2048]{1,0:T(8,128)(2,1)}, bf16[256,2048]{1,0:T(8,128)(2,1)}, u32[]{:S(2)}, u32[]{:S(2)}) collective-permute-start(bf16[256,2048]{1,0:T(8,128)(2,1)} %bitcast.159), channel_id=1, source_target_pairs={{0,1},{1,0},{2,3},{3,2},{4,5},{5,4},{6,7},{7,6},{8,9},{9,8},{10,11... | collective-permute-start | bytes 3145736 | tf_op jit(solution)/shard_map/ppermute | solution.py:104
  89.0 40.1 %collective-permute-start.21 = (bf16[256,2048]{1,0:T(8,128)(2,1)}, bf16[256,2048]{1,0:T(8,128)(2,1)}, u32[]{:S(2)}, u32[]{:S(2)}) collective-permute-start(bf16[256,2048]{1,0:T(8,128)(2,1)} %bitcast.160), channel_id=1, source_target_pairs={{1,2},{2,1},{5,6},{6,5},{9,10},{10,9},{13,14},{14,13},{17,18},{18,... | collective-permute-start | bytes 3145736 | tf_op jit(solution)/shard_map/ppermute | solution.py:104
  93.1 36.0 %collective-permute-start.18 = (bf16[40,2048]{1,0:T(8,128)(2,1)S(1)}, bf16[40,2048]{1,0:T(8,128)(2,1)S(1)}, u32[]{:S(2)}, u32[]{:S(2)}) collective-permute-start(bf16[40,2048]{1,0:T(8,128)(2,1)S(1)} %constant_dynamic-slice_fusion.4), channel_id=1, source_target_pairs={{0,2},{1,3},{2,0},{3,1},{4,6},{5,7},{6,4},{7,5},{8,10},{9,11},{10,... | collective-permute-start | bytes 491528 | tf_op jit(solution)/shard_map/ppermute | solution.py:104
  94.6 34.5 %collective-permute-start.19 = (bf16[40,2048]{1,0:T(8,128)(2,1)S(1)}, bf16[40,2048]{1,0:T(8,128)(2,1)S(1)}, u32[]{:S(2)}, u32[]{:S(2)}) collective-permute-start(bf16[40,2048]{1,0:T(8,128)(2,1)S(1)} %constant_dynamic-slice_fusion.4), channel_id=1, source_target_pairs={{0,3},{1,0},{2,1},{3,2},{4,7},{5,4},{6,5},{7,6},{8,11},{9,8},{10,9... | collective-permute-start | bytes 491528 | tf_op jit(solution)/shard_map/ppermute | solution.py:104
  164.3 34.7 %collective-permute-start.30 = (bf16[256,2048]{1,0:T(8,128)(2,1)}, bf16[256,2048]{1,0:T(8,128)(2,1)S(1)}, u32[]{:S(2)}, u32[]{:S(2)}) collective-permute-start(bf16[256,2048]{1,0:T(8,128)(2,1)} %collective-permute-done.25), channel_id=1, source_target_pairs={{1,0},{2,3},{5,4},{6,7},{9,8},{10,11},{13,12},{14,15},{17,16},{18,... | collective-permute-start | bytes 3145736 | tf_op jit(solution)/shard_map/ppermute | solution.py:104
  178.5 36.1 %collective-permute-start.28 = (bf16[256,2048]{1,0:T(8,128)(2,1)S(1)}, bf16[256,2048]{1,0:T(8,128)(2,1)}, u32[]{:S(2)}, u32[]{:S(2)}) collective-permute-start(bf16[256,2048]{1,0:T(8,128)(2,1)S(1)} %multiply_convert_fusion.hn_ref.refs_8_), channel_id=1, source_target_pairs={{0,1},{1,0},{2,3},{3,2},{4,5},{5,4},{6,7},{7,6},{8,9},{9,8},{10,11... | collective-permute-start | bytes 3145736 | tf_op jit(solution)/shard_map/ppermute | solution.py:104
  180.9 33.6 %collective-permute-start.29 = (bf16[256,2048]{1,0:T(8,128)(2,1)S(1)}, bf16[256,2048]{1,0:T(8,128)(2,1)}, u32[]{:S(2)}, u32[]{:S(2)}) collective-permute-start(bf16[256,2048]{1,0:T(8,128)(2,1)S(1)} %multiply_convert_fusion.hn_ref.refs_8_), channel_id=1, source_target_pairs={{1,2},{2,1},{5,6},{6,5},{9,10},{10,9},{13,14},{14,13},{17,18},{18,... | collective-permute-start | bytes 3145736 | tf_op jit(solution)/shard_map/ppermute | solution.py:104
  292.8 33.6 %collective-permute-start.36 = (bf16[256,2048]{1,0:T(8,128)(2,1)}, bf16[256,2048]{1,0:T(8,128)(2,1)S(1)}, u32[]{:S(2)}, u32[]{:S(2)}) collective-permute-start(bf16[256,2048]{1,0:T(8,128)(2,1)} %add_convert_fusion.6), channel_id=1, source_target_pairs={{1,2},{2,1},{5,6},{6,5},{9,10},{10,9},{13,14},{14,13},{17,18},{18,... | collective-permute-start | bytes 3145736 | tf_op jit(solution)/shard_map/ppermute | solution.py:104
  293.5 32.9 %collective-permute-start.35 = (bf16[256,2048]{1,0:T(8,128)(2,1)}, bf16[256,2048]{1,0:T(8,128)(2,1)}, u32[]{:S(2)}, u32[]{:S(2)}) collective-permute-start(bf16[256,2048]{1,0:T(8,128)(2,1)} %get-tuple-element.379), channel_id=1, source_target_pairs={{0,1},{3,2},{4,5},{7,6},{8,9},{11,10},{12,13},{15,14},{16,17},{19,... | collective-permute-start | bytes 3145736 | tf_op jit(solution)/shard_map/ppermute | solution.py:104
  327.4 291.9 %all-gather.2.cloned.1.call-start = ((), (), s32[]{:S(2)}) async-start(), calls=%async_computation.2 | async-start | bytes 17694720 | tf_op jit(solution)/shard_map/all_gather | solution.py:850
  430.8 29.5 %collective-permute-start.47 = (bf16[640,256]{1,0:T(8,128)(2,1)S(1)}, bf16[640,256]{1,0:T(8,128)(2,1)S(1)}, u32[]{:S(2)}, u32[]{:S(2)}) collective-permute-start(bf16[640,256]{1,0:T(8,128)(2,1)S(1)} %pad_maximum_fusion.8), channel_id=1, source_target_pairs={{0,2},{1,3},{2,0},{3,1},{4,6},{5,7},{6,4},{7,5},{8,10},{9,11},{10,... | collective-permute-start | bytes 983048 | tf_op jit(solution)/shard_map/ppermute | solution.py:104
  468.4 31.7 %collective-permute-start.52 = (bf16[4,320,256]{2,1,0:T(8,128)(2,1)}, bf16[4,320,256]{2,1,0:T(8,128)(2,1)S(1)}, u32[]{:S(2)}, u32[]{:S(2)}) collective-permute-start(bf16[4,320,256]{2,1,0:T(8,128)(2,1)} %get-tuple-element.492), channel_id=1, source_target_pairs={{0,8},{4,12},{8,0},{12,4},{16,24},{20,28},{24,16},{28,20},{1,9},{5... | collective-permute-start | bytes 1966088 | tf_op jit(solution)/shard_map/ppermute | solution.py:67
  470.4 34.5 %collective-permute-start.53 = (bf16[4,320,256]{2,1,0:T(8,128)(2,1)}, bf16[4,320,256]{2,1,0:T(8,128)(2,1)}, u32[]{:S(2)}, u32[]{:S(2)}) collective-permute-start(bf16[4,320,256]{2,1,0:T(8,128)(2,1)} %get-tuple-element.491), channel_id=1, source_target_pairs={{0,16},{4,20},{8,24},{12,28},{16,0},{20,4},{24,8},{28,12},{1,17},{... | collective-permute-start | bytes 1966088 | tf_op jit(solution)/shard_map/ppermute | solution.py:67
  471.9 49.2 %collective-permute-start.54 = (bf16[4,320,256]{2,1,0:T(8,128)(2,1)}, bf16[4,320,256]{2,1,0:T(8,128)(2,1)}, u32[]{:S(2)}, u32[]{:S(2)}) collective-permute-start(bf16[4,320,256]{2,1,0:T(8,128)(2,1)} %get-tuple-element.490), channel_id=1, source_target_pairs={{0,24},{4,28},{8,16},{12,20},{16,8},{20,12},{24,0},{28,4},{1,25},{... | collective-permute-start | bytes 1966088 | tf_op jit(solution)/shard_map/ppermute | solution.py:67
  475.0 46.1 %collective-permute-start.49 = (bf16[1280,256]{1,0:T(8,128)(2,1)S(1)}, bf16[1280,256]{1,0:T(8,128)(2,1)S(1)}, u32[]{:S(2)}, u32[]{:S(2)}) collective-permute-start(bf16[1280,256]{1,0:T(8,128)(2,1)S(1)} %get-tuple-element.424.dq_ref.refs_4_), channel_id=1, source_target_pairs={{0,1},{1,2},{2,3},{3,0},{4,5},{5,6},{6,7},{7,4},{8,9},{9,10},{10,1... | collective-permute-start | bytes 1966088 | tf_op jit(solution)/shard_map/ppermute | solution.py:104
  475.3 45.8 %collective-permute-start.50 = (bf16[1280,256]{1,0:T(8,128)(2,1)S(1)}, bf16[1280,256]{1,0:T(8,128)(2,1)}, u32[]{:S(2)}, u32[]{:S(2)}) collective-permute-start(bf16[1280,256]{1,0:T(8,128)(2,1)S(1)} %get-tuple-element.424.dq_ref.refs_4_), channel_id=1, source_target_pairs={{0,2},{1,3},{2,0},{3,1},{4,6},{5,7},{6,4},{7,5},{8,10},{9,11},{10,... | collective-permute-start | bytes 1966088 | tf_op jit(solution)/shard_map/ppermute | solution.py:104
  525.6 53.5 %collective-permute-start.55 = (bf16[640,256]{1,0:T(8,128)(2,1)S(1)}, bf16[640,256]{1,0:T(8,128)(2,1)}, u32[]{:S(2)}, u32[]{:S(2)}) collective-permute-start(bf16[640,256]{1,0:T(8,128)(2,1)S(1)} %pad_maximum_fusion.11.dkv_ref.refs_8_), channel_id=1, source_target_pairs={{0,1},{1,2},{2,3},{3,0},{4,5},{5,6},{6,7},{7,4},{8,9},{9,10},{10,1... | collective-permute-start | bytes 983048 | tf_op jit(solution)/shard_map/ppermute | solution.py:104
  534.9 44.2 %collective-permute-start.56 = (bf16[640,256]{1,0:T(8,128)(2,1)S(1)}, bf16[640,256]{1,0:T(8,128)(2,1)}, u32[]{:S(2)}, u32[]{:S(2)}) collective-permute-start(bf16[640,256]{1,0:T(8,128)(2,1)S(1)} %pad_maximum_fusion.11.dkv_ref.refs_8_), channel_id=1, source_target_pairs={{0,2},{1,3},{2,0},{3,1},{4,6},{5,7},{6,4},{7,5},{8,10},{9,11},{10,... | collective-permute-start | bytes 983048 | tf_op jit(solution)/shard_map/ppermute | solution.py:104
  537.1 42.0 %collective-permute-start.57 = (bf16[640,256]{1,0:T(8,128)(2,1)S(1)}, bf16[640,256]{1,0:T(8,128)(2,1)}, u32[]{:S(2)}, u32[]{:S(2)}) collective-permute-start(bf16[640,256]{1,0:T(8,128)(2,1)S(1)} %pad_maximum_fusion.11.dkv_ref.refs_8_), channel_id=1, source_target_pairs={{0,3},{1,0},{2,1},{3,2},{4,7},{5,4},{6,5},{7,6},{8,11},{9,8},{10,9... | collective-permute-start | bytes 983048 | tf_op jit(solution)/shard_map/ppermute | solution.py:104
  542.2 36.1 %collective-permute-start.59 = (bf16[320,256]{1,0:T(8,128)(2,1)}, bf16[320,256]{1,0:T(8,128)(2,1)}, u32[]{:S(2)}, u32[]{:S(2)}) collective-permute-start(bf16[320,256]{1,0:T(8,128)(2,1)} %get-tuple-element.503), channel_id=1, source_target_pairs={{0,2},{1,3},{2,0},{3,1},{4,6},{5,7},{6,4},{7,5},{8,10},{9,11},{10,... | collective-permute-start | bytes 491528 | tf_op jit(solution)/shard_map/ppermute | solution.py:104
  622.2 29.4 %collective-permute-start.77 = (bf16[256,2048]{1,0:T(8,128)(2,1)}, bf16[256,2048]{1,0:T(8,128)(2,1)}, u32[]{:S(2)}, u32[]{:S(2)}) collective-permute-start(bf16[256,2048]{1,0:T(8,128)(2,1)} %add_convert_fusion.1), channel_id=1, source_target_pairs={{0,1},{1,0},{2,3},{3,2},{4,5},{5,4},{6,7},{7,6},{8,9},{9,8},{10,11... | collective-permute-start | bytes 3145736 | tf_op jit(solution)/shard_map/ppermute | solution.py:104
  (138 other events, 2065.5 us)
Sparse Core Ops, SparseCore 0:
  326.6 107.6 reduce-scatter.1
  460.4 112.4 all-gather.1
